TPU v7x, 256 devices: a whole 4x4x8 slice. The times are simulated.
256 devices in a mesh: row: 64 (over y, x_hi, z), ch: 4 (over x_lo, core).
Axes of the slice: x: 4 (x_hi: 2, x_lo: 2; x = x_hi * 2 + x_lo), y: 4, z: 8, core: 2. Of those that a mesh axis runs over, the one named last changes fastest.
Arguments:
- pair_field: bfloat16 [128, 512, 512], P('ch', 'row'), may hold values from -25 to 25
- input_gain: float32 [128], replicated, may hold values from 0.5 to 1.5
- input_bias: float32 [128], replicated, may hold values from -1.2 to 1.2
- left_weight: bfloat16 [128, 128], P(None, 'ch'), may hold values from -0.5 to 0.5
- left_gate: bfloat16 [128, 128], P(None, 'ch'), may hold values from -0.5 to 0.5
- right_weight: bfloat16 [128, 128], P(None, 'ch'), may hold values from -0.5 to 0.5
- right_gate: bfloat16 [128, 128], P(None, 'ch'), may hold values from -0.5 to 0.5
- gate_weight: bfloat16 [128, 128], P(None, 'ch'), may hold values from -0.5 to 0.5
- output_gain: float32 [128], replicated, may hold values from 0.5 to 1.5
- output_bias: float32 [128], replicated, may hold values from -1.2 to 1.2
- final_weight: bfloat16 [128, 128], P(None, 'ch'), may hold values from -0.5 to 0.5
Outputs:
- transposed: bfloat16 [128, 512, 512], P('ch', 'row')
All inputs are finite; a program needn't handle non-finite values.
Results may differ from a plain program's by a relative error of at most 0.012.
Values may be sent and summed in bfloat16 or wider, within the bound.
No kernel may reach another device: no remote copies, remote signals or barrier semaphores. Data moves between devices by JAX's collectives and lax.ppermute only.
A program may use at most 64 MiB of HBM per device.

v0:
```python
import jax
import jax.numpy as jnp
from jax import lax
from jax.sharding import PartitionSpec as P

epsilon = 1e-05


def layer_norm(values, gain, bias):
    average = jnp.mean(values, axis=0, keepdims=True)
    centred = values - average
    variance = jnp.mean(centred * centred, axis=0, keepdims=True)
    return centred * lax.rsqrt(variance + epsilon) * gain[:, None, None] + bias[:, None, None]


def project(normed, weight):
    flat_field = normed.reshape(normed.shape[0], normed.shape[1] * normed.shape[2])
    result = jnp.dot(jnp.transpose(weight), flat_field, preferred_element_type=jnp.float32)
    return result.reshape(weight.shape[1], normed.shape[1], normed.shape[2])


def contract(first, second, form):
    return jnp.einsum(
        form, first.astype(jnp.float32), second.astype(jnp.float32), precision=lax.Precision.HIGHEST
    )


def body(
    pair_field,
    input_gain,
    input_bias,
    left_weight,
    left_gate,
    right_weight,
    right_gate,
    gate_weight,
    output_gain,
    output_bias,
    final_weight,
):
    gathered = lax.all_gather(pair_field, "ch", axis=0, tiled=True)
    normed = layer_norm(gathered.astype(jnp.float32), input_gain, input_bias).astype(jnp.bfloat16)
    left_factor = (
        jax.nn.sigmoid(project(normed, left_gate)) * project(normed, left_weight)
    ).astype(jnp.bfloat16)
    right_factor = (
        jax.nn.sigmoid(project(normed, right_gate)) * project(normed, right_weight)
    ).astype(jnp.bfloat16)
    gating = jax.nn.sigmoid(project(normed, gate_weight)).astype(jnp.bfloat16)
    product = contract(
        left_factor, lax.all_gather(right_factor, "row", axis=1, tiled=True), "cik,cjk->cij"
    )
    hidden_all = lax.all_gather(product.astype(jnp.bfloat16), "ch", axis=0, tiled=True)
    hidden_normed = layer_norm(hidden_all.astype(jnp.float32), output_gain, output_bias).astype(
        jnp.bfloat16
    )
    update = (gating.astype(jnp.float32) * project(hidden_normed, final_weight)).astype(
        jnp.bfloat16
    )
    return lax.all_to_all(
        jnp.swapaxes(update, 1, 2), "row", split_axis=1, concat_axis=2, tiled=True
    )


def solution(mesh):
    placed = (
        P("ch", "row", None),
        P(),
        P(),
        P(None, "ch"),
        P(None, "ch"),
        P(None, "ch"),
        P(None, "ch"),
        P(None, "ch"),
        P(),
        P(),
        P(None, "ch"),
    )
    return jax.shard_map(
        body, mesh=mesh, in_specs=placed, out_specs=P("ch", "row", None), check_vma=False
    )
```

profile of v0, /device:TPU:1, one launch (start us, length us, event | category | flops | bytes accessed | tf_op | source)
XLA Modules:
  0.0 340.5 jit_solution(7408528371137574967)
XLA Ops:
  6.5 0.0 copy-start
  6.5 0.0 all-gather.4.cloned.1.call-start
  6.5 0.7 all-gather.4.cloned.1.call-update
  7.3 0.0 all-gather.6.cloned.1.call-start
  7.3 29.3 %all-gather.4.cloned.1.call-done = bf16[128,8,512]{2,1,0:T(8,128)(2,1)} async-done(((bf16[32,8,512]{2,1,0:T(8,128)(2,1)}), bf16[128,8,512]{2,1,0:T(8,128)(2,1)}) %all-gather.4.cloned.1.call-update) | async-done | bytes 1048592 | tf_op jit(solution)/shard_map/all_gather | solution.py:41
  36.7 1.5 convert_reduce_fusion.1
  38.2 1.6 fusion.22
  39.7 0.0 copy-done.6
  39.7 0.0 copy-done.7
  39.8 0.0 copy-done.2
  39.8 0.4 fusion.25
  40.2 0.0 copy-start.3
  40.2 0.4 copy.19
  40.6 0.0 copy-done
  40.6 0.0 copy-start.10
  40.6 0.3 fusion.2
  40.9 0.0 copy-done.3
  40.9 0.3 fusion.12
  41.2 0.0 copy-start.4
  41.2 0.8 copy.21
  42.0 0.0 all-gather.6.cloned.1.call-update
  42.0 0.0 all-gather.8.cloned.1.call-start
  42.1 0.3 fusion.5
  42.4 0.3 fusion.11
  42.7 0.1 copy.20
  42.8 223.6 %all-gather.6.cloned.1.call-done = bf16[32,512,512]{2,1,0:T(8,128)(2,1)} async-done(((bf16[32,8,512]{2,1,0:T(8,128)(2,1)}), bf16[32,512,512]{2,1,0:T(8,128)(2,1)}) %all-gather.6.cloned.1.call-update) | async-done | bytes 16777232 | tf_op jit(solution)/shard_map/all_gather | solution.py:51
  266.4 10.9 %convolution_convert_fusion = bf16[32,8,512]{2,1,0:T(8,128)(2,1)} fusion(bf16[32,8,512]{2,1,0:T(8,128)(2,1)S(1)} %bitcast.48, bf16[32,512,512]{2,1,0:T(8,128)(2,1)} %all-gather.6.cloned.1.call-done), kind=kOutput, calls=%fused_computation.36 | convolution fusion | flops 134348800 | bytes 17301504 | tf_op jit(solution)/shard_map/cik,cjk->cij/dot_general | solution.py:23
  277.3 0.0 all-gather.8.cloned.1.call-update
  277.3 0.0 copy-start.8
  277.3 0.0 copy-start.9
  277.3 0.3 fusion.10
  277.6 22.2 %all-gather.8.cloned.1.call-done = bf16[128,8,512]{2,1,0:T(8,128)(2,1)} async-done(((bf16[32,8,512]{2,1,0:T(8,128)(2,1)}), bf16[128,8,512]{2,1,0:T(8,128)(2,1)}) %all-gather.8.cloned.1.call-update) | async-done | bytes 1048592 | tf_op jit(solution)/shard_map/all_gather | solution.py:53
  299.9 1.5 convert_reduce_fusion
  301.4 1.6 fusion.18
  303.0 0.0 copy-done.8
  303.0 0.0 copy-start.5
  303.0 0.4 fusion.21
  303.4 0.4 copy.22
  303.8 0.0 copy-done.5
  303.8 0.3 fusion.13
  304.1 0.1 copy.23
  304.2 0.8 copy.16
  305.1 0.1 bitcast_bitcast_fusion
  305.1 1.0 reshape.87
  306.1 25.8 %all_to_all.18 = bf16[64,2,1024]{2,1,0:T(2,128)(2,1)S(1)} all-to-all(bf16[64,2,1024]{2,1,0:T(2,128)(2,1)S(1)} %reshape.87), channel_id=1, replica_groups=mesh['row'=64,'ch'=4] {'row'}, dimensions={0} | all-to-all | bytes 524288 | tf_op jit(solution)/shard_map/all_to_all | solution.py:60
  332.0 0.5 reshape.88
  332.5 0.2 copy.25
  332.7 1.3 copy.18
  (14 shorter events, 0.1 us)
Async XLA Ops:
  6.5 34.1 %copy-start = (bf16[128,32]{0,1:T(8,128)(2,1)S(1)}, bf16[128,32]{0,1:T(8,128)(2,1)}, u32[]{:S(2)}) copy-start(bf16[128,32]{0,1:T(8,128)(2,1)} %param.17) | copy-start | bytes 24580
  6.5 33.2 %copy-start.6 = (f32[128]{0:T(128)S(1)}, f32[128]{0:T(128)}, u32[]{:S(2)}) copy-start(f32[128]{0:T(128)} %param.13) | copy-start | bytes 1540
  6.5 33.2 %copy-start.7 = (f32[128]{0:T(128)S(1)}, f32[128]{0:T(128)}, u32[]{:S(2)}) copy-start(f32[128]{0:T(128)} %param.12) | copy-start | bytes 1540
  6.5 30.1 %all-gather.4.cloned.1.call-start = ((), (), s32[]{:S(2)}) async-start(), calls=%async_computation.1 | async-start | bytes 1310720 | tf_op jit(solution)/shard_map/all_gather | solution.py:41
  7.3 259.1 %all-gather.6.cloned.1.call-start = ((), (), s32[]{:S(2)}) async-start(), calls=%async_computation.2 | async-start | bytes 17039360 | tf_op jit(solution)/shard_map/all_gather | solution.py:51
  36.7 3.1 copy-start.2
  40.2 0.7 copy-start.3
  40.6 1.5 copy-start.10
  41.2 1.2 copy-start.4
  42.0 257.9 %all-gather.8.cloned.1.call-start = ((), (), s32[]{:S(2)}) async-start(), calls=%async_computation.3 | async-start | bytes 1310720 | tf_op jit(solution)/shard_map/all_gather | solution.py:53
  266.4 11.0 %copy-start.11 = (bf16[128,32]{0,1:T(8,128)(2,1)S(1)}, bf16[128,32]{0,1:T(8,128)(2,1)}, u32[]{:S(2)}) copy-start(bf16[128,32]{0,1:T(8,128)(2,1)} %param.18) | copy-start | bytes 24580
  277.3 25.6 %copy-start.8 = (f32[128]{0:T(128)S(1)}, f32[128]{0:T(128)}, u32[]{:S(2)}) copy-start(f32[128]{0:T(128)} %param.20) | copy-start | bytes 1540
  277.3 25.6 %copy-start.9 = (f32[128]{0:T(128)S(1)}, f32[128]{0:T(128)}, u32[]{:S(2)}) copy-start(f32[128]{0:T(128)} %param.19) | copy-start | bytes 1540
  299.9 3.1 copy-start.1
  303.0 0.8 copy-start.5
Sparse Core Ops, SparseCore 0:
  9.2 27.4 all-gather.3
  42.1 224.1 all-gather.5
  277.4 22.4 all-gather.7
where the time goes:
time: 341 us; the launch traced here: 340 us
  waiting for transfers between devices  276 us (81%)
  blocking collectives  25.8 us (8%)
  between operations  13.4 us (4%)
  matrix products  12.6 us (4%)
  other arithmetic  6.98 us (2%)
  local copies, waits for them, and re-layouts  5.68 us (2%)
    all_gather x1, waiting for transfers between devices, body(): lax.all_gather(right_factor, 'row', axis=1, tiled=True)  224 us
    all_gather x1, waiting for transfers between devices, body(): gathered = lax.all_gather(pair_field, 'ch', axis=0, tiled=True)  29.3 us
    all_to_all x1, blocking collectives, body(): lax.all_to_all(jnp.swapaxes(update, 1, 2), 'row', split_axis=1, concat_ax...  25.8 us
    all_gather x1, waiting for transfers between devices, body(): lax.all_gather(product.astype(jnp.bfloat16), 'ch', axis=0, tiled=True)  22.2 us
    dot_general x1, matrix products, contract(): jnp.einsum(form, first.astype(jnp.float32), second.astype(jnp.float32), p...  10.9 us
  transfers between devices with their start and end apart: 3, of which 3 were waited for; matrix products, arithmetic and copies ran while one was open for 0% of the time, Pallas kernels for 0%

commit v1 on v0

v1 whole, which is shorter than its diff:
```python
import jax
import jax.numpy as jnp
from jax import lax
from jax.sharding import PartitionSpec as P

epsilon = 1e-05


def layer_norm(values, gain, bias):
    average = jnp.mean(values, axis=-2, keepdims=True)
    centred = values - average
    variance = jnp.mean(centred * centred, axis=-2, keepdims=True)
    return centred * lax.rsqrt(variance + epsilon) * gain[:, None] + bias[:, None]


def swap(array, step):
    return lax.ppermute(array, "ch", [(s, s ^ step) for s in range(4)])


def place(blocks, mine):
    stacked = jnp.stack(blocks)
    return jnp.stack([lax.dynamic_index_in_dim(stacked, mine ^ t, 0, False) for t in range(4)])


def body(
    pair_field,
    input_gain,
    input_bias,
    left_weight,
    left_gate,
    right_weight,
    right_gate,
    gate_weight,
    output_gain,
    output_bias,
    final_weight,
):
    mine = lax.axis_index("ch")
    core = mine % 2
    everyone = ("row", "ch")
    weights = jnp.concatenate(
        [w.T for w in (left_weight, left_gate, right_weight, right_gate)], axis=1
    )
    late = lax.all_gather(
        jnp.concatenate([gate_weight.T, final_weight.T], axis=1), "ch", axis=0, tiled=True
    )
    field = jnp.swapaxes(pair_field, 0, 1)

    def message(step):
        part = lax.dynamic_slice(field, (2 * (mine ^ step), 0, 0), (2, 32, 512))
        return jnp.concatenate([part.reshape(64, 512), weights], axis=0)

    got = place([message(0)] + [swap(message(t), t) for t in (1, 2, 3)], mine)
    whole = jnp.swapaxes(got[:, :64].reshape(4, 2, 32, 512), 0, 1).reshape(2, 128, 512)
    wide = got[:, 64:].reshape(128, 4, 128)
    normed = layer_norm(whole.astype(jnp.float32), input_gain, input_bias).astype(jnp.bfloat16)

    def project(weight):
        return jnp.einsum("dc,ack->dak", weight, normed, preferred_element_type=jnp.float32)

    left = jax.nn.sigmoid(project(wide[:, 1])) * project(wide[:, 0])
    right = jax.nn.sigmoid(project(wide[:, 3])) * project(wide[:, 2])
    sent = jnp.concatenate(
        [left.reshape(256, 4, 128), right.reshape(256, 4, 128)], axis=1
    ).astype(jnp.bfloat16)
    factors = lax.all_to_all(sent, everyone, 0, 0, tiled=True)
    other = swap(factors[:, :4], 1)
    own = factors[:, :4].reshape(256, 512)
    other = other.reshape(256, 512)
    rows = jnp.stack([jnp.where(core == 0, own, other), jnp.where(core == 0, other, own)], axis=1)
    product = jnp.einsum(
        "jk,ik->ji",
        factors[:, 4:].reshape(256, 512),
        rows.reshape(512, 512),
        preferred_element_type=jnp.float32,
    ).astype(jnp.bfloat16)
    gating = jax.nn.sigmoid(
        jnp.einsum("ec,acj->jae", late[:, :128], normed, preferred_element_type=jnp.float32)
    ).astype(jnp.bfloat16)
    sent = jnp.concatenate([product.reshape(256, 4, 128), gating.reshape(256, 4, 128)], axis=1)
    got = lax.all_to_all(sent, everyone, 0, 0, tiled=True)
    hidden = jnp.swapaxes(got[:, :4].reshape(128, 2, 512), 0, 1)
    normed = layer_norm(hidden.astype(jnp.float32), output_gain, output_bias).astype(jnp.bfloat16)
    update = jnp.einsum("ed,jdi->jei", late[:, 128:], normed, preferred_element_type=jnp.float32)
    gating = got[:, 4:].reshape(256, 2, 2, 128).transpose(1, 3, 0, 2).reshape(2, 128, 512)
    update = (update * gating.astype(jnp.float32)).astype(jnp.bfloat16)

    def part(step):
        return lax.dynamic_slice(update, (0, 32 * (mine ^ step), 0), (2, 32, 512))

    got = place([part(0)] + [swap(part(t), t) for t in (1, 2, 3)], mine)
    return jnp.swapaxes(got.reshape(8, 32, 512), 0, 1)


def solution(mesh):
    placed = (
        P("ch", "row", None),
        P(),
        P(),
        P(None, "ch"),
        P(None, "ch"),
        P(None, "ch"),
        P(None, "ch"),
        P(None, "ch"),
        P(),
        P(),
        P(None, "ch"),
    )
    return jax.shard_map(
        body, mesh=mesh, in_specs=placed, out_specs=P("ch", "row", None), check_vma=False
    )
```

time: 341 us -> 90.7 us (0.27)
  waiting for transfers between devices: 276 us -> 40.9 us
  starting transfers between devices: 0.08 us -> 25.6 us
  blocking collectives: 25.8 us -> 7.46 us
  between operations: 13.4 us -> 0.46 us
  matrix products: 12.6 us -> 1.97 us
    all_gather x3 -> x0, waiting for transfers between devices: 275 us -> none  [the longest x1 224 us: body(): lax.all_gather(right_factor, 'row', axis=1, tiled=True)]
    all_to_all x0 -> x2, waiting for transfers between devices: none -> 34 us  [the longest x1 21.1 us: body(): got = lax.all_to_all(sent, everyone, 0, 0, tiled=True)]
    all_to_all x1 -> x0, blocking collectives: 25.8 us -> none  [body(): lax.all_to_all(jnp.swapaxes(update, 1, 2), 'row', split_axis=1, concat_ax...]
    all_to_all x0 -> x2, starting transfers between devices: none -> 18 us  [the longest x1 12.6 us: body(): factors = lax.all_to_all(sent, everyone, 0, 0, tiled=True)]
    dot_general x7, matrix products: 12.6 us -> 1.97 us  [the longest x4 1 us: project(): jnp.einsum('dc,ack->dak', weight, normed, preferred_element_type=jnp.floa...]
    ppermute x0 -> x7, starting transfers between devices: none -> 7.68 us  [swap(): return lax.ppermute(array, 'ch', [(s, s ^ step) for s in range(4)])]
    all_gather x0 -> x1, blocking collectives: none -> 7.46 us  [body(): lax.all_gather(jnp.concatenate([gate_weight.T, final_weight.T], axis=1),...]
    ppermute x0 -> x7, waiting for transfers between devices: none -> 6.98 us  [swap(): return lax.ppermute(array, 'ch', [(s, s ^ step) for s in range(4)])]
  transfers between devices with their start and end apart: 3 -> 9, of which waited for: 3 -> 7; matrix products, arithmetic and copies ran while one was open for 0% -> 1% of each run, Pallas kernels for 0% -> 0%
where the time goes in v1:
time: 90.7 us; the launch traced here: 90.2 us
  waiting for transfers between devices  40.9 us (45%)
  starting transfers between devices  25.6 us (28%)
  local copies, waits for them, and re-layouts  8.92 us (10%)
  blocking collectives  7.46 us (8%)
  other arithmetic  4.84 us (5%)
  matrix products  1.97 us (2%)
    all_to_all x1, waiting for transfers between devices, body(): got = lax.all_to_all(sent, everyone, 0, 0, tiled=True)  21.1 us
    all_to_all x1, waiting for transfers between devices, body(): factors = lax.all_to_all(sent, everyone, 0, 0, tiled=True)  12.9 us
    all_to_all x1, starting transfers between devices, body(): factors = lax.all_to_all(sent, everyone, 0, 0, tiled=True)  12.6 us
    ppermute x7, starting transfers between devices, swap(): return lax.ppermute(array, 'ch', [(s, s ^ step) for s in range(4)])  7.68 us
    all_gather x1, blocking collectives, body(): lax.all_gather(jnp.concatenate([gate_weight.T, final_weight.T], axis=1),...  7.46 us
    ppermute x7, waiting for transfers between devices, swap(): return lax.ppermute(array, 'ch', [(s, s ^ step) for s in range(4)])  6.98 us
    all_to_all x1, starting transfers between devices, body(): got = lax.all_to_all(sent, everyone, 0, 0, tiled=True)  5.33 us
    unnamed x24, local copies, waits for them, and re-layouts  3.31 us
  transfers between devices with their start and end apart: 9, of which 7 were waited for; matrix products, arithmetic and copies ran while one was open for 1% of the time, Pallas kernels for 0%

profile of v1, /device:TPU:1, one launch (start us, length us, event | category | flops | bytes accessed | tf_op | source)
XLA Modules:
  0.0 90.2 jit_solution(11001124090783543311)
XLA Ops:
  0.0 1.7 %constant_dynamic-slice_fusion.14 = (bf16[32,2,512]{2,1,0:T(2,128)(2,1)S(1)}, bf16[32,2,512]{2,1,0:T(2,128)(2,1)S(1)}, bf16[32,2,512]{2,1,0:T(2,128)(2,1)S(1)}, bf16[32,2,512]{2,1,0:T(2,128)(2,1)S(1)}) fusion(bf16[32,8,512]{2,1,0:T(8,128)(2,1)} %param.11, s32[]{:T(128)S(6)} %select_n.81, s32[]{:T(128)S(6)} %select_n.83, s32[]{:T(128)S(6)} %select_n.82, ...), kind=kLoop, calls=%fused_computation.85 | loop fusion | bytes 524304 | tf_op jit(solution)/shard_map/dynamic-slice
  1.8 0.6 copy-done.1
  2.5 3.3 %collective-permute-start = (bf16[96,512]{1,0:T(8,128)(2,1)S(1)}, bf16[96,512]{1,0:T(8,128)(2,1)S(1)}, u32[]{:S(2)}, u32[]{:S(2)}) collective-permute-start(bf16[96,512]{1,0:T(8,128)(2,1)S(1)} %get-tuple-element.33), channel_id=1, source_target_pairs={{0,1},{1,0},{2,3},{3,2},{4,5},{5,4},{6,7},{7,6},{8,9},{9,8},{10,11... | collective-permute-start | bytes 294920 | tf_op jit(solution)/shard_map/ppermute | solution.py:17
  5.9 1.8 %collective-permute-start.2 = (bf16[96,512]{1,0:T(8,128)(2,1)S(1)}, bf16[96,512]{1,0:T(8,128)(2,1)S(1)}, u32[]{:S(2)}, u32[]{:S(2)}) collective-permute-start(bf16[96,512]{1,0:T(8,128)(2,1)S(1)} %pad_maximum_fusion.13), channel_id=1, source_target_pairs={{0,3},{1,2},{2,1},{3,0},{4,7},{5,6},{6,5},{7,4},{8,11},{9,10},{10,... | collective-permute-start | bytes 294920 | tf_op jit(solution)/shard_map/ppermute | solution.py:17
  7.7 0.7 copy-done.7
  8.4 0.6 copy-done.6
  9.1 1.1 %collective-permute-done.1 = bf16[96,512]{1,0:T(8,128)(2,1)S(1)} collective-permute-done((bf16[96,512]{1,0:T(8,128)(2,1)S(1)}, bf16[96,512]{1,0:T(8,128)(2,1)S(1)}, u32[]{:S(2)}, u32[]{:S(2)}) %collective-permute-start.1) | collective-permute-done | bytes 98336 | tf_op jit(solution)/shard_map/ppermute | solution.py:17
  10.2 2.3 %collective-permute-done.2 = bf16[96,512]{1,0:T(8,128)(2,1)S(1)} collective-permute-done((bf16[96,512]{1,0:T(8,128)(2,1)S(1)}, bf16[96,512]{1,0:T(8,128)(2,1)S(1)}, u32[]{:S(2)}, u32[]{:S(2)}) %collective-permute-start.2) | collective-permute-done | bytes 98336 | tf_op jit(solution)/shard_map/ppermute | solution.py:17
  12.7 0.2 fusion.26
  13.1 0.2 add_convert_fusion.1
  13.3 0.3 fusion.6
  13.6 0.2 fusion.11
  13.8 0.3 copy.64
  14.1 0.2 reshape.143
  14.3 0.3 fusion.9
  14.6 0.2 fusion.10
  14.8 0.3 copy.61
  15.1 0.2 reshape.142
  15.3 1.1 %pad_maximum_fusion = bf16[256,8,128]{2,1,0:T(8,128)(2,1)} fusion(bf16[256,4,128]{2,1,0:T(4,128)(2,1)S(1)} %reshape.143, bf16[256,4,128]{2,1,0:T(4,128)(2,1)S(1)} %reshape.142), kind=kLoop, calls=%fused_computation.22 | loop fusion | flops 1048576 | bytes 1048576 | tf_op jit(solution)/shard_map/concatenate | solution.py:63
  16.3 12.6 %all-to-all-start = ((bf16[256,8,128]{2,1,0:T(8,128)(2,1)}), bf16[256,8,128]{2,1,0:T(8,128)(2,1)S(1)}, u32[]{:S(2)}, u32[]{:S(2)}) async-start(bf16[256,8,128]{2,1,0:T(8,128)(2,1)} %pad_maximum_fusion), calls=%async_computation | async-start | bytes 1048576 | tf_op jit(solution)/shard_map/all_to_all | solution.py:66
  29.0 0.7 copy-done.5
  29.7 7.5 %all_gather.3 = bf16[128,256]{1,0:T(8,128)(2,1)S(1)} all-gather(bf16[32,256]{1,0:T(8,128)(2,1)S(1)} %pad_maximum_fusion.14), channel_id=1, replica_groups=mesh['row'=64,'ch'=4] {'ch'}, dimensions={0}, use_global_device_ids=true | all-gather | bytes 81920 | tf_op jit(solution)/shard_map/all_gather | solution.py:44
  37.2 12.9 %all-to-all-done = bf16[256,8,128]{2,1,0:T(8,128)(2,1)S(1)} async-done(((bf16[256,8,128]{2,1,0:T(8,128)(2,1)}), bf16[256,8,128]{2,1,0:T(8,128)(2,1)S(1)}, u32[]{:S(2)}, u32[]{:S(2)}) %all-to-all-start) | async-done | bytes 524320 | tf_op jit(solution)/shard_map/all_to_all | solution.py:66
  50.1 0.3 collective-permute-start.3
  50.4 0.2 fusion.18
  50.6 0.3 fusion.14
  51.0 0.3 copy.69
  51.3 0.5 collective-permute-done.3
  51.7 0.3 broadcast_select_fusion.1
  52.1 0.1 select_n.99
  52.4 1.2 %pad_maximum_fusion.1 = bf16[256,2,512]{2,1,0:T(2,128)(2,1)S(1)} fusion(bf16[256,1,512]{2,1,0:T(2,128)(2,1)S(1)} %select_n.100, bf16[256,1,512]{2,1,0:T(2,128)(2,1)S(1)} %select_n.99), kind=kLoop, calls=%fused_computation.23 | loop fusion | flops 1048576 | bytes 1048576 | tf_op jit(solution)/shard_map/stack | solution.py:70
  53.6 0.2 reshape.145
  53.8 0.3 convolution_convert_fusion
  54.2 1.1 %pad_maximum_fusion.2 = bf16[256,8,128]{2,1,0:T(8,128)(2,1)} fusion(bf16[256,4,128]{2,1,0:T(4,128)(2,1)S(1)} %bitcast.119, bf16[256,4,128]{2,1,0:T(4,128)(2,1)S(1)} %reshape.146), kind=kLoop, calls=%fused_computation.24 | loop fusion | flops 1048576 | bytes 1048576 | tf_op jit(solution)/shard_map/concatenate | solution.py:80
  55.3 5.3 %all-to-all-start.1 = ((bf16[256,8,128]{2,1,0:T(8,128)(2,1)}), bf16[256,8,128]{2,1,0:T(8,128)(2,1)S(1)}, u32[]{:S(2)}, u32[]{:S(2)}) async-start(bf16[256,8,128]{2,1,0:T(8,128)(2,1)} %pad_maximum_fusion.2), calls=%async_computation.1 | async-start | bytes 1048576 | tf_op jit(solution)/shard_map/all_to_all | solution.py:81
  60.7 21.1 %all-to-all-done.1 = bf16[256,8,128]{2,1,0:T(8,128)(2,1)S(1)} async-done(((bf16[256,8,128]{2,1,0:T(8,128)(2,1)}), bf16[256,8,128]{2,1,0:T(8,128)(2,1)S(1)}, u32[]{:S(2)}, u32[]{:S(2)}) %all-to-all-start.1) | async-done | bytes 524320 | tf_op jit(solution)/shard_map/all_to_all | solution.py:81
  81.8 0.1 slice_convert_fusion.1
  81.9 0.4 reshape.151
  82.3 0.2 copy.71
  82.5 0.2 copy.72
  83.0 0.6 copy-done.8
  83.6 0.3 fusion.13
  83.9 0.6 collective-permute-start.6
  84.5 1.1 %collective-permute-start.5 = (bf16[2,32,512]{2,1,0:T(8,128)(2,1)S(1)}, bf16[2,32,512]{2,1,0:T(8,128)(2,1)S(1)}, u32[]{:S(2)}, u32[]{:S(2)}) collective-permute-start(bf16[2,32,512]{2,1,0:T(8,128)(2,1)S(1)} %get-tuple-element.22), channel_id=1, source_target_pairs={{0,2},{1,3},{2,0},{3,1},{4,6},{5,7},{6,4},{7,5},{8,10},{9,11},{10,... | collective-permute-start | bytes 196616 | tf_op jit(solution)/shard_map/ppermute | solution.py:17
  85.6 0.6 collective-permute-start.4
  86.2 2.2 %collective-permute-done.6 = bf16[2,32,512]{2,1,0:T(8,128)(2,1)S(1)} collective-permute-done((bf16[2,32,512]{2,1,0:T(8,128)(2,1)S(1)}, bf16[2,32,512]{2,1,0:T(8,128)(2,1)S(1)}, u32[]{:S(2)}, u32[]{:S(2)}) %collective-permute-start.6) | collective-permute-done | bytes 65568 | tf_op jit(solution)/shard_map/ppermute | solution.py:17
  88.3 0.9 %collective-permute-done.5 = bf16[2,32,512]{2,1,0:T(8,128)(2,1)S(1)} collective-permute-done((bf16[2,32,512]{2,1,0:T(8,128)(2,1)S(1)}, bf16[2,32,512]{2,1,0:T(8,128)(2,1)S(1)}, u32[]{:S(2)}, u32[]{:S(2)}) %collective-permute-start.5) | collective-permute-done | bytes 65568 | tf_op jit(solution)/shard_map/ppermute | solution.py:17
  89.4 0.9 copy.101
  (49 shorter events, 1.4 us)
Async XLA Ops:
  1.7 0.7 copy-start.1
  1.7 0.7 copy-start.2
  1.7 0.7 copy-start.3
  1.8 0.7 copy-start
  2.5 6.6 %collective-permute-start = (bf16[96,512]{1,0:T(8,128)(2,1)S(1)}, bf16[96,512]{1,0:T(8,128)(2,1)S(1)}, u32[]{:S(2)}, u32[]{:S(2)}) collective-permute-start(bf16[96,512]{1,0:T(8,128)(2,1)S(1)} %get-tuple-element.33), channel_id=1, source_target_pairs={{0,1},{1,0},{2,3},{3,2},{4,5},{5,4},{6,7},{7,6},{8,9},{9,8},{10,11... | collective-permute-start | bytes 294920 | tf_op jit(solution)/shard_map/ppermute | solution.py:17
  5.8 4.4 %collective-permute-start.1 = (bf16[96,512]{1,0:T(8,128)(2,1)S(1)}, bf16[96,512]{1,0:T(8,128)(2,1)S(1)}, u32[]{:S(2)}, u32[]{:S(2)}) collective-permute-start(bf16[96,512]{1,0:T(8,128)(2,1)S(1)} %get-tuple-element.34), channel_id=1, source_target_pairs={{0,2},{1,3},{2,0},{3,1},{4,6},{5,7},{6,4},{7,5},{8,10},{9,11},{10,... | collective-permute-start | bytes 294920 | tf_op jit(solution)/shard_map/ppermute | solution.py:17
  5.9 6.6 %collective-permute-start.2 = (bf16[96,512]{1,0:T(8,128)(2,1)S(1)}, bf16[96,512]{1,0:T(8,128)(2,1)S(1)}, u32[]{:S(2)}, u32[]{:S(2)}) collective-permute-start(bf16[96,512]{1,0:T(8,128)(2,1)S(1)} %pad_maximum_fusion.13), channel_id=1, source_target_pairs={{0,3},{1,2},{2,1},{3,0},{4,7},{5,6},{6,5},{7,4},{8,11},{9,10},{10,... | collective-permute-start | bytes 294920 | tf_op jit(solution)/shard_map/ppermute | solution.py:17
  7.7 0.7 copy-start.7
  8.3 0.7 copy-start.6
  16.3 33.7 %all-to-all-start = ((bf16[256,8,128]{2,1,0:T(8,128)(2,1)}), bf16[256,8,128]{2,1,0:T(8,128)(2,1)S(1)}, u32[]{:S(2)}, u32[]{:S(2)}) async-start(bf16[256,8,128]{2,1,0:T(8,128)(2,1)} %pad_maximum_fusion), calls=%async_computation | async-start | bytes 1048576 | tf_op jit(solution)/shard_map/all_to_all | solution.py:66
  29.0 0.7 copy-start.5
  29.0 0.7 copy-start.4
  50.1 1.6 %collective-permute-start.3 = (bf16[256,4,128]{2,1,0:T(4,128)(2,1)S(1)}, bf16[256,4,128]{2,1,0:T(4,128)(2,1)S(1)}, u32[]{:S(2)}, u32[]{:S(2)}) collective-permute-start(bf16[256,4,128]{2,1,0:T(4,128)(2,1)S(1)} %slice.55), channel_id=1, source_target_pairs={{0,1},{1,0},{2,3},{3,2},{4,5},{5,4},{6,7},{7,6},{8,9},{9,8},{10,11... | collective-permute-start | bytes 786440 | tf_op jit(solution)/shard_map/ppermute | solution.py:17
  55.3 26.5 %all-to-all-start.1 = ((bf16[256,8,128]{2,1,0:T(8,128)(2,1)}), bf16[256,8,128]{2,1,0:T(8,128)(2,1)S(1)}, u32[]{:S(2)}, u32[]{:S(2)}) async-start(bf16[256,8,128]{2,1,0:T(8,128)(2,1)} %pad_maximum_fusion.2), calls=%async_computation.1 | async-start | bytes 1048576 | tf_op jit(solution)/shard_map/all_to_all | solution.py:81
  82.9 0.7 copy-start.8
  82.9 0.7 copy-start.9
  83.9 4.4 %collective-permute-start.6 = (bf16[2,32,512]{2,1,0:T(8,128)(2,1)S(1)}, bf16[2,32,512]{2,1,0:T(8,128)(2,1)S(1)}, u32[]{:S(2)}, u32[]{:S(2)}) collective-permute-start(bf16[2,32,512]{2,1,0:T(8,128)(2,1)S(1)} %get-tuple-element.21), channel_id=1, source_target_pairs={{0,3},{1,2},{2,1},{3,0},{4,7},{5,6},{6,5},{7,4},{8,11},{9,10},{10,... | collective-permute-start | bytes 196616 | tf_op jit(solution)/shard_map/ppermute | solution.py:17
  84.5 4.8 %collective-permute-start.5 = (bf16[2,32,512]{2,1,0:T(8,128)(2,1)S(1)}, bf16[2,32,512]{2,1,0:T(8,128)(2,1)S(1)}, u32[]{:S(2)}, u32[]{:S(2)}) collective-permute-start(bf16[2,32,512]{2,1,0:T(8,128)(2,1)S(1)} %get-tuple-element.22), channel_id=1, source_target_pairs={{0,2},{1,3},{2,0},{3,1},{4,6},{5,7},{6,4},{7,5},{8,10},{9,11},{10,... | collective-permute-start | bytes 196616 | tf_op jit(solution)/shard_map/ppermute | solution.py:17
  85.6 3.7 %collective-permute-start.4 = (bf16[2,32,512]{2,1,0:T(8,128)(2,1)S(1)}, bf16[2,32,512]{2,1,0:T(8,128)(2,1)S(1)}, u32[]{:S(2)}, u32[]{:S(2)}) collective-permute-start(bf16[2,32,512]{2,1,0:T(8,128)(2,1)S(1)} %get-tuple-element.23), channel_id=1, source_target_pairs={{0,1},{1,0},{2,3},{3,2},{4,5},{5,4},{6,7},{7,6},{8,9},{9,8},{10,11... | collective-permute-start | bytes 196616 | tf_op jit(solution)/shard_map/ppermute | solution.py:17

commit v2 on v1

--- a/solution.py
+++ b/solution.py
@@ -39,20 +39,20 @@
     core = mine % 2
     everyone = ("row", "ch")
     weights = jnp.concatenate(
-        [w.T for w in (left_weight, left_gate, right_weight, right_gate)], axis=1
+        [
+            w.T
+            for w in (left_weight, left_gate, right_weight, right_gate, gate_weight, final_weight)
+        ],
+        axis=1,
     )
-    late = lax.all_gather(
-        jnp.concatenate([gate_weight.T, final_weight.T], axis=1), "ch", axis=0, tiled=True
-    )
+    wide = place([weights] + [swap(weights, t) for t in (1, 2, 3)], mine).reshape(128, 6, 128)
     field = jnp.swapaxes(pair_field, 0, 1)
 
     def message(step):
-        part = lax.dynamic_slice(field, (2 * (mine ^ step), 0, 0), (2, 32, 512))
-        return jnp.concatenate([part.reshape(64, 512), weights], axis=0)
+        return lax.dynamic_slice(field, (2 * (mine ^ step), 0, 0), (2, 32, 512))
 
     got = place([message(0)] + [swap(message(t), t) for t in (1, 2, 3)], mine)
-    whole = jnp.swapaxes(got[:, :64].reshape(4, 2, 32, 512), 0, 1).reshape(2, 128, 512)
-    wide = got[:, 64:].reshape(128, 4, 128)
+    whole = jnp.swapaxes(got, 0, 1).reshape(2, 128, 512)
     normed = layer_norm(whole.astype(jnp.float32), input_gain, input_bias).astype(jnp.bfloat16)
 
     def project(weight):
@@ -75,14 +75,14 @@
         preferred_element_type=jnp.float32,
     ).astype(jnp.bfloat16)
     gating = jax.nn.sigmoid(
-        jnp.einsum("ec,acj->jae", late[:, :128], normed, preferred_element_type=jnp.float32)
+        jnp.einsum("ec,acj->jae", wide[:, 4], normed, preferred_element_type=jnp.float32)
     ).astype(jnp.bfloat16)
-    sent = jnp.concatenate([product.reshape(256, 4, 128), gating.reshape(256, 4, 128)], axis=1)
-    got = lax.all_to_all(sent, everyone, 0, 0, tiled=True)
-    hidden = jnp.swapaxes(got[:, :4].reshape(128, 2, 512), 0, 1)
+    gating = lax.all_to_all(gating.reshape(256, 4, 128), everyone, 0, 0, tiled=True)
+    got = lax.all_to_all(product.reshape(256, 4, 128), everyone, 0, 0, tiled=True)
+    hidden = jnp.swapaxes(got.reshape(128, 2, 512), 0, 1)
     normed = layer_norm(hidden.astype(jnp.float32), output_gain, output_bias).astype(jnp.bfloat16)
-    update = jnp.einsum("ed,jdi->jei", late[:, 128:], normed, preferred_element_type=jnp.float32)
-    gating = got[:, 4:].reshape(256, 2, 2, 128).transpose(1, 3, 0, 2).reshape(2, 128, 512)
+    update = jnp.einsum("ed,jdi->jei", wide[:, 5], normed, preferred_element_type=jnp.float32)
+    gating = gating.reshape(256, 2, 2, 128).transpose(1, 3, 0, 2).reshape(2, 128, 512)
     update = (update * gating.astype(jnp.float32)).astype(jnp.bfloat16)
 
     def part(step):

time: 90.7 us -> 108 us (1.19)
  blocking collectives: 7.46 us -> 34.9 us
  waiting for transfers between devices: 40.9 us -> 32.8 us
  starting transfers between devices: 25.6 us -> 20.6 us
  local copies, waits for them, and re-layouts: 8.92 us -> 13 us
    all_to_all x0 -> x1, blocking collectives: none -> 34.9 us  [body(): factors = lax.all_to_all(sent, everyone, 0, 0, tiled=True)]
    all_gather x1 -> x0, blocking collectives: 7.46 us -> none  [body(): lax.all_gather(jnp.concatenate([gate_weight.T, final_weight.T], axis=1),...]
    all_to_all x2, starting transfers between devices: 18 us -> 10.9 us  [the longest x1 5.49 us: body(): lax.all_to_all(gating.reshape(256, 4, 128), everyone, 0, 0, tiled=True)]
    all_to_all x2, waiting for transfers between devices: 34 us -> 27.8 us  [the longest x1 15.1 us: body(): lax.all_to_all(product.reshape(256, 4, 128), everyone, 0, 0, tiled=True)]
    unnamed x24 -> x23, local copies, waits for them, and re-layouts: 3.31 us -> 5.38 us
    ppermute x7 -> x10, starting transfers between devices: 7.68 us -> 9.69 us  [swap(): return lax.ppermute(array, 'ch', [(s, s ^ step) for s in range(4)])]
    ppermute x7 -> x10, waiting for transfers between devices: 6.98 us -> 4.98 us  [swap(): return lax.ppermute(array, 'ch', [(s, s ^ step) for s in range(4)])]
    another operation x3 -> x2, local copies, waits for them, and re-layouts: 2.22 us -> 0.54 us
  transfers between devices with their start and end apart: 9 -> 12, of which waited for: 7 -> 5; matrix products, arithmetic and copies ran while one was open for 1% -> 7% of each run, Pallas kernels for 0% -> 0%
where the time goes in v2:
time: 108 us
  blocking collectives  34.9 us (32%)
  waiting for transfers between devices  32.8 us (30%)
  starting transfers between devices  20.6 us (19%)
  local copies, waits for them, and re-layouts  13 us (12%)
  other arithmetic  3.87 us (4%)
  matrix products  2.01 us (2%)
    all_to_all x1, blocking collectives, body(): factors = lax.all_to_all(sent, everyone, 0, 0, tiled=True)  34.9 us
    all_to_all x1, waiting for transfers between devices, body(): lax.all_to_all(product.reshape(256, 4, 128), everyone, 0, 0, tiled=True)  15.1 us
    all_to_all x1, waiting for transfers between devices, body(): lax.all_to_all(gating.reshape(256, 4, 128), everyone, 0, 0, tiled=True)  12.6 us
    ppermute x10, starting transfers between devices, swap(): return lax.ppermute(array, 'ch', [(s, s ^ step) for s in range(4)])  9.69 us
    all_to_all x1, starting transfers between devices, body(): lax.all_to_all(gating.reshape(256, 4, 128), everyone, 0, 0, tiled=True)  5.49 us
    all_to_all x1, starting transfers between devices, body(): lax.all_to_all(product.reshape(256, 4, 128), everyone, 0, 0, tiled=True)  5.42 us
    unnamed x23, local copies, waits for them, and re-layouts  5.38 us
    ppermute x10, waiting for transfers between devices, swap(): return lax.ppermute(array, 'ch', [(s, s ^ step) for s in range(4)])  4.98 us
  transfers between devices with their start and end apart: 12, of which 5 were waited for; matrix products, arithmetic and copies ran while one was open for 7% of the time, Pallas kernels for 0%

profile of v2, /device:TPU:1, one launch (start us, length us, event | category | flops | bytes accessed | tf_op | source)
XLA Modules:
  0.0 107.6 jit_solution(10988048688458073153)
XLA Ops:
  0.0 0.7 constant_dynamic-update-slice_fusion.5
  0.7 0.7 copy-done.1
  1.4 0.7 copy-done.2
  2.1 0.7 copy-done.3
  2.8 0.7 copy-done.4
  3.5 3.2 %collective-permute-start = (bf16[32,768]{1,0:T(8,128)(2,1)S(1)}, bf16[32,768]{1,0:T(8,128)(2,1)S(1)}, u32[]{:S(2)}, u32[]{:S(2)}) collective-permute-start(bf16[32,768]{1,0:T(8,128)(2,1)S(1)} %constant_dynamic-update-slice_fusion), channel_id=1, source_target_pairs={{0,1},{1,0},{2,3},{3,2},{4,5},{5,4},{6,7},{7,6},{8,9},{9,8},{10,11... | collective-permute-start | bytes 147464 | tf_op jit(solution)/shard_map/ppermute | solution.py:17
  6.8 1.6 %collective-permute-start.2 = (bf16[32,768]{1,0:T(8,128)(2,1)S(1)}, bf16[32,768]{1,0:T(8,128)(2,1)S(1)}, u32[]{:S(2)}, u32[]{:S(2)}) collective-permute-start(bf16[32,768]{1,0:T(8,128)(2,1)S(1)} %constant_dynamic-update-slice_fusion), channel_id=1, source_target_pairs={{0,3},{1,2},{2,1},{3,0},{4,7},{5,6},{6,5},{7,4},{8,11},{9,10},{10,... | collective-permute-start | bytes 147464 | tf_op jit(solution)/shard_map/ppermute | solution.py:17
  8.4 1.5 %dynamic-slice_bitcast_fusion.4 = (bf16[1,2,32,512]{3,1,2,0:T(2,128)(2,1)S(1)}, bf16[2,32,512]{2,0,1:T(2,128)(2,1)S(1)}, bf16[2,32,512]{2,0,1:T(2,128)(2,1)S(1)}, bf16[2,32,512]{2,0,1:T(2,128)(2,1)S(1)}) fusion(bf16[32,8,512]{2,1,0:T(8,128)(2,1)} %param.11, s32[]{:T(128)S(6)} %select_n.89, s32[]{:T(128)S(6)} %select_n.90, s32[]{:T(128)S(6)} %select_n.92, ...), kind=kLoop, calls=%fused_computation.56 | loop fusion | bytes 524304 | tf_op jit(solution)/shard_map/stack | solution.py:21
  9.9 0.3 collective-permute-start.3
  10.3 0.7 copy-done.7
  11.0 0.6 copy-done.8
  11.7 1.9 %collective-permute-start.5 = (bf16[2,32,512]{2,0,1:T(2,128)(2,1)S(1)}, bf16[2,32,512]{2,0,1:T(2,128)(2,1)S(1)}, u32[]{:S(2)}, u32[]{:S(2)}) collective-permute-start(bf16[2,32,512]{2,0,1:T(2,128)(2,1)S(1)} %get-tuple-element.30), channel_id=1, source_target_pairs={{0,3},{1,2},{2,1},{3,0},{4,7},{5,6},{6,5},{7,4},{8,11},{9,10},{10,... | collective-permute-start | bytes 196616 | tf_op jit(solution)/shard_map/ppermute | solution.py:17
  13.7 0.2 reshape.121
  13.9 0.3 fusion.27
  14.2 1.5 %collective-permute-done.5 = bf16[2,32,512]{2,0,1:T(2,128)(2,1)S(1)} collective-permute-done((bf16[2,32,512]{2,0,1:T(2,128)(2,1)S(1)}, bf16[2,32,512]{2,0,1:T(2,128)(2,1)S(1)}, u32[]{:S(2)}, u32[]{:S(2)}) %collective-permute-start.5) | collective-permute-done | bytes 65568 | tf_op jit(solution)/shard_map/ppermute | solution.py:17
  15.8 0.5 pad_maximum_fusion.2
  16.4 0.4 bitcast_reduce_fusion.1
  16.8 0.4 fusion.17
  17.2 0.4 fusion.20
  17.9 0.3 fusion.9
  18.2 0.2 fusion.10
  18.5 0.3 copy.64
  18.9 0.3 fusion.6
  19.2 0.2 fusion.11
  19.5 0.3 copy.69
  19.9 0.3 pad_maximum_fusion
  20.2 34.9 %all_to_all.15 = bf16[256,8,128]{2,1,0:T(8,128)(2,1)S(1)} all-to-all(bf16[256,8,128]{2,1,0:T(8,128)(2,1)S(1)} %pad_maximum_fusion), channel_id=1, replica_groups=mesh['row'=64,'ch'=4] {'row','ch'}, dimensions={0} | all-to-all | bytes 1048576 | tf_op jit(solution)/shard_map/all_to_all | solution.py:66
  55.2 0.3 collective-permute-start.6
  55.5 0.3 fusion.14
  55.8 1.0 copy.76
  56.8 5.5 %all-to-all-start.2 = ((bf16[256,4,128]{2,1,0:T(4,128)(2,1)}), bf16[256,4,128]{2,1,0:T(4,128)(2,1)S(1)}, u32[]{:S(2)}, u32[]{:S(2)}) async-start(bf16[256,4,128]{2,1,0:T(4,128)(2,1)} %bitcast.35), calls=%async_computation.2 | async-start | bytes 524288 | tf_op jit(solution)/shard_map/all_to_all | solution.py:80
  62.3 0.3 broadcast_select_fusion.1
  63.0 1.2 %pad_maximum_fusion.1 = bf16[256,2,512]{2,1,0:T(2,128)(2,1)S(1)} fusion(bf16[256,1,512]{2,1,0:T(2,128)(2,1)S(1)} %select_n.104, bf16[256,1,512]{2,1,0:T(2,128)(2,1)S(1)} %select_n.103), kind=kLoop, calls=%fused_computation.23 | loop fusion | flops 1048576 | bytes 1048576 | tf_op jit(solution)/shard_map/stack | solution.py:70
  64.4 0.3 convolution_convert_fusion
  64.7 0.8 reshape.126
  65.5 12.6 %all-to-all-done.2 = bf16[256,4,128]{2,1,0:T(4,128)(2,1)S(1)} async-done(((bf16[256,4,128]{2,1,0:T(4,128)(2,1)}), bf16[256,4,128]{2,1,0:T(4,128)(2,1)S(1)}, u32[]{:S(2)}, u32[]{:S(2)}) %all-to-all-start.2) | async-done | bytes 262176 | tf_op jit(solution)/shard_map/all_to_all | solution.py:80
  78.1 5.4 %all-to-all-start.1 = ((bf16[256,4,128]{2,1,0:T(4,128)(2,1)}), bf16[256,4,128]{2,1,0:T(4,128)(2,1)S(1)}, u32[]{:S(2)}, u32[]{:S(2)}) async-start(bf16[256,4,128]{2,1,0:T(4,128)(2,1)} %reshape.126), calls=%async_computation.1 | async-start | bytes 524288 | tf_op jit(solution)/shard_map/all_to_all | solution.py:81
  83.7 0.4 copy.78
  84.3 15.1 %all-to-all-done.1 = bf16[256,4,128]{2,1,0:T(4,128)(2,1)S(1)} async-done(((bf16[256,4,128]{2,1,0:T(4,128)(2,1)}), bf16[256,4,128]{2,1,0:T(4,128)(2,1)S(1)}, u32[]{:S(2)}, u32[]{:S(2)}) %all-to-all-start.1) | async-done | bytes 262176 | tf_op jit(solution)/shard_map/all_to_all | solution.py:81
  99.4 0.3 reshape.130
  99.9 0.6 copy-done.5
  100.6 0.3 fusion.13
  100.9 0.5 collective-permute-start.7
  101.4 0.3 collective-permute-start.8
  101.7 1.5 %collective-permute-start.9 = (bf16[2,32,512]{2,1,0:T(8,128)(2,1)S(1)}, bf16[2,32,512]{2,1,0:T(8,128)(2,1)S(1)}, u32[]{:S(2)}, u32[]{:S(2)}) collective-permute-start(bf16[2,32,512]{2,1,0:T(8,128)(2,1)S(1)} %get-tuple-element.15), channel_id=1, source_target_pairs={{0,3},{1,2},{2,1},{3,0},{4,7},{5,6},{6,5},{7,4},{8,11},{9,10},{10,... | collective-permute-start | bytes 196616 | tf_op jit(solution)/shard_map/ppermute | solution.py:17
  103.2 1.8 %collective-permute-done.8 = bf16[2,32,512]{2,1,0:T(8,128)(2,1)S(1)} collective-permute-done((bf16[2,32,512]{2,1,0:T(8,128)(2,1)S(1)}, bf16[2,32,512]{2,1,0:T(8,128)(2,1)S(1)}, u32[]{:S(2)}, u32[]{:S(2)}) %collective-permute-start.8) | collective-permute-done | bytes 65568 | tf_op jit(solution)/shard_map/ppermute | solution.py:17
  105.0 1.7 %collective-permute-done.9 = bf16[2,32,512]{2,1,0:T(8,128)(2,1)S(1)} collective-permute-done((bf16[2,32,512]{2,1,0:T(8,128)(2,1)S(1)}, bf16[2,32,512]{2,1,0:T(8,128)(2,1)S(1)}, u32[]{:S(2)}, u32[]{:S(2)}) %collective-permute-start.9) | collective-permute-done | bytes 65568 | tf_op jit(solution)/shard_map/ppermute | solution.py:17
  106.7 0.9 copy.109
  (51 shorter events, 2.3 us)
Async XLA Ops:
  0.0 0.7 copy-start
  0.7 0.7 copy-start.1
  1.4 0.7 copy-start.2
  2.1 0.7 copy-start.3
  2.8 0.7 copy-start.4
  3.5 8.2 %collective-permute-start = (bf16[32,768]{1,0:T(8,128)(2,1)S(1)}, bf16[32,768]{1,0:T(8,128)(2,1)S(1)}, u32[]{:S(2)}, u32[]{:S(2)}) collective-permute-start(bf16[32,768]{1,0:T(8,128)(2,1)S(1)} %constant_dynamic-update-slice_fusion), channel_id=1, source_target_pairs={{0,1},{1,0},{2,3},{3,2},{4,5},{5,4},{6,7},{7,6},{8,9},{9,8},{10,11... | collective-permute-start | bytes 147464 | tf_op jit(solution)/shard_map/ppermute | solution.py:17
  6.8 6.8 %collective-permute-start.1 = (bf16[32,768]{1,0:T(8,128)(2,1)S(1)}, bf16[32,768]{1,0:T(8,128)(2,1)S(1)}, u32[]{:S(2)}, u32[]{:S(2)}) collective-permute-start(bf16[32,768]{1,0:T(8,128)(2,1)S(1)} %constant_dynamic-update-slice_fusion), channel_id=1, source_target_pairs={{0,2},{1,3},{2,0},{3,1},{4,6},{5,7},{6,4},{7,5},{8,10},{9,11},{10,... | collective-permute-start | bytes 147464 | tf_op jit(solution)/shard_map/ppermute | solution.py:17
  6.8 6.8 %collective-permute-start.2 = (bf16[32,768]{1,0:T(8,128)(2,1)S(1)}, bf16[32,768]{1,0:T(8,128)(2,1)S(1)}, u32[]{:S(2)}, u32[]{:S(2)}) collective-permute-start(bf16[32,768]{1,0:T(8,128)(2,1)S(1)} %constant_dynamic-update-slice_fusion), channel_id=1, source_target_pairs={{0,3},{1,2},{2,1},{3,0},{4,7},{5,6},{6,5},{7,4},{8,11},{9,10},{10,... | collective-permute-start | bytes 147464 | tf_op jit(solution)/shard_map/ppermute | solution.py:17
  9.9 4.3 %collective-permute-start.3 = (bf16[2,32,512]{2,0,1:T(2,128)(2,1)S(1)}, bf16[2,32,512]{2,0,1:T(2,128)(2,1)S(1)}, u32[]{:S(2)}, u32[]{:S(2)}) collective-permute-start(bf16[2,32,512]{2,0,1:T(2,128)(2,1)S(1)} %get-tuple-element.29), channel_id=1, source_target_pairs={{0,1},{1,0},{2,3},{3,2},{4,5},{5,4},{6,7},{7,6},{8,9},{9,8},{10,11... | collective-permute-start | bytes 196616 | tf_op jit(solution)/shard_map/ppermute | solution.py:17
  10.2 4.0 %collective-permute-start.4 = (bf16[2,32,512]{2,0,1:T(2,128)(2,1)S(1)}, bf16[2,32,512]{2,0,1:T(2,128)(2,1)S(1)}, u32[]{:S(2)}, u32[]{:S(2)}) collective-permute-start(bf16[2,32,512]{2,0,1:T(2,128)(2,1)S(1)} %get-tuple-element.31), channel_id=1, source_target_pairs={{0,2},{1,3},{2,0},{3,1},{4,6},{5,7},{6,4},{7,5},{8,10},{9,11},{10,... | collective-permute-start | bytes 196616 | tf_op jit(solution)/shard_map/ppermute | solution.py:17
  10.3 0.7 copy-start.7
  10.9 0.7 copy-start.8
  11.7 4.1 %collective-permute-start.5 = (bf16[2,32,512]{2,0,1:T(2,128)(2,1)S(1)}, bf16[2,32,512]{2,0,1:T(2,128)(2,1)S(1)}, u32[]{:S(2)}, u32[]{:S(2)}) collective-permute-start(bf16[2,32,512]{2,0,1:T(2,128)(2,1)S(1)} %get-tuple-element.30), channel_id=1, source_target_pairs={{0,3},{1,2},{2,1},{3,0},{4,7},{5,6},{6,5},{7,4},{8,11},{9,10},{10,... | collective-permute-start | bytes 196616 | tf_op jit(solution)/shard_map/ppermute | solution.py:17
  55.2 7.1 %collective-permute-start.6 = (bf16[256,4,128]{2,1,0:T(4,128)(2,1)S(1)}, bf16[256,4,128]{2,1,0:T(4,128)(2,1)S(1)}, u32[]{:S(2)}, u32[]{:S(2)}) collective-permute-start(bf16[256,4,128]{2,1,0:T(4,128)(2,1)S(1)} %slice.39), channel_id=1, source_target_pairs={{0,1},{1,0},{2,3},{3,2},{4,5},{5,4},{6,7},{7,6},{8,9},{9,8},{10,11... | collective-permute-start | bytes 786440 | tf_op jit(solution)/shard_map/ppermute | solution.py:17
  56.8 21.3 %all-to-all-start.2 = ((bf16[256,4,128]{2,1,0:T(4,128)(2,1)}), bf16[256,4,128]{2,1,0:T(4,128)(2,1)S(1)}, u32[]{:S(2)}, u32[]{:S(2)}) async-start(bf16[256,4,128]{2,1,0:T(4,128)(2,1)} %bitcast.35), calls=%async_computation.2 | async-start | bytes 524288 | tf_op jit(solution)/shard_map/all_to_all | solution.py:80
  78.1 21.3 %all-to-all-start.1 = ((bf16[256,4,128]{2,1,0:T(4,128)(2,1)}), bf16[256,4,128]{2,1,0:T(4,128)(2,1)S(1)}, u32[]{:S(2)}, u32[]{:S(2)}) async-start(bf16[256,4,128]{2,1,0:T(4,128)(2,1)} %reshape.126), calls=%async_computation.1 | async-start | bytes 524288 | tf_op jit(solution)/shard_map/all_to_all | solution.py:81
  99.9 0.7 copy-start.5
  99.9 0.7 copy-start.6
  100.9 2.3 %collective-permute-start.7 = (bf16[2,32,512]{2,1,0:T(8,128)(2,1)S(1)}, bf16[2,32,512]{2,1,0:T(8,128)(2,1)S(1)}, u32[]{:S(2)}, u32[]{:S(2)}) collective-permute-start(bf16[2,32,512]{2,1,0:T(8,128)(2,1)S(1)} %get-tuple-element.17), channel_id=1, source_target_pairs={{0,1},{1,0},{2,3},{3,2},{4,5},{5,4},{6,7},{7,6},{8,9},{9,8},{10,11... | collective-permute-start | bytes 196616 | tf_op jit(solution)/shard_map/ppermute | solution.py:17
  101.4 3.6 %collective-permute-start.8 = (bf16[2,32,512]{2,1,0:T(8,128)(2,1)S(1)}, bf16[2,32,512]{2,1,0:T(8,128)(2,1)S(1)}, u32[]{:S(2)}, u32[]{:S(2)}) collective-permute-start(bf16[2,32,512]{2,1,0:T(8,128)(2,1)S(1)} %get-tuple-element.16), channel_id=1, source_target_pairs={{0,2},{1,3},{2,0},{3,1},{4,6},{5,7},{6,4},{7,5},{8,10},{9,11},{10,... | collective-permute-start | bytes 196616 | tf_op jit(solution)/shard_map/ppermute | solution.py:17
  101.7 4.9 %collective-permute-start.9 = (bf16[2,32,512]{2,1,0:T(8,128)(2,1)S(1)}, bf16[2,32,512]{2,1,0:T(8,128)(2,1)S(1)}, u32[]{:S(2)}, u32[]{:S(2)}) collective-permute-start(bf16[2,32,512]{2,1,0:T(8,128)(2,1)S(1)} %get-tuple-element.15), channel_id=1, source_target_pairs={{0,3},{1,2},{2,1},{3,0},{4,7},{5,6},{6,5},{7,4},{8,11},{9,10},{10,... | collective-permute-start | bytes 196616 | tf_op jit(solution)/shard_map/ppermute | solution.py:17

commit v3 on v0

v3 whole, which is shorter than its diff:
```python
import jax
import jax.numpy as jnp
from jax import lax
from jax.experimental import pallas as pl
from jax.experimental.pallas import tpu as pltpu
from jax.sharding import PartitionSpec as P

epsilon = 1e-05
bf16, f32 = jnp.bfloat16, jnp.float32
vmem_bytes = 48 * 1024 * 1024


def call(kernel, name, outs, scratch, flops=0, work=1 << 20):
    return pl.pallas_call(
        kernel,
        name=name,
        out_shape=outs,
        scratch_shapes=scratch,
        compiler_params=pltpu.CompilerParams(vmem_limit_bytes=vmem_bytes),
        cost_estimate=pl.CostEstimate(flops=flops, bytes_accessed=work, transcendentals=0),
    )


def shape(*dims):
    return jax.ShapeDtypeStruct(dims, bf16)


def layer_norm(values, gain, bias):
    average = jnp.mean(values, axis=0, keepdims=True)
    centred = values - average
    variance = jnp.mean(centred * centred, axis=0, keepdims=True)
    wide = values.shape[1] // 128
    return centred * lax.rsqrt(variance + epsilon) * jnp.tile(gain, (1, wide)) + jnp.tile(
        bias, (1, wide)
    )


def column(row):
    return jnp.broadcast_to(row, (128, 128)).T


def lay_out(field, lw, lg, rw, rg, gw, fw, out0, out1, out2, out3, rows):
    mine = lax.axis_index("ch")
    for lane in range(4):
        rows[lane] = field[:, :, 128 * lane : 128 * (lane + 1)].astype(f32).reshape(256, 128)
    for step, out in enumerate((out0, out1, out2, out3)):
        for lane in range(4):
            at = slice(128 * lane, 128 * (lane + 1))
            for ii in range(2):
                out[32 * ii : 32 * (ii + 1), at] = rows[
                    lane, pl.ds(2 * (mine ^ step) + ii, 32, stride=8), :
                ].astype(bf16)
            out[64:96, at] = (lw, lg, rw, rg)[lane][...]
            out[96:112, at] = (gw, fw)[lane % 2][16 * (lane // 2) : 16 * (lane // 2 + 1), :]


def factors(in0, in1, in2, in3, gain, bias, out, normed_out, late, field, weights, rows):
    mine = lax.axis_index("ch")
    for step, block in enumerate((in0, in1, in2, in3)):
        first = pl.multiple_of((mine ^ step) * 32, 32)
        for ii in range(2):
            field[ii, pl.ds(first, 32), :] = block[32 * ii : 32 * (ii + 1), :].astype(f32)
        weights[pl.ds(first, 32), :] = block[64:96, :]
        late[pl.ds(first, 16), :] = block[96:112, 0:256]
        late[pl.ds(pl.multiple_of(first + 16, 16), 16), :] = block[96:112, 256:512]
    gains, biases = column(gain[...]), column(bias[...])
    for ii in range(2):
        normed = layer_norm(field[ii], gains, biases).astype(bf16)
        normed_out[ii] = normed

        def project(which):
            return jnp.dot(
                weights[:, 128 * which : 128 * (which + 1)], normed, preferred_element_type=f32
            )

        for side in range(2):
            factor = jax.nn.sigmoid(project(2 * side + 1)) * project(2 * side)
            for lane in range(4):
                rows[pl.ds(8 * ii + 4 * side + lane, 128, stride=16), :] = factor[
                    :, 128 * lane : 128 * (lane + 1)
                ]
    out[...] = rows[...].reshape(256, 8, 128).astype(bf16)


def gates(normed, late, out, rows):
    for ii in range(2):
        value = jax.nn.sigmoid(
            jnp.dot(late[:, 0:128], normed[ii], preferred_element_type=f32)
        )
        rows[...] = value.T
        for jj in range(2):
            out[2 * jj + ii] = rows[pl.ds(jj, 256, stride=2), :].astype(bf16)


def products(own, other, gating, out, mine_rows, other_rows, left, rows):
    core = lax.axis_index("ch") % 2
    mine_rows[...] = own[...].astype(f32).reshape(2048, 128)
    other_rows[...] = other[...].astype(f32).reshape(2048, 128)
    total = None
    for lane in range(4):
        left[lane, pl.ds(core, 256, stride=2), :] = mine_rows[pl.ds(lane, 256, stride=8), :]
        left[lane, pl.ds(1 - core, 256, stride=2), :] = other_rows[pl.ds(lane, 256, stride=8), :]
        right = mine_rows[pl.ds(4 + lane, 256, stride=8), :].astype(bf16)
        part = lax.dot_general(
            right, left[lane].astype(bf16), (((1,), (1,)), ((), ())), preferred_element_type=f32
        )
        total = part if total is None else total + part
    for lane in range(4):
        rows[pl.ds(lane, 256, stride=8), :] = total[:, 128 * lane : 128 * (lane + 1)]
        rows[pl.ds(4 + lane, 256, stride=8), :] = gating[lane].astype(f32)
    out[...] = rows[...].reshape(256, 8, 128).astype(bf16)


def updates(got, late, gain, bias, out0, out1, out2, out3, rows, gate_rows, update):
    mine = lax.axis_index("ch")
    rows[...] = got[...].astype(f32).reshape(2048, 128)
    gains, biases = column(gain[...]), column(bias[...])
    final = late[:, 128:256]
    for jj in range(2):
        for ii in range(2):
            gate_rows[pl.ds(ii, 256, stride=2), :] = rows[
                pl.ds(4 + 2 * jj + ii, 256, stride=8), :
            ]
        gating = gate_rows[...].T
        for lane in range(4):
            hidden = rows[pl.ds(8 * jj + lane, 128, stride=16), :]
            normed = layer_norm(hidden, gains, biases).astype(bf16)
            value = jnp.dot(final, normed, preferred_element_type=f32)
            at = slice(128 * lane, 128 * (lane + 1))
            update[jj, :, at] = (value * gating[:, at]).astype(bf16)
    for step, out in enumerate((out0, out1, out2, out3)):
        out[...] = update[:, pl.ds(pl.multiple_of((mine ^ step) * 32, 32), 32), :]


def arrange(in0, in1, in2, in3, out, rows):
    mine = lax.axis_index("ch")
    for lane in range(4):
        at = slice(128 * lane, 128 * (lane + 1))
        for step, block in enumerate((in0, in1, in2, in3)):
            for jj in range(2):
                rows[lane, pl.ds(2 * (mine ^ step) + jj, 32, stride=8), :] = block[
                    jj, :, at
                ].astype(f32)
        out[:, :, at] = rows[lane].reshape(32, 8, 128).astype(bf16)


def swap(array, step):
    return lax.ppermute(array, "ch", [(s, s ^ step) for s in range(4)])


def exchange(parts):
    return [parts[0]] + [swap(parts[step], step) for step in (1, 2, 3)]


def body(
    pair_field,
    input_gain,
    input_bias,
    left_weight,
    left_gate,
    right_weight,
    right_gate,
    gate_weight,
    output_gain,
    output_bias,
    final_weight,
):
    everyone = ("row", "ch")
    weights = (left_weight, left_gate, right_weight, right_gate, gate_weight, final_weight)
    parts = call(
        lay_out, "lay_out", (shape(112, 512),) * 4, [pltpu.VMEM((4, 256, 128), f32)]
    )(pair_field, *[w.T for w in weights])
    sent, normed, late = call(
        factors,
        "factors",
        (shape(256, 8, 128), shape(2, 128, 512), shape(128, 256)),
        [
            pltpu.VMEM((2, 128, 512), f32),
            pltpu.VMEM((128, 512), bf16),
            pltpu.VMEM((2048, 128), f32),
        ],
    )(*exchange(parts), input_gain.reshape(1, 128), input_bias.reshape(1, 128))
    own = lax.all_to_all(sent, everyone, 0, 0, tiled=True)
    gating = call(
        gates, "gates", shape(4, 256, 128), [pltpu.VMEM((512, 128), f32)], flops=1 << 30
    )(normed, late)
    sent = call(
        products,
        "products",
        shape(256, 8, 128),
        [
            pltpu.VMEM((2048, 128), f32),
            pltpu.VMEM((2048, 128), f32),
            pltpu.VMEM((4, 512, 128), f32),
            pltpu.VMEM((2048, 128), f32),
        ],
    )(own, swap(own, 1), gating)
    got = lax.all_to_all(sent, everyone, 0, 0, tiled=True)
    parts = call(
        updates,
        "updates",
        (shape(2, 32, 512),) * 4,
        [
            pltpu.VMEM((2048, 128), f32),
            pltpu.VMEM((512, 128), f32),
            pltpu.VMEM((2, 128, 512), bf16),
        ],
    )(got, late, output_gain.reshape(1, 128), output_bias.reshape(1, 128))
    return call(arrange, "arrange", shape(32, 8, 512), [pltpu.VMEM((4, 256, 128), f32)])(
        *exchange(parts)
    )


def solution(mesh):
    placed = (
        P("ch", "row", None),
        P(),
        P(),
        P(None, "ch"),
        P(None, "ch"),
        P(None, "ch"),
        P(None, "ch"),
        P(None, "ch"),
        P(),
        P(),
        P(None, "ch"),
    )
    return jax.shard_map(
        body, mesh=mesh, in_specs=placed, out_specs=P("ch", "row", None), check_vma=False
    )
```

time: 341 us -> 88 us (0.26)
  waiting for transfers between devices: 276 us -> 10.2 us
  blocking collectives: 25.8 us -> 59.7 us
  between operations: 13.4 us -> 0.05 us
  matrix products: 12.6 us -> 0 us
  starting transfers between devices: 0.08 us -> 7.51 us
  other arithmetic: 6.98 us -> 0 us
  Pallas kernels: 0 us -> 3.65 us
    all_gather x3 -> x0, waiting for transfers between devices: 275 us -> none  [the longest x1 224 us: body(): lax.all_gather(right_factor, 'row', axis=1, tiled=True)]
    all_to_all x1 -> x2, blocking collectives: 25.8 us -> 59.7 us  [the longest x1 33.5 us: body(): own = lax.all_to_all(sent, everyone, 0, 0, tiled=True)]
    dot_general x7 -> x0, matrix products: 12.6 us -> none  [the longest x1 10.9 us: contract(): jnp.einsum(form, first.astype(jnp.float32), second.astype(jnp.float32), p...]
    ppermute x0 -> x7, waiting for transfers between devices: none -> 10.2 us  [swap(): return lax.ppermute(array, 'ch', [(s, s ^ step) for s in range(4)])]
    ppermute x0 -> x7, starting transfers between devices: none -> 7.51 us  [swap(): return lax.ppermute(array, 'ch', [(s, s ^ step) for s in range(4)])]
    reduce_sum x4 -> x0, other arithmetic: 6.13 us -> none  [the longest x2 3.11 us: layer_norm(): variance = jnp.mean(centred * centred, axis=0, keepdims=True)]
    pallas_call x0 -> x6, Pallas kernels: none -> 3.65 us  [the longest x1 0.84 us: body(): call(arrange, 'arrange', shape(32, 8, 512), [pltpu.VMEM((4, 256, 128), f3...]
  transfers between devices with their start and end apart: 3 -> 7, of which waited for: 3 -> 5; matrix products, arithmetic and copies ran while one was open for 0% -> 0% of each run, Pallas kernels for 0% -> 0%
where the time goes in v3:
time: 88 us; the launch traced here: 87.5 us
  blocking collectives  59.7 us (68%)
  waiting for transfers between devices  10.2 us (12%)
  starting transfers between devices  7.51 us (9%)
  local copies, waits for them, and re-layouts  6.47 us (7%)
  Pallas kernels  3.65 us (4%)
    all_to_all x1, blocking collectives, body(): own = lax.all_to_all(sent, everyone, 0, 0, tiled=True)  33.5 us
    all_to_all x1, blocking collectives, body(): got = lax.all_to_all(sent, everyone, 0, 0, tiled=True)  26.1 us
    ppermute x7, waiting for transfers between devices, swap(): return lax.ppermute(array, 'ch', [(s, s ^ step) for s in range(4)])  10.2 us
    ppermute x7, starting transfers between devices, swap(): return lax.ppermute(array, 'ch', [(s, s ^ step) for s in range(4)])  7.51 us
    unnamed x22, local copies, waits for them, and re-layouts  6.47 us
  transfers between devices with their start and end apart: 7, of which 5 were waited for; matrix products, arithmetic and copies ran while one was open for 0% of the time, Pallas kernels for 0%

profile of v3, /device:TPU:1, one launch (start us, length us, event | category | flops | bytes accessed | tf_op | source)
XLA Modules:
  0.0 87.5 jit_solution(15620969796592303184)
XLA Ops:
  0.0 0.0 copy-start.1
  0.0 0.7 copy-done.1
  0.7 0.0 copy-start
  0.7 0.9 %copy-done = bf16[32,8,512]{2,1,0:T(8,128)(2,1)S(1)} copy-done((bf16[32,8,512]{2,1,0:T(8,128)(2,1)S(1)}, bf16[32,8,512]{2,1,0:T(8,128)(2,1)}, u32[]{:S(2)}) %copy-start) | copy-done | bytes 262168
  1.6 0.0 copy-start.2
  1.7 0.7 copy-done.2
  2.3 0.0 copy-start.3
  2.3 0.7 copy-done.3
  3.0 0.0 copy-start.4
  3.0 0.7 copy-done.4
  3.7 0.0 copy-start.5
  3.7 0.7 copy-done.5
  4.4 0.0 copy-start.6
  4.4 0.7 copy-done.6
  5.1 0.2 lay_out.1
  5.3 3.3 %collective-permute-start = (bf16[112,512]{1,0:T(8,128)(2,1)S(1)}, bf16[112,512]{1,0:T(8,128)(2,1)S(1)}, u32[]{:S(2)}, u32[]{:S(2)}) collective-permute-start(bf16[112,512]{1,0:T(8,128)(2,1)S(1)} %get-tuple-element.17), channel_id=1, source_target_pairs={{0,1},{1,0},{2,3},{3,2},{4,5},{5,4},{6,7},{7,6},{8,9},{9,8},{10,11... | collective-permute-start | bytes 344072 | tf_op jit(solution)/shard_map/ppermute | solution.py:148
  8.6 0.0 collective-permute-start.1
  8.6 1.7 %collective-permute-start.2 = (bf16[112,512]{1,0:T(8,128)(2,1)S(1)}, bf16[112,512]{1,0:T(8,128)(2,1)S(1)}, u32[]{:S(2)}, u32[]{:S(2)}) collective-permute-start(bf16[112,512]{1,0:T(8,128)(2,1)S(1)} %get-tuple-element.19), channel_id=1, source_target_pairs={{0,3},{1,2},{2,1},{3,0},{4,7},{5,6},{6,5},{7,4},{8,11},{9,10},{10,... | collective-permute-start | bytes 344072 | tf_op jit(solution)/shard_map/ppermute | solution.py:148
  10.4 0.0 collective-permute-done.in1
  10.4 3.0 %collective-permute-done.1.in2 = bf16[112,512]{1,0:T(8,128)(2,1)S(1)} collective-permute-done((bf16[112,512]{1,0:T(8,128)(2,1)S(1)}, bf16[112,512]{1,0:T(8,128)(2,1)S(1)}, u32[]{:S(2)}, u32[]{:S(2)}) %collective-permute-start.1) | collective-permute-done | bytes 114720 | tf_op jit(solution)/shard_map/ppermute | solution.py:148
  13.3 2.6 %collective-permute-done.2.in3 = bf16[112,512]{1,0:T(8,128)(2,1)S(1)} collective-permute-done((bf16[112,512]{1,0:T(8,128)(2,1)S(1)}, bf16[112,512]{1,0:T(8,128)(2,1)S(1)}, u32[]{:S(2)}, u32[]{:S(2)}) %collective-permute-start.2) | collective-permute-done | bytes 114720 | tf_op jit(solution)/shard_map/ppermute | solution.py:148
  16.0 0.0 copy-start.7
  16.0 0.0 copy-start.8
  16.0 0.7 copy-done.7
  16.6 0.0 copy-done.8
  16.7 0.8 factors.1
  17.4 33.5 %all_to_all.10.own = bf16[256,8,128]{2,1,0:T(8,128)(2,1)S(1)} all-to-all(bf16[256,8,128]{2,1,0:T(8,128)(2,1)S(1)} %get-tuple-element.20), channel_id=1, replica_groups=mesh['row'=64,'ch'=4] {'row','ch'}, dimensions={0} | all-to-all | bytes 1048576 | tf_op jit(solution)/shard_map/all_to_all | solution.py:183
  50.9 0.2 collective-permute-start.3
  51.2 0.4 gates.1.gating
  51.6 1.3 %collective-permute-done.3.other = bf16[256,8,128]{2,1,0:T(8,128)(2,1)S(1)} collective-permute-done((bf16[256,8,128]{2,1,0:T(8,128)(2,1)S(1)}, bf16[256,8,128]{2,1,0:T(8,128)(2,1)S(1)}, u32[]{:S(2)}, u32[]{:S(2)}) %collective-permute-start.3) | collective-permute-done | bytes 524320 | tf_op jit(solution)/shard_map/ppermute | solution.py:148
  52.9 0.8 products.1
  53.7 26.1 %all_to_all.11.got = bf16[256,8,128]{2,1,0:T(8,128)(2,1)S(1)} all-to-all(bf16[256,8,128]{2,1,0:T(8,128)(2,1)S(1)} %products.1), channel_id=1, replica_groups=mesh['row'=64,'ch'=4] {'row','ch'}, dimensions={0} | all-to-all | bytes 1048576 | tf_op jit(solution)/shard_map/all_to_all | solution.py:198
  79.8 0.0 copy-start.9
  79.8 0.0 copy-start.10
  79.8 0.7 copy-done.9
  80.5 0.0 copy-done.10
  80.5 0.6 updates.1
  81.2 0.3 collective-permute-start.4
  81.5 0.4 collective-permute-start.5
  81.9 1.5 %collective-permute-start.6 = (bf16[2,32,512]{2,1,0:T(8,128)(2,1)S(1)}, bf16[2,32,512]{2,1,0:T(8,128)(2,1)S(1)}, u32[]{:S(2)}, u32[]{:S(2)}) collective-permute-start(bf16[2,32,512]{2,1,0:T(8,128)(2,1)S(1)} %get-tuple-element.26), channel_id=1, source_target_pairs={{0,3},{1,2},{2,1},{3,0},{4,7},{5,6},{6,5},{7,4},{8,11},{9,10},{10,... | collective-permute-start | bytes 196616 | tf_op jit(solution)/shard_map/ppermute | solution.py:148
  83.4 0.0 collective-permute-done.4.in1
  83.4 1.2 %collective-permute-done.5.in2 = bf16[2,32,512]{2,1,0:T(8,128)(2,1)S(1)} collective-permute-done((bf16[2,32,512]{2,1,0:T(8,128)(2,1)S(1)}, bf16[2,32,512]{2,1,0:T(8,128)(2,1)S(1)}, u32[]{:S(2)}, u32[]{:S(2)}) %collective-permute-start.5) | collective-permute-done | bytes 65568 | tf_op jit(solution)/shard_map/ppermute | solution.py:148
  84.6 2.1 %collective-permute-done.6.in3 = bf16[2,32,512]{2,1,0:T(8,128)(2,1)S(1)} collective-permute-done((bf16[2,32,512]{2,1,0:T(8,128)(2,1)S(1)}, bf16[2,32,512]{2,1,0:T(8,128)(2,1)S(1)}, u32[]{:S(2)}, u32[]{:S(2)}) %collective-permute-start.6) | collective-permute-done | bytes 65568 | tf_op jit(solution)/shard_map/ppermute | solution.py:148
  86.7 0.8 arrange.1
Async XLA Ops:
  0.0 0.7 copy-start.1
  0.7 0.9 %copy-start = (bf16[32,8,512]{2,1,0:T(8,128)(2,1)S(1)}, bf16[32,8,512]{2,1,0:T(8,128)(2,1)}, u32[]{:S(2)}) copy-start(bf16[32,8,512]{2,1,0:T(8,128)(2,1)} %field.1) | copy-start | bytes 786436
  1.6 0.7 copy-start.2
  2.3 0.7 copy-start.3
  3.0 0.7 copy-start.4
  3.7 0.7 copy-start.5
  4.4 0.7 copy-start.6
  5.3 5.1 %collective-permute-start = (bf16[112,512]{1,0:T(8,128)(2,1)S(1)}, bf16[112,512]{1,0:T(8,128)(2,1)S(1)}, u32[]{:S(2)}, u32[]{:S(2)}) collective-permute-start(bf16[112,512]{1,0:T(8,128)(2,1)S(1)} %get-tuple-element.17), channel_id=1, source_target_pairs={{0,1},{1,0},{2,3},{3,2},{4,5},{5,4},{6,7},{7,6},{8,9},{9,8},{10,11... | collective-permute-start | bytes 344072 | tf_op jit(solution)/shard_map/ppermute | solution.py:148
  8.6 4.7 %collective-permute-start.1 = (bf16[112,512]{1,0:T(8,128)(2,1)S(1)}, bf16[112,512]{1,0:T(8,128)(2,1)S(1)}, u32[]{:S(2)}, u32[]{:S(2)}) collective-permute-start(bf16[112,512]{1,0:T(8,128)(2,1)S(1)} %get-tuple-element.18), channel_id=1, source_target_pairs={{0,2},{1,3},{2,0},{3,1},{4,6},{5,7},{6,4},{7,5},{8,10},{9,11},{10,... | collective-permute-start | bytes 344072 | tf_op jit(solution)/shard_map/ppermute | solution.py:148
  8.6 7.3 %collective-permute-start.2 = (bf16[112,512]{1,0:T(8,128)(2,1)S(1)}, bf16[112,512]{1,0:T(8,128)(2,1)S(1)}, u32[]{:S(2)}, u32[]{:S(2)}) collective-permute-start(bf16[112,512]{1,0:T(8,128)(2,1)S(1)} %get-tuple-element.19), channel_id=1, source_target_pairs={{0,3},{1,2},{2,1},{3,0},{4,7},{5,6},{6,5},{7,4},{8,11},{9,10},{10,... | collective-permute-start | bytes 344072 | tf_op jit(solution)/shard_map/ppermute | solution.py:148
  16.0 0.7 copy-start.7
  16.0 0.7 copy-start.8
  50.9 1.9 %collective-permute-start.3 = (bf16[256,8,128]{2,1,0:T(8,128)(2,1)S(1)}, bf16[256,8,128]{2,1,0:T(8,128)(2,1)S(1)}, u32[]{:S(2)}, u32[]{:S(2)}) collective-permute-start(bf16[256,8,128]{2,1,0:T(8,128)(2,1)S(1)} %all_to_all.10.own), channel_id=1, source_target_pairs={{0,1},{1,0},{2,3},{3,2},{4,5},{5,4},{6,7},{7,6},{8,9},{9,8},{10,11... | collective-permute-start | bytes 1572872 | tf_op jit(solution)/shard_map/ppermute | solution.py:148
  79.8 0.7 copy-start.9
  79.8 0.7 copy-start.10
  81.2 2.2 %collective-permute-start.4 = (bf16[2,32,512]{2,1,0:T(8,128)(2,1)S(1)}, bf16[2,32,512]{2,1,0:T(8,128)(2,1)S(1)}, u32[]{:S(2)}, u32[]{:S(2)}) collective-permute-start(bf16[2,32,512]{2,1,0:T(8,128)(2,1)S(1)} %get-tuple-element.24), channel_id=1, source_target_pairs={{0,1},{1,0},{2,3},{3,2},{4,5},{5,4},{6,7},{7,6},{8,9},{9,8},{10,11... | collective-permute-start | bytes 196616 | tf_op jit(solution)/shard_map/ppermute | solution.py:148
  81.5 3.1 %collective-permute-start.5 = (bf16[2,32,512]{2,1,0:T(8,128)(2,1)S(1)}, bf16[2,32,512]{2,1,0:T(8,128)(2,1)S(1)}, u32[]{:S(2)}, u32[]{:S(2)}) collective-permute-start(bf16[2,32,512]{2,1,0:T(8,128)(2,1)S(1)} %get-tuple-element.25), channel_id=1, source_target_pairs={{0,2},{1,3},{2,0},{3,1},{4,6},{5,7},{6,4},{7,5},{8,10},{9,11},{10,... | collective-permute-start | bytes 196616 | tf_op jit(solution)/shard_map/ppermute | solution.py:148
  81.9 4.8 %collective-permute-start.6 = (bf16[2,32,512]{2,1,0:T(8,128)(2,1)S(1)}, bf16[2,32,512]{2,1,0:T(8,128)(2,1)S(1)}, u32[]{:S(2)}, u32[]{:S(2)}) collective-permute-start(bf16[2,32,512]{2,1,0:T(8,128)(2,1)S(1)} %get-tuple-element.26), channel_id=1, source_target_pairs={{0,3},{1,2},{2,1},{3,0},{4,7},{5,6},{6,5},{7,4},{8,11},{9,10},{10,... | collective-permute-start | bytes 196616 | tf_op jit(solution)/shard_map/ppermute | solution.py:148

commit v4 on v3

v4 whole, which is shorter than its diff:
```python
import jax
import jax.numpy as jnp
from jax import lax
from jax.experimental import pallas as pl
from jax.experimental.pallas import tpu as pltpu
from jax.sharding import Mesh
from jax.sharding import PartitionSpec as P

epsilon = 1e-05
bf16, f32 = jnp.bfloat16, jnp.float32


def call(kernel, name, outs, scratch, flops=0, work=1 << 20, **more):
    return pl.pallas_call(
        kernel,
        name=name,
        out_shape=outs,
        scratch_shapes=scratch,
        cost_estimate=pl.CostEstimate(flops=flops, bytes_accessed=work, transcendentals=0),
        **more,
    )


def shape(*dims):
    return jax.ShapeDtypeStruct(dims, bf16)


def layer_norm(values, gain, bias):
    average = jnp.mean(values, axis=0, keepdims=True)
    centred = values - average
    variance = jnp.mean(centred * centred, axis=0, keepdims=True)
    wide = values.shape[1] // 128
    return centred * lax.rsqrt(variance + epsilon) * jnp.tile(gain, (1, wide)) + jnp.tile(
        bias, (1, wide)
    )


def column(row):
    return jnp.broadcast_to(row, (128, 128)).T


def position():
    return 2 * lax.axis_index("xl") + lax.axis_index("core")


def lay_out(*refs):
    sources, outs, vectors = refs[:11], refs[11:15], refs[15]
    field, weights, rows, semaphores = refs[16:]
    copies = [
        pltpu.make_async_copy(source, target, semaphores.at[at])
        for at, (source, target) in enumerate(
            zip(
                sources,
                [field]
                + [weights.at[w] for w in range(6)]
                + [vectors.at[pl.ds(v, 1)] for v in range(4)],
            )
        )
    ]
    for copy in copies:
        copy.start()
    for copy in copies:
        copy.wait()
    mine = position()
    for lane in range(4):
        rows[lane] = field[:, :, 128 * lane : 128 * (lane + 1)].astype(f32).reshape(256, 128)
    for step, out in enumerate(outs):
        for lane in range(4):
            at = slice(128 * lane, 128 * (lane + 1))
            for ii in range(2):
                out[32 * ii : 32 * (ii + 1), at] = rows[
                    lane, pl.ds(2 * (mine ^ step) + ii, 32, stride=8), :
                ].astype(bf16)
            out[64:96, at] = weights[lane]
            out[96:112, at] = weights[4 + lane % 2, 16 * (lane // 2) : 16 * (lane // 2 + 1), :]


def factors(in0, in1, in2, in3, vectors, out, normed_out, late, field, weights, rows):
    mine = position()
    for step, block in enumerate((in0, in1, in2, in3)):
        first = pl.multiple_of((mine ^ step) * 32, 32)
        for ii in range(2):
            field[ii, pl.ds(first, 32), :] = block[32 * ii : 32 * (ii + 1), :].astype(f32)
        weights[pl.ds(first, 32), :] = block[64:96, :]
        late[pl.ds(first, 16), :] = block[96:112, 0:256]
        late[pl.ds(pl.multiple_of(first + 16, 16), 16), :] = block[96:112, 256:512]
    gains, biases = column(vectors[0:1]), column(vectors[1:2])
    for ii in range(2):
        normed = layer_norm(field[ii], gains, biases).astype(bf16)
        normed_out[ii] = normed

        def project(which):
            return jnp.dot(
                weights[:, 128 * which : 128 * (which + 1)], normed, preferred_element_type=f32
            )

        for side in range(2):
            factor = jax.nn.sigmoid(project(2 * side + 1)) * project(2 * side)
            for lane in range(4):
                rows[pl.ds(8 * side + 4 * ii + lane, 128, stride=16), :] = factor[
                    :, 128 * lane : 128 * (lane + 1)
                ]
    out[...] = rows[...].reshape(128, 16, 128).astype(bf16)


def gates(normed, late, kept, given, rows):
    core = lax.axis_index("core")
    for ii in range(2):
        value = jax.nn.sigmoid(
            jnp.dot(late[:, 0:128], normed[ii], preferred_element_type=f32)
        )
        rows[...] = value.T
        for jj in range(2):
            kept[2 * ii + jj] = rows[pl.ds(2 * core + jj, 128, stride=4), :].astype(bf16)
            given[2 * ii + jj] = rows[pl.ds(2 * (1 - core) + jj, 128, stride=4), :].astype(bf16)


def products(own, other, kept, given, out, mine_rows, other_rows, left, rows):
    core = lax.axis_index("core")
    mine_rows[...] = own[...].astype(f32).reshape(2048, 128)
    other_rows[...] = other[...].astype(f32).reshape(1024, 128)
    total = None
    for lane in range(4):
        for ii in range(2):
            left[lane, pl.ds(2 * core + ii, 128, stride=4), :] = mine_rows[
                pl.ds(4 * ii + lane, 128, stride=16), :
            ]
            left[lane, pl.ds(2 * (1 - core) + ii, 128, stride=4), :] = other_rows[
                pl.ds(4 * ii + lane, 128, stride=8), :
            ]
        right = jnp.concatenate(
            [mine_rows[pl.ds(8 + 4 * jj + lane, 128, stride=16), :] for jj in range(2)], axis=0
        ).astype(bf16)
        part = lax.dot_general(
            right, left[lane].astype(bf16), (((1,), (1,)), ((), ())), preferred_element_type=f32
        )
        total = part if total is None else total + part
    for jj in range(2):
        for lane in range(4):
            rows[pl.ds(4 * jj + lane, 128, stride=16), :] = total[
                128 * jj : 128 * (jj + 1), 128 * lane : 128 * (lane + 1)
            ]
        for ii in range(2):
            at = 8 + 4 * jj + ii
            rows[pl.ds(at + 2 * core, 128, stride=16), :] = kept[2 * ii + jj].astype(f32)
            rows[pl.ds(at + 2 * (1 - core), 128, stride=16), :] = given[2 * ii + jj].astype(f32)
    out[...] = rows[...].reshape(128, 16, 128).astype(bf16)


def updates(got, late, vectors, out0, out1, out2, out3, rows, gate_rows, update):
    mine = position()
    rows[...] = got[...].astype(f32).reshape(2048, 128)
    gains, biases = column(vectors[2:3]), column(vectors[3:4])
    final = late[:, 128:256]
    for jj in range(2):
        for ii in range(4):
            gate_rows[pl.ds(ii, 128, stride=4), :] = rows[
                pl.ds(8 + 4 * jj + ii, 128, stride=16), :
            ]
        gating = gate_rows[...].T
        for lane in range(4):
            hidden = rows[pl.ds(4 * jj + lane, 128, stride=16), :]
            normed = layer_norm(hidden, gains, biases).astype(bf16)
            value = jnp.dot(final, normed, preferred_element_type=f32)
            at = slice(128 * lane, 128 * (lane + 1))
            update[jj, :, at] = (value * gating[:, at]).astype(bf16)
    for step, out in enumerate((out0, out1, out2, out3)):
        out[...] = update[:, pl.ds(pl.multiple_of((mine ^ step) * 32, 32), 32), :]


def arrange(in0, in1, in2, in3, out, rows):
    mine = position()
    for lane in range(4):
        at = slice(128 * lane, 128 * (lane + 1))
        for step, block in enumerate((in0, in1, in2, in3)):
            for jj in range(2):
                rows[lane, pl.ds(2 * (mine ^ step) + jj, 32, stride=8), :] = block[
                    jj, :, at
                ].astype(f32)
        out[:, :, at] = rows[lane].reshape(32, 8, 128).astype(bf16)


def swap(array, step):
    return lax.ppermute(array, ("xl", "core"), [(s, s ^ step) for s in range(4)])


def exchange(parts):
    return [parts[0]] + [swap(parts[step], step) for step in (1, 2, 3)]


def body(
    pair_field,
    input_gain,
    input_bias,
    left_weight,
    left_gate,
    right_weight,
    right_gate,
    gate_weight,
    output_gain,
    output_bias,
    final_weight,
):
    same_core = ("row", "xl")
    weights = (left_weight, left_gate, right_weight, right_gate, gate_weight, final_weight)
    vectors = (input_gain, input_bias, output_gain, output_bias)
    *parts, vectors = call(
        lay_out,
        "lay_out",
        (shape(112, 512),) * 4 + (jax.ShapeDtypeStruct((4, 128), f32),),
        [
            pltpu.VMEM((32, 8, 512), bf16),
            pltpu.VMEM((6, 32, 128), bf16),
            pltpu.VMEM((4, 256, 128), f32),
            pltpu.SemaphoreType.DMA((11,)),
        ],
        in_specs=[pl.BlockSpec(memory_space=pl.ANY)] * 11,
    )(pair_field, *[w.T for w in weights], *[v.reshape(1, 128) for v in vectors])
    sent, normed, late = call(
        factors,
        "factors",
        (shape(128, 16, 128), shape(2, 128, 512), shape(128, 256)),
        [
            pltpu.VMEM((2, 128, 512), f32),
            pltpu.VMEM((128, 512), bf16),
            pltpu.VMEM((2048, 128), f32),
        ],
    )(*exchange(parts), vectors)
    own = lax.all_to_all(sent, same_core, 0, 0, tiled=True)
    kept, given = call(
        gates,
        "gates",
        (shape(4, 128, 128),) * 2,
        [pltpu.VMEM((512, 128), f32)],
        flops=1 << 30,
    )(normed, late)
    sent = call(
        products,
        "products",
        shape(128, 16, 128),
        [
            pltpu.VMEM((2048, 128), f32),
            pltpu.VMEM((1024, 128), f32),
            pltpu.VMEM((4, 512, 128), f32),
            pltpu.VMEM((2048, 128), f32),
        ],
    )(own, swap(own[:, :8], 1), kept, swap(given, 1))
    got = lax.all_to_all(sent, same_core, 0, 0, tiled=True)
    parts = call(
        updates,
        "updates",
        (shape(2, 32, 512),) * 4,
        [
            pltpu.VMEM((2048, 128), f32),
            pltpu.VMEM((512, 128), f32),
            pltpu.VMEM((2, 128, 512), bf16),
        ],
    )(got, late, vectors)
    return call(arrange, "arrange", shape(32, 8, 512), [pltpu.VMEM((4, 256, 128), f32)])(
        *exchange(parts)
    )


def solution(mesh):
    mesh = Mesh(mesh.devices.reshape(64, 2, 2), ("row", "xl", "core"))
    ch = ("xl", "core")
    placed = (
        P(ch, "row", None),
        P(),
        P(),
        P(None, ch),
        P(None, ch),
        P(None, ch),
        P(None, ch),
        P(None, ch),
        P(),
        P(),
        P(None, ch),
    )
    return jax.shard_map(
        body, mesh=mesh, in_specs=placed, out_specs=P(ch, "row", None), check_vma=False
    )
```

time: 88 us -> 96.1 us (1.092)
  Pallas kernels: 3.65 us -> 13.8 us
  local copies, waits for them, and re-layouts: 6.47 us -> 2.04 us
  starting transfers between devices: 7.51 us -> 11.3 us
  blocking collectives: 59.7 us -> 57.4 us
    pallas_call x4, Pallas kernels: 2.17 us -> 9.58 us  [the longest x1 2.98 us: body(): call(products, 'products', shape(128, 16, 128), [pltpu.VMEM((2048, 128),...]
    unnamed x22 -> x18, local copies, waits for them, and re-layouts: 6.47 us -> 2.02 us
    ppermute x7 -> x8, starting transfers between devices: 7.51 us -> 11.3 us  [swap(): lax.ppermute(array, ('xl', 'core'), [(s, s ^ step) for s in range(4)])]
    all_to_all x2, blocking collectives: 59.7 us -> 57.4 us  [the longest x1 31.7 us: body(): own = lax.all_to_all(sent, same_core, 0, 0, tiled=True)]
    pallas_call x1, Pallas kernels: 0.64 us -> 2.46 us  [body(): call(updates, 'updates', (shape(2, 32, 512),) * 4, [pltpu.VMEM((2048, 128...]
    ppermute x7 -> x8, waiting for transfers between devices: 10.2 us -> 11.1 us  [swap(): lax.ppermute(array, ('xl', 'core'), [(s, s ^ step) for s in range(4)])]
  transfers between devices with their start and end apart: 7 -> 8, of which waited for: 5 -> 5; matrix products, arithmetic and copies ran while one was open for 0% -> 0% of each run, Pallas kernels for 0% -> 2%
where the time goes in v4:
time: 96.1 us; the launch traced here: 95.7 us
  blocking collectives  57.4 us (60%)
  Pallas kernels  13.8 us (14%)
  starting transfers between devices  11.3 us (12%)
  waiting for transfers between devices  11.1 us (12%)
  local copies, waits for them, and re-layouts  2.04 us (2%)
    all_to_all x1, blocking collectives, body(): own = lax.all_to_all(sent, same_core, 0, 0, tiled=True)  31.7 us
    all_to_all x1, blocking collectives, body(): got = lax.all_to_all(sent, same_core, 0, 0, tiled=True)  25.7 us
    ppermute x8, starting transfers between devices, swap(): lax.ppermute(array, ('xl', 'core'), [(s, s ^ step) for s in range(4)])  11.3 us
    ppermute x8, waiting for transfers between devices, swap(): lax.ppermute(array, ('xl', 'core'), [(s, s ^ step) for s in range(4)])  11.1 us
    pallas_call x1, Pallas kernels, body(): call(products, 'products', shape(128, 16, 128), [pltpu.VMEM((2048, 128),...  2.98 us
    pallas_call x1, Pallas kernels, body(): call(factors, 'factors', (shape(128, 16, 128), shape(2, 128, 512), shape(...  2.64 us
    pallas_call x1, Pallas kernels, body(): call(updates, 'updates', (shape(2, 32, 512),) * 4, [pltpu.VMEM((2048, 128...  2.46 us
    pallas_call x1, Pallas kernels, body(): call(gates, 'gates', (shape(4, 128, 128),) * 2, [pltpu.VMEM((512, 128), f...  2.04 us
  transfers between devices with their start and end apart: 8, of which 5 were waited for; matrix products, arithmetic and copies ran while one was open for 0% of the time, Pallas kernels for 2%

profile of v4, /device:TPU:1, one launch (start us, length us, event | category | flops | bytes accessed | tf_op | source)
XLA Modules:
  0.0 95.7 jit_solution(10042085516890784398)
XLA Ops:
  0.0 1.9 %lay_out.1 = (bf16[112,512]{1,0:T(8,128)(2,1)}, bf16[112,512]{1,0:T(8,128)(2,1)}, bf16[112,512]{1,0:T(8,128)(2,1)}, bf16[112,512]{1,0:T(8,128)(2,1)}, f32[4,128]{1,0:T(4,128)}) custom-call(bf16[32,8,512]{2,1,0:T(8,128)(2,1)} %refs_0_.1, bf16[32,128]{1,0:T(8,128)(2,1)} %bitcast.10, bf16[32,128]{1,0:T(8,128)(2,1)} %bitcast.11, bf16[32,128]{1,0:T(8,128)(2,1)} %bitcast.12, ...), custom_call_target="tpu_custom_call" | custom-call | bytes 1048576 | tf_op jit(solution)/shard_map/lay_out/pallas_call | solution.py:207
  1.9 3.3 %collective-permute-start = (bf16[112,512]{1,0:T(8,128)(2,1)}, bf16[112,512]{1,0:T(8,128)(2,1)S(1)}, u32[]{:S(2)}, u32[]{:S(2)}) collective-permute-start(bf16[112,512]{1,0:T(8,128)(2,1)} %get-tuple-element.20), channel_id=1, source_target_pairs={{0,1},{1,0},{2,3},{3,2},{4,5},{5,4},{6,7},{7,6},{8,9},{9,8},{10,11... | collective-permute-start | bytes 344072 | tf_op jit(solution)/shard_map/ppermute | solution.py:184
  5.3 0.0 collective-permute-start.1
  5.3 1.7 %collective-permute-start.2 = (bf16[112,512]{1,0:T(8,128)(2,1)}, bf16[112,512]{1,0:T(8,128)(2,1)S(1)}, u32[]{:S(2)}, u32[]{:S(2)}) collective-permute-start(bf16[112,512]{1,0:T(8,128)(2,1)} %get-tuple-element.22), channel_id=1, source_target_pairs={{0,3},{1,2},{2,1},{3,0},{4,7},{5,6},{6,5},{7,4},{8,11},{9,10},{10,... | collective-permute-start | bytes 344072 | tf_op jit(solution)/shard_map/ppermute | solution.py:184
  7.0 0.0 collective-permute-done.in1
  7.0 0.0 copy-start.3
  7.0 3.2 %collective-permute-done.1.in2 = bf16[112,512]{1,0:T(8,128)(2,1)S(1)} collective-permute-done((bf16[112,512]{1,0:T(8,128)(2,1)}, bf16[112,512]{1,0:T(8,128)(2,1)S(1)}, u32[]{:S(2)}, u32[]{:S(2)}) %collective-permute-start.1) | collective-permute-done | bytes 114720 | tf_op jit(solution)/shard_map/ppermute | solution.py:184
  10.2 0.0 copy-start.4
  10.2 2.6 %collective-permute-done.2.in3 = bf16[112,512]{1,0:T(8,128)(2,1)S(1)} collective-permute-done((bf16[112,512]{1,0:T(8,128)(2,1)}, bf16[112,512]{1,0:T(8,128)(2,1)S(1)}, u32[]{:S(2)}, u32[]{:S(2)}) %collective-permute-start.2) | collective-permute-done | bytes 114720 | tf_op jit(solution)/shard_map/ppermute | solution.py:184
  12.8 0.0 copy-start.5
  12.8 0.0 copy-done.3
  12.8 0.0 copy-done.4
  12.8 0.6 copy-done.5
  13.5 2.6 %factors.1 = (bf16[128,16,128]{2,1,0:T(8,128)(2,1)}, bf16[2,128,512]{2,1,0:T(8,128)(2,1)}, bf16[128,256]{1,0:T(8,128)(2,1)}) custom-call(bf16[112,512]{1,0:T(8,128)(2,1)} %get-tuple-element.19.in0, bf16[112,512]{1,0:T(8,128)(2,1)} %copy-done.3, bf16[112,512]{1,0:T(8,128)(2,1)} %copy-done.4, bf16[112,512]{1,0:T(8,128)(2,1)} %copy-done.5, ...), custom_call_target="tpu_custom_call" | custom-call | bytes 1048576 | tf_op jit(solution)/shard_map/factors/pallas_call | solution.py:219
  16.1 31.7 %all_to_all.10.own = bf16[128,16,128]{2,1,0:T(8,128)(2,1)S(1)} all-to-all(bf16[128,16,128]{2,1,0:T(8,128)(2,1)} %get-tuple-element.24), channel_id=1, replica_groups=mesh['row'=64,'xl'=2,'core'=2] {'row','xl'}, dimensions={0} | all-to-all | bytes 1048576 | tf_op jit(solution)/shard_map/all_to_all | solution.py:229
  47.8 0.0 copy-start
  47.9 2.9 %collective-permute-start.3 = (bf16[128,8,128]{2,1,0:T(8,128)(2,1)S(1)}, bf16[128,8,128]{2,1,0:T(8,128)(2,1)S(1)}, u32[]{:S(2)}, u32[]{:S(2)}) collective-permute-start(bf16[128,8,128]{2,1,0:T(8,128)(2,1)S(1)} %slice.4), channel_id=1, source_target_pairs={{0,1},{1,0},{2,3},{3,2},{4,5},{5,4},{6,7},{7,6},{8,9},{9,8},{10,11... | collective-permute-start | bytes 786440 | tf_op jit(solution)/shard_map/ppermute | solution.py:184
  50.7 2.0 %gates.1 = (bf16[4,128,128]{2,1,0:T(8,128)(2,1)}, bf16[4,128,128]{2,1,0:T(8,128)(2,1)}) custom-call(bf16[2,128,512]{2,1,0:T(8,128)(2,1)} %get-tuple-element.25.normed, bf16[128,256]{1,0:T(8,128)(2,1)} %get-tuple-element.26.late), custom_call_target="tpu_custom_call" | custom-call | flops 1073741824 | bytes 1048576 | tf_op jit(solution)/shard_map/gates/pallas_call | solution.py:230
  52.8 0.0 copy-done
  52.8 0.1 collective-permute-start.4
  52.9 1.5 %collective-permute-done.4.given = bf16[4,128,128]{2,1,0:T(8,128)(2,1)S(1)} collective-permute-done((bf16[4,128,128]{2,1,0:T(8,128)(2,1)}, bf16[4,128,128]{2,1,0:T(8,128)(2,1)S(1)}, u32[]{:S(2)}, u32[]{:S(2)}) %collective-permute-start.4) | collective-permute-done | bytes 131104 | tf_op jit(solution)/shard_map/ppermute | solution.py:184
  54.3 0.0 copy-start.2
  54.4 0.0 collective-permute-done.3.other
  54.4 0.0 copy-start.1
  54.4 0.6 copy-done.2
  55.0 0.1 copy-done.1
  55.1 3.0 %products.1 = bf16[128,16,128]{2,1,0:T(8,128)(2,1)} custom-call(bf16[128,16,128]{2,1,0:T(8,128)(2,1)} %copy-done, bf16[128,8,128]{2,1,0:T(8,128)(2,1)} %copy-done.1, bf16[4,128,128]{2,1,0:T(8,128)(2,1)} %get-tuple-element.27.kept, bf16[4,128,128]{2,1,0:T(8,128)(2,1)} %copy-done.2), custom_call_target="tpu_custom_call" | custom-call | bytes 1048576 | tf_op jit(solution)/shard_map/products/pallas_call | solution.py:237
  58.1 25.7 %all_to_all.11.got = bf16[128,16,128]{2,1,0:T(8,128)(2,1)} all-to-all(bf16[128,16,128]{2,1,0:T(8,128)(2,1)} %products.1), channel_id=1, replica_groups=mesh['row'=64,'xl'=2,'core'=2] {'row','xl'}, dimensions={0} | all-to-all | bytes 1048576 | tf_op jit(solution)/shard_map/all_to_all | solution.py:248
  83.7 2.5 %updates.1 = (bf16[2,32,512]{2,1,0:T(8,128)(2,1)}, bf16[2,32,512]{2,1,0:T(8,128)(2,1)}, bf16[2,32,512]{2,1,0:T(8,128)(2,1)}, bf16[2,32,512]{2,1,0:T(8,128)(2,1)}) custom-call(bf16[128,16,128]{2,1,0:T(8,128)(2,1)} %all_to_all.11.got, bf16[128,256]{1,0:T(8,128)(2,1)} %get-tuple-element.26.late, f32[4,128]{1,0:T(4,128)} %get-tuple-element.23.vectors), custom_call_target="tpu_custom_call" | custom-call | bytes 1048576 | tf_op jit(solution)/shard_map/updates/pallas_call | solution.py:249
  86.2 1.7 %collective-permute-start.5 = (bf16[2,32,512]{2,1,0:T(8,128)(2,1)}, bf16[2,32,512]{2,1,0:T(8,128)(2,1)S(1)}, u32[]{:S(2)}, u32[]{:S(2)}) collective-permute-start(bf16[2,32,512]{2,1,0:T(8,128)(2,1)} %get-tuple-element.30), channel_id=1, source_target_pairs={{0,1},{1,0},{2,3},{3,2},{4,5},{5,4},{6,7},{7,6},{8,9},{9,8},{10,11... | collective-permute-start | bytes 196616 | tf_op jit(solution)/shard_map/ppermute | solution.py:184
  87.9 0.9 collective-permute-start.6
  88.8 0.8 collective-permute-start.7
  89.5 0.0 collective-permute-done.5.in1
  89.5 0.0 copy-start.6
  89.5 2.3 %collective-permute-done.6.in2 = bf16[2,32,512]{2,1,0:T(8,128)(2,1)S(1)} collective-permute-done((bf16[2,32,512]{2,1,0:T(8,128)(2,1)}, bf16[2,32,512]{2,1,0:T(8,128)(2,1)S(1)}, u32[]{:S(2)}, u32[]{:S(2)}) %collective-permute-start.6) | collective-permute-done | bytes 65568 | tf_op jit(solution)/shard_map/ppermute | solution.py:184
  91.8 0.0 copy-start.7
  91.8 1.5 %collective-permute-done.7.in3 = bf16[2,32,512]{2,1,0:T(8,128)(2,1)S(1)} collective-permute-done((bf16[2,32,512]{2,1,0:T(8,128)(2,1)}, bf16[2,32,512]{2,1,0:T(8,128)(2,1)S(1)}, u32[]{:S(2)}, u32[]{:S(2)}) %collective-permute-start.7) | collective-permute-done | bytes 65568 | tf_op jit(solution)/shard_map/ppermute | solution.py:184
  93.3 0.0 copy-start.8
  93.3 0.0 copy-done.6
  93.3 0.0 copy-done.7
  93.3 0.6 copy-done.8
  94.0 1.8 %arrange.1 = bf16[32,8,512]{2,1,0:T(8,128)(2,1)} custom-call(bf16[2,32,512]{2,1,0:T(8,128)(2,1)} %get-tuple-element.29.in0, bf16[2,32,512]{2,1,0:T(8,128)(2,1)} %copy-done.6, bf16[2,32,512]{2,1,0:T(8,128)(2,1)} %copy-done.7, bf16[2,32,512]{2,1,0:T(8,128)(2,1)} %copy-done.8), custom_call_target="tpu_custom_call" | custom-call | bytes 1048576 | tf_op jit(solution)/shard_map/arrange/pallas_call | solution.py:259
  (1 shorter events, 0.0 us)
Async XLA Ops:
  1.9 5.1 %collective-permute-start = (bf16[112,512]{1,0:T(8,128)(2,1)}, bf16[112,512]{1,0:T(8,128)(2,1)S(1)}, u32[]{:S(2)}, u32[]{:S(2)}) collective-permute-start(bf16[112,512]{1,0:T(8,128)(2,1)} %get-tuple-element.20), channel_id=1, source_target_pairs={{0,1},{1,0},{2,3},{3,2},{4,5},{5,4},{6,7},{7,6},{8,9},{9,8},{10,11... | collective-permute-start | bytes 344072 | tf_op jit(solution)/shard_map/ppermute | solution.py:184
  5.3 4.9 %collective-permute-start.1 = (bf16[112,512]{1,0:T(8,128)(2,1)}, bf16[112,512]{1,0:T(8,128)(2,1)S(1)}, u32[]{:S(2)}, u32[]{:S(2)}) collective-permute-start(bf16[112,512]{1,0:T(8,128)(2,1)} %get-tuple-element.21), channel_id=1, source_target_pairs={{0,2},{1,3},{2,0},{3,1},{4,6},{5,7},{6,4},{7,5},{8,10},{9,11},{10,... | collective-permute-start | bytes 344072 | tf_op jit(solution)/shard_map/ppermute | solution.py:184
  5.3 7.6 %collective-permute-start.2 = (bf16[112,512]{1,0:T(8,128)(2,1)}, bf16[112,512]{1,0:T(8,128)(2,1)S(1)}, u32[]{:S(2)}, u32[]{:S(2)}) collective-permute-start(bf16[112,512]{1,0:T(8,128)(2,1)} %get-tuple-element.22), channel_id=1, source_target_pairs={{0,3},{1,2},{2,1},{3,0},{4,7},{5,6},{6,5},{7,4},{8,11},{9,10},{10,... | collective-permute-start | bytes 344072 | tf_op jit(solution)/shard_map/ppermute | solution.py:184
  7.0 5.8 %copy-start.3 = (bf16[112,512]{1,0:T(8,128)(2,1)}, bf16[112,512]{1,0:T(8,128)(2,1)S(1)}, u32[]{:S(2)}) copy-start(bf16[112,512]{1,0:T(8,128)(2,1)S(1)} %collective-permute-done.in1) | copy-start | bytes 344068
  10.2 2.6 %copy-start.4 = (bf16[112,512]{1,0:T(8,128)(2,1)}, bf16[112,512]{1,0:T(8,128)(2,1)S(1)}, u32[]{:S(2)}) copy-start(bf16[112,512]{1,0:T(8,128)(2,1)S(1)} %collective-permute-done.1.in2) | copy-start | bytes 344068
  12.8 0.7 copy-start.5
  47.8 5.0 %copy-start = (bf16[128,16,128]{2,1,0:T(8,128)(2,1)}, bf16[128,16,128]{2,1,0:T(8,128)(2,1)S(1)}, u32[]{:S(2)}) copy-start(bf16[128,16,128]{2,1,0:T(8,128)(2,1)S(1)} %all_to_all.10.own) | copy-start | bytes 1572868
  47.9 6.5 %collective-permute-start.3 = (bf16[128,8,128]{2,1,0:T(8,128)(2,1)S(1)}, bf16[128,8,128]{2,1,0:T(8,128)(2,1)S(1)}, u32[]{:S(2)}, u32[]{:S(2)}) collective-permute-start(bf16[128,8,128]{2,1,0:T(8,128)(2,1)S(1)} %slice.4), channel_id=1, source_target_pairs={{0,1},{1,0},{2,3},{3,2},{4,5},{5,4},{6,7},{7,6},{8,9},{9,8},{10,11... | collective-permute-start | bytes 786440 | tf_op jit(solution)/shard_map/ppermute | solution.py:184
  52.8 1.6 %collective-permute-start.4 = (bf16[4,128,128]{2,1,0:T(8,128)(2,1)}, bf16[4,128,128]{2,1,0:T(8,128)(2,1)S(1)}, u32[]{:S(2)}, u32[]{:S(2)}) collective-permute-start(bf16[4,128,128]{2,1,0:T(8,128)(2,1)} %get-tuple-element.28), channel_id=1, source_target_pairs={{0,1},{1,0},{2,3},{3,2},{4,5},{5,4},{6,7},{7,6},{8,9},{9,8},{10,11... | collective-permute-start | bytes 393224 | tf_op jit(solution)/shard_map/ppermute | solution.py:184
  54.3 0.6 copy-start.2
  54.4 0.7 copy-start.1
  86.2 3.3 %collective-permute-start.5 = (bf16[2,32,512]{2,1,0:T(8,128)(2,1)}, bf16[2,32,512]{2,1,0:T(8,128)(2,1)S(1)}, u32[]{:S(2)}, u32[]{:S(2)}) collective-permute-start(bf16[2,32,512]{2,1,0:T(8,128)(2,1)} %get-tuple-element.30), channel_id=1, source_target_pairs={{0,1},{1,0},{2,3},{3,2},{4,5},{5,4},{6,7},{7,6},{8,9},{9,8},{10,11... | collective-permute-start | bytes 196616 | tf_op jit(solution)/shard_map/ppermute | solution.py:184
  87.9 3.9 %collective-permute-start.6 = (bf16[2,32,512]{2,1,0:T(8,128)(2,1)}, bf16[2,32,512]{2,1,0:T(8,128)(2,1)S(1)}, u32[]{:S(2)}, u32[]{:S(2)}) collective-permute-start(bf16[2,32,512]{2,1,0:T(8,128)(2,1)} %get-tuple-element.31), channel_id=1, source_target_pairs={{0,2},{1,3},{2,0},{3,1},{4,6},{5,7},{6,4},{7,5},{8,10},{9,11},{10,... | collective-permute-start | bytes 196616 | tf_op jit(solution)/shard_map/ppermute | solution.py:184
  88.8 4.6 %collective-permute-start.7 = (bf16[2,32,512]{2,1,0:T(8,128)(2,1)}, bf16[2,32,512]{2,1,0:T(8,128)(2,1)S(1)}, u32[]{:S(2)}, u32[]{:S(2)}) collective-permute-start(bf16[2,32,512]{2,1,0:T(8,128)(2,1)} %get-tuple-element.32), channel_id=1, source_target_pairs={{0,3},{1,2},{2,1},{3,0},{4,7},{5,6},{6,5},{7,4},{8,11},{9,10},{10,... | collective-permute-start | bytes 196616 | tf_op jit(solution)/shard_map/ppermute | solution.py:184
  89.5 3.8 %copy-start.6 = (bf16[2,32,512]{2,1,0:T(8,128)(2,1)}, bf16[2,32,512]{2,1,0:T(8,128)(2,1)S(1)}, u32[]{:S(2)}) copy-start(bf16[2,32,512]{2,1,0:T(8,128)(2,1)S(1)} %collective-permute-done.5.in1) | copy-start | bytes 196612
  91.8 1.5 %copy-start.7 = (bf16[2,32,512]{2,1,0:T(8,128)(2,1)}, bf16[2,32,512]{2,1,0:T(8,128)(2,1)S(1)}, u32[]{:S(2)}) copy-start(bf16[2,32,512]{2,1,0:T(8,128)(2,1)S(1)} %collective-permute-done.6.in2) | copy-start | bytes 196612
  93.3 0.6 copy-start.8

commit v5 on v4

--- a/solution.py
+++ b/solution.py
@@ -8,15 +8,17 @@
 
 epsilon = 1e-05
 bf16, f32 = jnp.bfloat16, jnp.float32
-
-
-def call(kernel, name, outs, scratch, flops=0, work=1 << 20, **more):
+vmem_bytes = 16 * 1024 * 1024
+
+
+def call(kernel, name, outs, scratch, flops=0, work=1 << 20, limit=vmem_bytes, **more):
     return pl.pallas_call(
         kernel,
         name=name,
         out_shape=outs,
         scratch_shapes=scratch,
         cost_estimate=pl.CostEstimate(flops=flops, bytes_accessed=work, transcendentals=0),
+        compiler_params=pltpu.CompilerParams(vmem_limit_bytes=limit),
         **more,
     )
 
@@ -214,7 +216,8 @@
             pltpu.VMEM((4, 256, 128), f32),
             pltpu.SemaphoreType.DMA((11,)),
         ],
-        in_specs=[pl.BlockSpec(memory_space=pl.ANY)] * 11,
+        limit=60 * 1024 * 1024,
+        in_specs=[pl.BlockSpec(memory_space=pltpu.HBM)] * 11,
     )(pair_field, *[w.T for w in weights], *[v.reshape(1, 128) for v in vectors])
     sent, normed, late = call(
         factors,

time: 96.1 us -> 85.6 us (0.89)
  Pallas kernels: 13.8 us -> 5.61 us
  blocking collectives: 57.4 us -> 55.7 us
  local copies, waits for them, and re-layouts: 2.04 us -> 0.92 us
  starting transfers between devices: 11.3 us -> 12.4 us
    pallas_call x1, Pallas kernels: 2.98 us -> 1.02 us  [body(): call(products, 'products', shape(128, 16, 128), [pltpu.VMEM((2048, 128),...]
    pallas_call x1, Pallas kernels: 2.64 us -> 0.76 us  [body(): call(factors, 'factors', (shape(128, 16, 128), shape(2, 128, 512), shape(...]
    pallas_call x1, Pallas kernels: 2.46 us -> 0.69 us  [body(): call(updates, 'updates', (shape(2, 32, 512),) * 4, [pltpu.VMEM((2048, 128...]
    pallas_call x1, Pallas kernels: 2.04 us -> 0.38 us  [body(): call(gates, 'gates', (shape(4, 128, 128),) * 2, [pltpu.VMEM((512, 128), f...]
    all_to_all x1, blocking collectives: 25.7 us -> 24.2 us  [body(): got = lax.all_to_all(sent, same_core, 0, 0, tiled=True)]
    unnamed x18 -> x4, local copies, waits for them, and re-layouts: 2.02 us -> 0.9 us
    ppermute x8, starting transfers between devices: 11.3 us -> 12.4 us  [swap(): lax.ppermute(array, ('xl', 'core'), [(s, s ^ step) for s in range(4)])]
  transfers between devices with their start and end apart: 8 -> 8, of which waited for: 5 -> 5; matrix products, arithmetic and copies ran while one was open for 0% -> 0% of each run, Pallas kernels for 2% -> 0%
where the time goes in v5:
time: 85.6 us; the launch traced here: 85.4 us
  blocking collectives  55.7 us (65%)
  starting transfers between devices  12.4 us (14%)
  waiting for transfers between devices  10.7 us (12%)
  Pallas kernels  5.61 us (7%)
  local copies, waits for them, and re-layouts  0.92 us (1%)
    all_to_all x1, blocking collectives, body(): own = lax.all_to_all(sent, same_core, 0, 0, tiled=True)  31.5 us
    all_to_all x1, blocking collectives, body(): got = lax.all_to_all(sent, same_core, 0, 0, tiled=True)  24.2 us
    ppermute x8, starting transfers between devices, swap(): lax.ppermute(array, ('xl', 'core'), [(s, s ^ step) for s in range(4)])  12.4 us
    ppermute x8, waiting for transfers between devices, swap(): lax.ppermute(array, ('xl', 'core'), [(s, s ^ step) for s in range(4)])  10.7 us
    pallas_call x1, Pallas kernels, body(): call(lay_out, 'lay_out', (shape(112, 512),) * 4 + (jax.ShapeDtypeStruct((...  1.92 us
  transfers between devices with their start and end apart: 8, of which 5 were waited for; matrix products, arithmetic and copies ran while one was open for 0% of the time, Pallas kernels for 0%

profile of v5, /device:TPU:1, one launch (start us, length us, event | category | flops | bytes accessed | tf_op | source)
XLA Modules:
  0.0 85.4 jit_solution(3437670332695490743)
XLA Ops:
  0.0 1.9 %lay_out.1 = (bf16[112,512]{1,0:T(8,128)(2,1)}, bf16[112,512]{1,0:T(8,128)(2,1)}, bf16[112,512]{1,0:T(8,128)(2,1)}, bf16[112,512]{1,0:T(8,128)(2,1)}, f32[4,128]{1,0:T(4,128)}) custom-call(bf16[32,8,512]{2,1,0:T(8,128)(2,1)} %refs_0_.1, bf16[32,128]{1,0:T(8,128)(2,1)} %bitcast.10, bf16[32,128]{1,0:T(8,128)(2,1)} %bitcast.11, bf16[32,128]{1,0:T(8,128)(2,1)} %bitcast.12, ...), custom_call_target="tpu_custom_call" | custom-call | bytes 1048576 | tf_op jit(solution)/shard_map/lay_out/pallas_call | solution.py:209
  1.9 3.3 %collective-permute-start = (bf16[112,512]{1,0:T(8,128)(2,1)}, bf16[112,512]{1,0:T(8,128)(2,1)S(1)}, u32[]{:S(2)}, u32[]{:S(2)}) collective-permute-start(bf16[112,512]{1,0:T(8,128)(2,1)} %get-tuple-element.20), channel_id=1, source_target_pairs={{0,1},{1,0},{2,3},{3,2},{4,5},{5,4},{6,7},{7,6},{8,9},{9,8},{10,11... | collective-permute-start | bytes 344072 | tf_op jit(solution)/shard_map/ppermute | solution.py:186
  5.3 0.0 collective-permute-start.1
  5.3 0.0 copy-start.1
  5.3 1.7 %collective-permute-start.2 = (bf16[112,512]{1,0:T(8,128)(2,1)}, bf16[112,512]{1,0:T(8,128)(2,1)S(1)}, u32[]{:S(2)}, u32[]{:S(2)}) collective-permute-start(bf16[112,512]{1,0:T(8,128)(2,1)} %get-tuple-element.22), channel_id=1, source_target_pairs={{0,3},{1,2},{2,1},{3,0},{4,7},{5,6},{6,5},{7,4},{8,11},{9,10},{10,... | collective-permute-start | bytes 344072 | tf_op jit(solution)/shard_map/ppermute | solution.py:186
  7.0 0.0 collective-permute-done.in1
  7.0 3.2 %collective-permute-done.1.in2 = bf16[112,512]{1,0:T(8,128)(2,1)S(1)} collective-permute-done((bf16[112,512]{1,0:T(8,128)(2,1)}, bf16[112,512]{1,0:T(8,128)(2,1)S(1)}, u32[]{:S(2)}, u32[]{:S(2)}) %collective-permute-start.1) | collective-permute-done | bytes 114720 | tf_op jit(solution)/shard_map/ppermute | solution.py:186
  10.2 2.6 %collective-permute-done.2.in3 = bf16[112,512]{1,0:T(8,128)(2,1)S(1)} collective-permute-done((bf16[112,512]{1,0:T(8,128)(2,1)}, bf16[112,512]{1,0:T(8,128)(2,1)S(1)}, u32[]{:S(2)}, u32[]{:S(2)}) %collective-permute-start.2) | collective-permute-done | bytes 114720 | tf_op jit(solution)/shard_map/ppermute | solution.py:186
  12.8 0.0 copy-done.1
  12.8 0.0 copy-start
  12.8 0.9 %copy-done = bf16[112,512]{1,0:T(8,128)(2,1)S(1)} copy-done((bf16[112,512]{1,0:T(8,128)(2,1)S(1)}, bf16[112,512]{1,0:T(8,128)(2,1)}, u32[]{:S(2)}) %copy-start) | copy-done | bytes 114712
  13.7 0.8 factors.1
  14.5 31.5 %all_to_all.10.own = bf16[128,16,128]{2,1,0:T(8,128)(2,1)S(1)} all-to-all(bf16[128,16,128]{2,1,0:T(8,128)(2,1)S(1)} %get-tuple-element.24), channel_id=1, replica_groups=mesh['row'=64,'xl'=2,'core'=2] {'row','xl'}, dimensions={0} | all-to-all | bytes 1048576 | tf_op jit(solution)/shard_map/all_to_all | solution.py:232
  46.0 2.9 %collective-permute-start.3 = (bf16[128,8,128]{2,1,0:T(8,128)(2,1)S(1)}, bf16[128,8,128]{2,1,0:T(8,128)(2,1)S(1)}, u32[]{:S(2)}, u32[]{:S(2)}) collective-permute-start(bf16[128,8,128]{2,1,0:T(8,128)(2,1)S(1)} %slice.4), channel_id=1, source_target_pairs={{0,1},{1,0},{2,3},{3,2},{4,5},{5,4},{6,7},{7,6},{8,9},{9,8},{10,11... | collective-permute-start | bytes 786440 | tf_op jit(solution)/shard_map/ppermute | solution.py:186
  48.9 0.4 gates.1
  49.3 0.1 collective-permute-start.4
  49.4 1.3 %collective-permute-done.4.given = bf16[4,128,128]{2,1,0:T(8,128)(2,1)S(1)} collective-permute-done((bf16[4,128,128]{2,1,0:T(8,128)(2,1)S(1)}, bf16[4,128,128]{2,1,0:T(8,128)(2,1)S(1)}, u32[]{:S(2)}, u32[]{:S(2)}) %collective-permute-start.4) | collective-permute-done | bytes 131104 | tf_op jit(solution)/shard_map/ppermute | solution.py:186
  50.7 0.0 collective-permute-done.3.other
  50.7 1.0 %products.1 = bf16[128,16,128]{2,1,0:T(8,128)(2,1)S(1)} custom-call(bf16[128,16,128]{2,1,0:T(8,128)(2,1)S(1)} %all_to_all.10.own, bf16[128,8,128]{2,1,0:T(8,128)(2,1)S(1)} %collective-permute-done.3.other, bf16[4,128,128]{2,1,0:T(8,128)(2,1)S(1)} %get-tuple-element.27.kept, bf16[4,128,128]{2,1,0:T(8,128)(2,1)S(1)} %collective-permute-done.4.given), custom_call_target="tpu_custom_call" | custom-call | bytes 1048576 | tf_op jit(solution)/shard_map/products/pallas_call | solution.py:240
  51.8 24.2 %all_to_all.11.got = bf16[128,16,128]{2,1,0:T(8,128)(2,1)S(1)} all-to-all(bf16[128,16,128]{2,1,0:T(8,128)(2,1)S(1)} %products.1), channel_id=1, replica_groups=mesh['row'=64,'xl'=2,'core'=2] {'row','xl'}, dimensions={0} | all-to-all | bytes 1048576 | tf_op jit(solution)/shard_map/all_to_all | solution.py:251
  76.0 0.7 updates.1
  76.7 2.6 %collective-permute-start.5 = (bf16[2,32,512]{2,1,0:T(8,128)(2,1)S(1)}, bf16[2,32,512]{2,1,0:T(8,128)(2,1)S(1)}, u32[]{:S(2)}, u32[]{:S(2)}) collective-permute-start(bf16[2,32,512]{2,1,0:T(8,128)(2,1)S(1)} %get-tuple-element.30), channel_id=1, source_target_pairs={{0,1},{1,0},{2,3},{3,2},{4,5},{5,4},{6,7},{7,6},{8,9},{9,8},{10,11... | collective-permute-start | bytes 196616 | tf_op jit(solution)/shard_map/ppermute | solution.py:186
  79.3 0.6 collective-permute-start.6
  79.9 1.1 %collective-permute-start.7 = (bf16[2,32,512]{2,1,0:T(8,128)(2,1)S(1)}, bf16[2,32,512]{2,1,0:T(8,128)(2,1)S(1)}, u32[]{:S(2)}, u32[]{:S(2)}) collective-permute-start(bf16[2,32,512]{2,1,0:T(8,128)(2,1)S(1)} %get-tuple-element.32), channel_id=1, source_target_pairs={{0,3},{1,2},{2,1},{3,0},{4,7},{5,6},{6,5},{7,4},{8,11},{9,10},{10,... | collective-permute-start | bytes 196616 | tf_op jit(solution)/shard_map/ppermute | solution.py:186
  81.0 0.0 collective-permute-done.5.in1
  81.0 1.9 %collective-permute-done.6.in2 = bf16[2,32,512]{2,1,0:T(8,128)(2,1)S(1)} collective-permute-done((bf16[2,32,512]{2,1,0:T(8,128)(2,1)S(1)}, bf16[2,32,512]{2,1,0:T(8,128)(2,1)S(1)}, u32[]{:S(2)}, u32[]{:S(2)}) %collective-permute-start.6) | collective-permute-done | bytes 65568 | tf_op jit(solution)/shard_map/ppermute | solution.py:186
  83.0 1.6 %collective-permute-done.7.in3 = bf16[2,32,512]{2,1,0:T(8,128)(2,1)S(1)} collective-permute-done((bf16[2,32,512]{2,1,0:T(8,128)(2,1)S(1)}, bf16[2,32,512]{2,1,0:T(8,128)(2,1)S(1)}, u32[]{:S(2)}, u32[]{:S(2)}) %collective-permute-start.7) | collective-permute-done | bytes 65568 | tf_op jit(solution)/shard_map/ppermute | solution.py:186
  84.5 0.8 arrange.1
  (1 shorter events, 0.0 us)
Async XLA Ops:
  1.9 5.1 %collective-permute-start = (bf16[112,512]{1,0:T(8,128)(2,1)}, bf16[112,512]{1,0:T(8,128)(2,1)S(1)}, u32[]{:S(2)}, u32[]{:S(2)}) collective-permute-start(bf16[112,512]{1,0:T(8,128)(2,1)} %get-tuple-element.20), channel_id=1, source_target_pairs={{0,1},{1,0},{2,3},{3,2},{4,5},{5,4},{6,7},{7,6},{8,9},{9,8},{10,11... | collective-permute-start | bytes 344072 | tf_op jit(solution)/shard_map/ppermute | solution.py:186
  5.3 4.9 %collective-permute-start.1 = (bf16[112,512]{1,0:T(8,128)(2,1)}, bf16[112,512]{1,0:T(8,128)(2,1)S(1)}, u32[]{:S(2)}, u32[]{:S(2)}) collective-permute-start(bf16[112,512]{1,0:T(8,128)(2,1)} %get-tuple-element.21), channel_id=1, source_target_pairs={{0,2},{1,3},{2,0},{3,1},{4,6},{5,7},{6,4},{7,5},{8,10},{9,11},{10,... | collective-permute-start | bytes 344072 | tf_op jit(solution)/shard_map/ppermute | solution.py:186
  5.3 7.6 %copy-start.1 = (f32[4,128]{1,0:T(4,128)S(1)}, f32[4,128]{1,0:T(4,128)}, u32[]{:S(2)}) copy-start(f32[4,128]{1,0:T(4,128)} %get-tuple-element.23.vectors) | copy-start | bytes 6148
  5.3 7.6 %collective-permute-start.2 = (bf16[112,512]{1,0:T(8,128)(2,1)}, bf16[112,512]{1,0:T(8,128)(2,1)S(1)}, u32[]{:S(2)}, u32[]{:S(2)}) collective-permute-start(bf16[112,512]{1,0:T(8,128)(2,1)} %get-tuple-element.22), channel_id=1, source_target_pairs={{0,3},{1,2},{2,1},{3,0},{4,7},{5,6},{6,5},{7,4},{8,11},{9,10},{10,... | collective-permute-start | bytes 344072 | tf_op jit(solution)/shard_map/ppermute | solution.py:186
  12.8 0.9 %copy-start = (bf16[112,512]{1,0:T(8,128)(2,1)S(1)}, bf16[112,512]{1,0:T(8,128)(2,1)}, u32[]{:S(2)}) copy-start(bf16[112,512]{1,0:T(8,128)(2,1)} %get-tuple-element.19.in0) | copy-start | bytes 344068
  46.0 4.7 %collective-permute-start.3 = (bf16[128,8,128]{2,1,0:T(8,128)(2,1)S(1)}, bf16[128,8,128]{2,1,0:T(8,128)(2,1)S(1)}, u32[]{:S(2)}, u32[]{:S(2)}) collective-permute-start(bf16[128,8,128]{2,1,0:T(8,128)(2,1)S(1)} %slice.4), channel_id=1, source_target_pairs={{0,1},{1,0},{2,3},{3,2},{4,5},{5,4},{6,7},{7,6},{8,9},{9,8},{10,11... | collective-permute-start | bytes 786440 | tf_op jit(solution)/shard_map/ppermute | solution.py:186
  49.3 1.4 %collective-permute-start.4 = (bf16[4,128,128]{2,1,0:T(8,128)(2,1)S(1)}, bf16[4,128,128]{2,1,0:T(8,128)(2,1)S(1)}, u32[]{:S(2)}, u32[]{:S(2)}) collective-permute-start(bf16[4,128,128]{2,1,0:T(8,128)(2,1)S(1)} %get-tuple-element.28), channel_id=1, source_target_pairs={{0,1},{1,0},{2,3},{3,2},{4,5},{5,4},{6,7},{7,6},{8,9},{9,8},{10,11... | collective-permute-start | bytes 393224 | tf_op jit(solution)/shard_map/ppermute | solution.py:186
  76.7 4.4 %collective-permute-start.5 = (bf16[2,32,512]{2,1,0:T(8,128)(2,1)S(1)}, bf16[2,32,512]{2,1,0:T(8,128)(2,1)S(1)}, u32[]{:S(2)}, u32[]{:S(2)}) collective-permute-start(bf16[2,32,512]{2,1,0:T(8,128)(2,1)S(1)} %get-tuple-element.30), channel_id=1, source_target_pairs={{0,1},{1,0},{2,3},{3,2},{4,5},{5,4},{6,7},{7,6},{8,9},{9,8},{10,11... | collective-permute-start | bytes 196616 | tf_op jit(solution)/shard_map/ppermute | solution.py:186
  79.3 3.7 %collective-permute-start.6 = (bf16[2,32,512]{2,1,0:T(8,128)(2,1)S(1)}, bf16[2,32,512]{2,1,0:T(8,128)(2,1)S(1)}, u32[]{:S(2)}, u32[]{:S(2)}) collective-permute-start(bf16[2,32,512]{2,1,0:T(8,128)(2,1)S(1)} %get-tuple-element.31), channel_id=1, source_target_pairs={{0,2},{1,3},{2,0},{3,1},{4,6},{5,7},{6,4},{7,5},{8,10},{9,11},{10,... | collective-permute-start | bytes 196616 | tf_op jit(solution)/shard_map/ppermute | solution.py:186
  79.9 4.6 %collective-permute-start.7 = (bf16[2,32,512]{2,1,0:T(8,128)(2,1)S(1)}, bf16[2,32,512]{2,1,0:T(8,128)(2,1)S(1)}, u32[]{:S(2)}, u32[]{:S(2)}) collective-permute-start(bf16[2,32,512]{2,1,0:T(8,128)(2,1)S(1)} %get-tuple-element.32), channel_id=1, source_target_pairs={{0,3},{1,2},{2,1},{3,0},{4,7},{5,6},{6,5},{7,4},{8,11},{9,10},{10,... | collective-permute-start | bytes 196616 | tf_op jit(solution)/shard_map/ppermute | solution.py:186

commit v6 on v5

--- a/solution.py
+++ b/solution.py
@@ -41,13 +41,20 @@
     return jnp.broadcast_to(row, (128, 128)).T
 
 
+def residue_order():
+    taken = lax.broadcasted_iota(jnp.int32, (128, 128), 0)
+    given = lax.broadcasted_iota(jnp.int32, (128, 128), 1)
+    matches = taken == given % 64 // 8 * 16 + given // 64 * 8 + given % 8
+    return matches.astype(f32).astype(bf16)
+
+
 def position():
     return 2 * lax.axis_index("xl") + lax.axis_index("core")
 
 
 def lay_out(*refs):
-    sources, outs, vectors = refs[:11], refs[11:15], refs[15]
-    field, weights, rows, semaphores = refs[16:]
+    sources, outs, shared, vectors = refs[:11], refs[11:15], refs[15], refs[16]
+    field, weights, rows, semaphores = refs[17:]
     copies = [
         pltpu.make_async_copy(source, target, semaphores.at[at])
         for at, (source, target) in enumerate(
@@ -73,19 +80,25 @@
                 out[32 * ii : 32 * (ii + 1), at] = rows[
                     lane, pl.ds(2 * (mine ^ step) + ii, 32, stride=8), :
                 ].astype(bf16)
-            out[64:96, at] = weights[lane]
-            out[96:112, at] = weights[4 + lane % 2, 16 * (lane // 2) : 16 * (lane // 2 + 1), :]
-
-
-def factors(in0, in1, in2, in3, vectors, out, normed_out, late, field, weights, rows):
+    for out, first in ((outs[0], 64), (outs[1], 64), (shared, 0)):
+        for lane in range(4):
+            at = slice(128 * lane, 128 * (lane + 1))
+            out[first : first + 32, at] = weights[lane]
+            out[first + 32 : first + 48, at] = weights[
+                4 + lane % 2, 16 * (lane // 2) : 16 * (lane // 2 + 1), :
+            ]
+
+
+def factors(in0, in1, in2, in3, shared2, shared3, vectors, out, normed_out, late, field, weights, rows):
     mine = position()
     for step, block in enumerate((in0, in1, in2, in3)):
         first = pl.multiple_of((mine ^ step) * 32, 32)
         for ii in range(2):
             field[ii, pl.ds(first, 32), :] = block[32 * ii : 32 * (ii + 1), :].astype(f32)
-        weights[pl.ds(first, 32), :] = block[64:96, :]
-        late[pl.ds(first, 16), :] = block[96:112, 0:256]
-        late[pl.ds(pl.multiple_of(first + 16, 16), 16), :] = block[96:112, 256:512]
+        block = (in0.at[64:112], in1.at[64:112], shared2, shared3)[step]
+        weights[pl.ds(first, 32), :] = block[0:32, :]
+        late[pl.ds(first, 16), :] = block[32:48, 0:256]
+        late[pl.ds(pl.multiple_of(first + 16, 16), 16), :] = block[32:48, 256:512]
     gains, biases = column(vectors[0:1]), column(vectors[1:2])
     for ii in range(2):
         normed = layer_norm(field[ii], gains, biases).astype(bf16)
@@ -107,11 +120,16 @@
 
 def gates(normed, late, kept, given, rows):
     core = lax.axis_index("core")
+    order = residue_order()
     for ii in range(2):
         value = jax.nn.sigmoid(
             jnp.dot(late[:, 0:128], normed[ii], preferred_element_type=f32)
-        )
-        rows[...] = value.T
+        ).astype(bf16)
+        for lane in range(4):
+            at = slice(128 * lane, 128 * (lane + 1))
+            rows[at] = lax.dot_general(
+                order, value[:, at], (((1,), (1,)), ((), ())), preferred_element_type=f32
+            )
         for jj in range(2):
             kept[2 * ii + jj] = rows[pl.ds(2 * core + jj, 128, stride=4), :].astype(bf16)
             given[2 * ii + jj] = rows[pl.ds(2 * (1 - core) + jj, 128, stride=4), :].astype(bf16)
@@ -172,6 +190,7 @@
 
 def arrange(in0, in1, in2, in3, out, rows):
     mine = position()
+    order = residue_order()
     for lane in range(4):
         at = slice(128 * lane, 128 * (lane + 1))
         for step, block in enumerate((in0, in1, in2, in3)):
@@ -179,11 +198,17 @@
                 rows[lane, pl.ds(2 * (mine ^ step) + jj, 32, stride=8), :] = block[
                     jj, :, at
                 ].astype(f32)
-        out[:, :, at] = rows[lane].reshape(32, 8, 128).astype(bf16)
+        placed = jnp.dot(rows[lane].astype(bf16), order, preferred_element_type=f32)
+        out[:, :, at] = placed.reshape(32, 8, 128).astype(bf16)
 
 
 def swap(array, step):
     return lax.ppermute(array, ("xl", "core"), [(s, s ^ step) for s in range(4)])
+
+
+def around(array, step):
+    pairs = [(s, s ^ (4 + step)) for s in range(8)]
+    return lax.ppermute(array, ("xh", "xl", "core"), pairs)
 
 
 def exchange(parts):
@@ -203,13 +228,14 @@
     output_bias,
     final_weight,
 ):
-    same_core = ("row", "xl")
+    same_core = ("y", "z", "xh", "xl")
     weights = (left_weight, left_gate, right_weight, right_gate, gate_weight, final_weight)
     vectors = (input_gain, input_bias, output_gain, output_bias)
-    *parts, vectors = call(
+    *parts, shared, vectors = call(
         lay_out,
         "lay_out",
-        (shape(112, 512),) * 4 + (jax.ShapeDtypeStruct((4, 128), f32),),
+        tuple(pltpu.VMEM((high, 512), bf16) for high in (112, 112, 64, 64, 48))
+        + (pltpu.VMEM((4, 128), f32),),
         [
             pltpu.VMEM((32, 8, 512), bf16),
             pltpu.VMEM((6, 32, 128), bf16),
@@ -228,7 +254,7 @@
             pltpu.VMEM((128, 512), bf16),
             pltpu.VMEM((2048, 128), f32),
         ],
-    )(*exchange(parts), vectors)
+    )(*exchange(parts), around(shared, 2), around(shared, 3), vectors)
     own = lax.all_to_all(sent, same_core, 0, 0, tiled=True)
     kept, given = call(
         gates,
@@ -265,10 +291,10 @@
 
 
 def solution(mesh):
-    mesh = Mesh(mesh.devices.reshape(64, 2, 2), ("row", "xl", "core"))
-    ch = ("xl", "core")
+    mesh = Mesh(mesh.devices.reshape(4, 2, 8, 2, 2), ("y", "xh", "z", "xl", "core"))
+    row, ch = ("y", "xh", "z"), ("xl", "core")
     placed = (
-        P(ch, "row", None),
+        P(ch, row, None),
         P(),
         P(),
         P(None, ch),
@@ -281,5 +307,5 @@
         P(None, ch),
     )
     return jax.shard_map(
-        body, mesh=mesh, in_specs=placed, out_specs=P(ch, "row", None), check_vma=False
-    )
+        body, mesh=mesh, in_specs=placed, out_specs=P(ch, row, None), check_vma=False
+    )

time: 85.6 us -> 83 us (0.970)
  starting transfers between devices: 12.4 us -> 15.4 us
  waiting for transfers between devices: 10.7 us -> 7.73 us
  blocking collectives: 55.7 us -> 54.3 us
  local copies, waits for them, and re-layouts: 0.92 us -> 0.02 us
    ppermute x8, waiting for transfers between devices: 10.7 us -> 4.85 us  [swap(): lax.ppermute(array, ('xl', 'core'), [(s, s ^ step) for s in range(4)])]
    ppermute x0 -> x2, waiting for transfers between devices: none -> 2.88 us  [around(): return lax.ppermute(array, ('xh', 'xl', 'core'), pairs)]
    ppermute x0 -> x2, starting transfers between devices: none -> 2.72 us  [around(): return lax.ppermute(array, ('xh', 'xl', 'core'), pairs)]
    all_to_all x1, blocking collectives: 31.5 us -> 30.1 us  [body(): own = lax.all_to_all(sent, same_core, 0, 0, tiled=True)]
    unnamed x4 -> x0, local copies, waits for them, and re-layouts: 0.9 us -> none
  transfers between devices with their start and end apart: 8 -> 10, of which waited for: 5 -> 5; matrix products, arithmetic and copies ran while one was open for 0% -> 0% of each run, Pallas kernels for 0% -> 1%
where the time goes in v6:
time: 83 us; the launch traced here: 82.8 us
  blocking collectives  54.3 us (65%)
  starting transfers between devices  15.4 us (19%)
  waiting for transfers between devices  7.73 us (9%)
  Pallas kernels  5.34 us (6%)
    all_to_all x1, blocking collectives, body(): own = lax.all_to_all(sent, same_core, 0, 0, tiled=True)  30.1 us
    all_to_all x1, blocking collectives, body(): got = lax.all_to_all(sent, same_core, 0, 0, tiled=True)  24.2 us
    ppermute x8, starting transfers between devices, swap(): lax.ppermute(array, ('xl', 'core'), [(s, s ^ step) for s in range(4)])  12.7 us
    ppermute x8, waiting for transfers between devices, swap(): lax.ppermute(array, ('xl', 'core'), [(s, s ^ step) for s in range(4)])  4.85 us
    ppermute x2, waiting for transfers between devices, around(): return lax.ppermute(array, ('xh', 'xl', 'core'), pairs)  2.88 us
    ppermute x2, starting transfers between devices, around(): return lax.ppermute(array, ('xh', 'xl', 'core'), pairs)  2.72 us
  transfers between devices with their start and end apart: 10, of which 5 were waited for; matrix products, arithmetic and copies ran while one was open for 0% of the time, Pallas kernels for 1%

profile of v6, /device:TPU:1, one launch (start us, length us, event | category | flops | bytes accessed | tf_op | source)
XLA Modules:
  0.0 82.8 jit_solution(369453117992405154)
XLA Ops:
  0.0 1.2 %lay_out.1 = (bf16[112,512]{1,0:T(8,128)(2,1)S(1)}, bf16[112,512]{1,0:T(8,128)(2,1)S(1)}, bf16[64,512]{1,0:T(8,128)(2,1)S(1)}, bf16[64,512]{1,0:T(8,128)(2,1)S(1...) custom-call(bf16[32,8,512]{2,1,0:T(8,128)(2,1)} %refs_0_.1, bf16[32,128]{1,0:T(8,128)(2,1)} %bitcast.10, ...), custom_call_target="tpu_custom_call" | custom-call | bytes 1048576 | tf_op jit(solution)/shard_map/lay_out/pallas_call | solution.py:234
  1.2 3.3 %collective-permute-start = (bf16[112,512]{1,0:T(8,128)(2,1)S(1)}, bf16[112,512]{1,0:T(8,128)(2,1)S(1)}, u32[]{:S(2)}, u32[]{:S(2)}) collective-permute-start(bf16[112,512]{1,0:T(8,128)(2,1)S(1)} %get-tuple-element.21), channel_id=1, source_target_pairs={{0,1},{1,0},{2,3},{3,2},{4,5},{5,4},{6,7},{7,6},{8,9},{9,8},{10,11... | collective-permute-start | bytes 344072 | tf_op jit(solution)/shard_map/ppermute | solution.py:206
  4.6 0.0 collective-permute-start.1
  4.6 1.7 %collective-permute-start.2 = (bf16[64,512]{1,0:T(8,128)(2,1)S(1)}, bf16[64,512]{1,0:T(8,128)(2,1)S(1)}, u32[]{:S(2)}, u32[]{:S(2)}) collective-permute-start(bf16[64,512]{1,0:T(8,128)(2,1)S(1)} %get-tuple-element.23), channel_id=1, source_target_pairs={{0,3},{1,2},{2,1},{3,0},{4,7},{5,6},{6,5},{7,4},{8,11},{9,10},{10,... | collective-permute-start | bytes 196616 | tf_op jit(solution)/shard_map/ppermute | solution.py:206
  6.3 0.8 collective-permute-start.4
  7.1 1.9 %collective-permute-start.3 = (bf16[48,512]{1,0:T(8,128)(2,1)S(1)}, bf16[48,512]{1,0:T(8,128)(2,1)S(1)}, u32[]{:S(2)}, u32[]{:S(2)}) collective-permute-start(bf16[48,512]{1,0:T(8,128)(2,1)S(1)} %get-tuple-element.24), channel_id=1, source_target_pairs={{0,34},{1,35},{2,32},{3,33},{32,2},{33,3},{34,0},{35,1},{4,38},{5,... | collective-permute-start | bytes 147464 | tf_op jit(solution)/shard_map/ppermute | solution.py:211
  9.0 2.3 %collective-permute-done.4.shared3 = bf16[48,512]{1,0:T(8,128)(2,1)S(1)} collective-permute-done((bf16[48,512]{1,0:T(8,128)(2,1)S(1)}, bf16[48,512]{1,0:T(8,128)(2,1)S(1)}, u32[]{:S(2)}, u32[]{:S(2)}) %collective-permute-start.4) | collective-permute-done | bytes 49184 | tf_op jit(solution)/shard_map/ppermute | solution.py:211
  11.3 0.6 collective-permute-done.3.shared2
  11.9 0.0 collective-permute-done.1.in2
  11.9 0.0 collective-permute-done.2.in3
  11.9 0.0 collective-permute-done.in1
  11.9 0.8 factors.1
  12.7 30.1 %all_to_all.10.own = bf16[128,16,128]{2,1,0:T(8,128)(2,1)S(1)} all-to-all(bf16[128,16,128]{2,1,0:T(8,128)(2,1)S(1)} %get-tuple-element.26), channel_id=1, replica_groups=mesh['y'=4,'xh'=2,'z'=8,'xl'=2,'core'=2] {'y','z','xh','xl'}, dimensions={0} | all-to-all | bytes 1048576 | tf_op jit(solution)/shard_map/all_to_all | solution.py:258
  42.8 3.5 %collective-permute-start.5 = (bf16[128,8,128]{2,1,0:T(8,128)(2,1)S(1)}, bf16[128,8,128]{2,1,0:T(8,128)(2,1)S(1)}, u32[]{:S(2)}, u32[]{:S(2)}) collective-permute-start(bf16[128,8,128]{2,1,0:T(8,128)(2,1)S(1)} %slice.4), channel_id=1, source_target_pairs={{0,1},{1,0},{2,3},{3,2},{4,5},{5,4},{6,7},{7,6},{8,9},{9,8},{10,11... | collective-permute-start | bytes 786440 | tf_op jit(solution)/shard_map/ppermute | solution.py:206
  46.4 0.6 gates.1
  47.0 0.1 collective-permute-start.6
  47.1 1.3 %collective-permute-done.6.given = bf16[4,128,128]{2,1,0:T(8,128)(2,1)S(1)} collective-permute-done((bf16[4,128,128]{2,1,0:T(8,128)(2,1)S(1)}, bf16[4,128,128]{2,1,0:T(8,128)(2,1)S(1)}, u32[]{:S(2)}, u32[]{:S(2)}) %collective-permute-start.6) | collective-permute-done | bytes 131104 | tf_op jit(solution)/shard_map/ppermute | solution.py:206
  48.4 0.0 collective-permute-done.5.other
  48.4 1.0 %products.1 = bf16[128,16,128]{2,1,0:T(8,128)(2,1)S(1)} custom-call(bf16[128,16,128]{2,1,0:T(8,128)(2,1)S(1)} %all_to_all.10.own, bf16[128,8,128]{2,1,0:T(8,128)(2,1)S(1)} %collective-permute-done.5.other, bf16[4,128,128]{2,1,0:T(8,128)(2,1)S(1)} %get-tuple-element.29.kept, bf16[4,128,128]{2,1,0:T(8,128)(2,1)S(1)} %collective-permute-done.6.given), custom_call_target="tpu_custom_call" | custom-call | bytes 1048576 | tf_op jit(solution)/shard_map/products/pallas_call | solution.py:266
  49.4 24.2 %all_to_all.11.got = bf16[128,16,128]{2,1,0:T(8,128)(2,1)S(1)} all-to-all(bf16[128,16,128]{2,1,0:T(8,128)(2,1)S(1)} %products.1), channel_id=1, replica_groups=mesh['y'=4,'xh'=2,'z'=8,'xl'=2,'core'=2] {'y','z','xh','xl'}, dimensions={0} | all-to-all | bytes 1048576 | tf_op jit(solution)/shard_map/all_to_all | solution.py:277
  73.6 0.7 updates.1
  74.3 2.2 %collective-permute-start.7 = (bf16[2,32,512]{2,1,0:T(8,128)(2,1)S(1)}, bf16[2,32,512]{2,1,0:T(8,128)(2,1)S(1)}, u32[]{:S(2)}, u32[]{:S(2)}) collective-permute-start(bf16[2,32,512]{2,1,0:T(8,128)(2,1)S(1)} %get-tuple-element.32), channel_id=1, source_target_pairs={{0,1},{1,0},{2,3},{3,2},{4,5},{5,4},{6,7},{7,6},{8,9},{9,8},{10,11... | collective-permute-start | bytes 196616 | tf_op jit(solution)/shard_map/ppermute | solution.py:206
  76.5 0.7 collective-permute-start.8
  77.2 1.0 %collective-permute-start.9 = (bf16[2,32,512]{2,1,0:T(8,128)(2,1)S(1)}, bf16[2,32,512]{2,1,0:T(8,128)(2,1)S(1)}, u32[]{:S(2)}, u32[]{:S(2)}) collective-permute-start(bf16[2,32,512]{2,1,0:T(8,128)(2,1)S(1)} %get-tuple-element.34), channel_id=1, source_target_pairs={{0,3},{1,2},{2,1},{3,0},{4,7},{5,6},{6,5},{7,4},{8,11},{9,10},{10,... | collective-permute-start | bytes 196616 | tf_op jit(solution)/shard_map/ppermute | solution.py:206
  78.3 0.0 collective-permute-done.7.in1
  78.3 1.9 %collective-permute-done.8.in2 = bf16[2,32,512]{2,1,0:T(8,128)(2,1)S(1)} collective-permute-done((bf16[2,32,512]{2,1,0:T(8,128)(2,1)S(1)}, bf16[2,32,512]{2,1,0:T(8,128)(2,1)S(1)}, u32[]{:S(2)}, u32[]{:S(2)}) %collective-permute-start.8) | collective-permute-done | bytes 65568 | tf_op jit(solution)/shard_map/ppermute | solution.py:206
  80.2 1.6 %collective-permute-done.9.in3 = bf16[2,32,512]{2,1,0:T(8,128)(2,1)S(1)} collective-permute-done((bf16[2,32,512]{2,1,0:T(8,128)(2,1)S(1)}, bf16[2,32,512]{2,1,0:T(8,128)(2,1)S(1)}, u32[]{:S(2)}, u32[]{:S(2)}) %collective-permute-start.9) | collective-permute-done | bytes 65568 | tf_op jit(solution)/shard_map/ppermute | solution.py:206
  81.8 1.0 %arrange.1 = bf16[32,8,512]{2,1,0:T(8,128)(2,1)} custom-call(bf16[2,32,512]{2,1,0:T(8,128)(2,1)S(1)} %get-tuple-element.31.in0, bf16[2,32,512]{2,1,0:T(8,128)(2,1)S(1)} %collective-permute-done.7.in1, bf16[2,32,512]{2,1,0:T(8,128)(2,1)S(1)} %collective-permute-done.8.in2, bf16[2,32,512]{2,1,0:T(8,128)(2,1)S(1)} %collective-permute-done.9.in3), custom_call_target="tpu_custom_call" | custom-call | bytes 1048576 | tf_op jit(solution)/shard_map/arrange/pallas_call | solution.py:288
  (1 shorter events, 0.0 us)
Async XLA Ops:
  1.2 10.7 %collective-permute-start = (bf16[112,512]{1,0:T(8,128)(2,1)S(1)}, bf16[112,512]{1,0:T(8,128)(2,1)S(1)}, u32[]{:S(2)}, u32[]{:S(2)}) collective-permute-start(bf16[112,512]{1,0:T(8,128)(2,1)S(1)} %get-tuple-element.21), channel_id=1, source_target_pairs={{0,1},{1,0},{2,3},{3,2},{4,5},{5,4},{6,7},{7,6},{8,9},{9,8},{10,11... | collective-permute-start | bytes 344072 | tf_op jit(solution)/shard_map/ppermute | solution.py:206
  4.6 7.3 %collective-permute-start.1 = (bf16[64,512]{1,0:T(8,128)(2,1)S(1)}, bf16[64,512]{1,0:T(8,128)(2,1)S(1)}, u32[]{:S(2)}, u32[]{:S(2)}) collective-permute-start(bf16[64,512]{1,0:T(8,128)(2,1)S(1)} %get-tuple-element.22), channel_id=1, source_target_pairs={{0,2},{1,3},{2,0},{3,1},{4,6},{5,7},{6,4},{7,5},{8,10},{9,11},{10,... | collective-permute-start | bytes 196616 | tf_op jit(solution)/shard_map/ppermute | solution.py:206
  4.6 7.3 %collective-permute-start.2 = (bf16[64,512]{1,0:T(8,128)(2,1)S(1)}, bf16[64,512]{1,0:T(8,128)(2,1)S(1)}, u32[]{:S(2)}, u32[]{:S(2)}) collective-permute-start(bf16[64,512]{1,0:T(8,128)(2,1)S(1)} %get-tuple-element.23), channel_id=1, source_target_pairs={{0,3},{1,2},{2,1},{3,0},{4,7},{5,6},{6,5},{7,4},{8,11},{9,10},{10,... | collective-permute-start | bytes 196616 | tf_op jit(solution)/shard_map/ppermute | solution.py:206
  6.3 5.0 %collective-permute-start.4 = (bf16[48,512]{1,0:T(8,128)(2,1)S(1)}, bf16[48,512]{1,0:T(8,128)(2,1)S(1)}, u32[]{:S(2)}, u32[]{:S(2)}) collective-permute-start(bf16[48,512]{1,0:T(8,128)(2,1)S(1)} %get-tuple-element.24), channel_id=1, source_target_pairs={{0,35},{1,34},{2,33},{3,32},{32,3},{33,2},{34,1},{35,0},{4,39},{5,... | collective-permute-start | bytes 147464 | tf_op jit(solution)/shard_map/ppermute | solution.py:211
  7.1 4.8 %collective-permute-start.3 = (bf16[48,512]{1,0:T(8,128)(2,1)S(1)}, bf16[48,512]{1,0:T(8,128)(2,1)S(1)}, u32[]{:S(2)}, u32[]{:S(2)}) collective-permute-start(bf16[48,512]{1,0:T(8,128)(2,1)S(1)} %get-tuple-element.24), channel_id=1, source_target_pairs={{0,34},{1,35},{2,32},{3,33},{32,2},{33,3},{34,0},{35,1},{4,38},{5,... | collective-permute-start | bytes 147464 | tf_op jit(solution)/shard_map/ppermute | solution.py:211
  42.8 5.6 %collective-permute-start.5 = (bf16[128,8,128]{2,1,0:T(8,128)(2,1)S(1)}, bf16[128,8,128]{2,1,0:T(8,128)(2,1)S(1)}, u32[]{:S(2)}, u32[]{:S(2)}) collective-permute-start(bf16[128,8,128]{2,1,0:T(8,128)(2,1)S(1)} %slice.4), channel_id=1, source_target_pairs={{0,1},{1,0},{2,3},{3,2},{4,5},{5,4},{6,7},{7,6},{8,9},{9,8},{10,11... | collective-permute-start | bytes 786440 | tf_op jit(solution)/shard_map/ppermute | solution.py:206
  47.0 1.4 %collective-permute-start.6 = (bf16[4,128,128]{2,1,0:T(8,128)(2,1)S(1)}, bf16[4,128,128]{2,1,0:T(8,128)(2,1)S(1)}, u32[]{:S(2)}, u32[]{:S(2)}) collective-permute-start(bf16[4,128,128]{2,1,0:T(8,128)(2,1)S(1)} %get-tuple-element.30), channel_id=1, source_target_pairs={{0,1},{1,0},{2,3},{3,2},{4,5},{5,4},{6,7},{7,6},{8,9},{9,8},{10,11... | collective-permute-start | bytes 393224 | tf_op jit(solution)/shard_map/ppermute | solution.py:206
  74.3 4.0 %collective-permute-start.7 = (bf16[2,32,512]{2,1,0:T(8,128)(2,1)S(1)}, bf16[2,32,512]{2,1,0:T(8,128)(2,1)S(1)}, u32[]{:S(2)}, u32[]{:S(2)}) collective-permute-start(bf16[2,32,512]{2,1,0:T(8,128)(2,1)S(1)} %get-tuple-element.32), channel_id=1, source_target_pairs={{0,1},{1,0},{2,3},{3,2},{4,5},{5,4},{6,7},{7,6},{8,9},{9,8},{10,11... | collective-permute-start | bytes 196616 | tf_op jit(solution)/shard_map/ppermute | solution.py:206
  76.5 3.7 %collective-permute-start.8 = (bf16[2,32,512]{2,1,0:T(8,128)(2,1)S(1)}, bf16[2,32,512]{2,1,0:T(8,128)(2,1)S(1)}, u32[]{:S(2)}, u32[]{:S(2)}) collective-permute-start(bf16[2,32,512]{2,1,0:T(8,128)(2,1)S(1)} %get-tuple-element.33), channel_id=1, source_target_pairs={{0,2},{1,3},{2,0},{3,1},{4,6},{5,7},{6,4},{7,5},{8,10},{9,11},{10,... | collective-permute-start | bytes 196616 | tf_op jit(solution)/shard_map/ppermute | solution.py:206
  77.2 4.6 %collective-permute-start.9 = (bf16[2,32,512]{2,1,0:T(8,128)(2,1)S(1)}, bf16[2,32,512]{2,1,0:T(8,128)(2,1)S(1)}, u32[]{:S(2)}, u32[]{:S(2)}) collective-permute-start(bf16[2,32,512]{2,1,0:T(8,128)(2,1)S(1)} %get-tuple-element.34), channel_id=1, source_target_pairs={{0,3},{1,2},{2,1},{3,0},{4,7},{5,6},{6,5},{7,4},{8,11},{9,10},{10,... | collective-permute-start | bytes 196616 | tf_op jit(solution)/shard_map/ppermute | solution.py:206

commit v7 on v0

v7 whole, which is shorter than its diff:
```python
import jax
import jax.numpy as jnp
from jax import lax
from jax.experimental import pallas as pl
from jax.experimental.pallas import tpu as pltpu
from jax.sharding import Mesh
from jax.sharding import PartitionSpec as P

epsilon = 1e-05
bf16, f32 = jnp.bfloat16, jnp.float32
vmem_bytes = 16 * 1024 * 1024


def call(kernel, name, outs, scratch, flops=0, work=1 << 20, limit=vmem_bytes, **more):
    return pl.pallas_call(
        kernel,
        name=name,
        out_shape=outs,
        scratch_shapes=scratch,
        cost_estimate=pl.CostEstimate(flops=flops, bytes_accessed=work, transcendentals=0),
        compiler_params=pltpu.CompilerParams(vmem_limit_bytes=limit),
        **more,
    )


def shape(*dims):
    return jax.ShapeDtypeStruct(dims, bf16)


def layer_norm(values, gain, bias):
    average = jnp.mean(values, axis=0, keepdims=True)
    centred = values - average
    variance = jnp.mean(centred * centred, axis=0, keepdims=True)
    wide = values.shape[1] // 128
    return centred * lax.rsqrt(variance + epsilon) * jnp.tile(gain, (1, wide)) + jnp.tile(
        bias, (1, wide)
    )


def column(row):
    return jnp.broadcast_to(row, (128, 128)).T


def residue_order():
    taken = lax.broadcasted_iota(jnp.int32, (128, 128), 0)
    given = lax.broadcasted_iota(jnp.int32, (128, 128), 1)
    matches = taken == given % 64 // 8 * 16 + given // 64 * 8 + given % 8
    return matches.astype(f32).astype(bf16)


def position():
    return 2 * lax.axis_index("xl") + lax.axis_index("core")


def residue(i):
    return slice(32 * i + 48 * (i // 4), 32 * (i + 1) + 48 * (i // 4))


def lay_out(*refs):
    sources, (whole, vectors) = refs[:11], refs[11:13]
    field, weights, rows, semaphores = refs[13:]
    copies = [
        pltpu.make_async_copy(source, target, semaphores.at[at])
        for at, (source, target) in enumerate(
            zip(
                sources,
                [field]
                + [weights.at[w] for w in range(6)]
                + [vectors.at[pl.ds(v, 1)] for v in range(4)],
            )
        )
    ]
    for copy in copies:
        copy.start()
    for copy in copies:
        copy.wait()
    for lane in range(4):
        at = slice(128 * lane, 128 * (lane + 1))
        rows[lane] = field[:, :, at].astype(f32).reshape(256, 128)
        for i in range(8):
            whole[residue(i), at] = rows[lane, pl.ds(i, 32, stride=8), :].astype(bf16)
        whole[128:160, at] = weights[lane]
        whole[160:176, at] = weights[4 + lane % 2, 16 * (lane // 2) : 16 * (lane // 2 + 1), :]


def scatter_field(own, mate, out, field, columns, rows):
    order = residue_order()
    for i in range(8):
        field[64 * i : 64 * i + 32, :] = mate[residue(i), :]
        field[64 * i + 32 : 64 * (i + 1), :] = own[residue(i), :]
    for group in range(4):
        for block in range(4):
            at = slice(128 * block, 128 * (block + 1))
            columns[at] = lax.dot_general(
                order,
                field[128 * group : 128 * (group + 1), at],
                (((1,), (1,)), ((), ())),
                preferred_element_type=f32,
            )
        for jj in range(4):
            rows[pl.ds(4 * jj + group, 128, stride=16), :] = columns[pl.ds(jj, 128, stride=4), :]
    out[...] = rows[...].reshape(128, 16, 128).astype(bf16)


def gather_field(got, vectors, out, rows, columns):
    rows[...] = got[...].astype(f32).reshape(2048, 128)
    gains, biases = column(vectors[0:1]), column(vectors[1:2])
    low = lax.broadcasted_iota(jnp.int32, (64, 128), 1) < 64
    for jj in range(4):
        for group in range(4):
            near = rows[pl.ds(4 * jj + group, 64, stride=32), :]
            far = rows[pl.ds(16 + 4 * jj + group, 64, stride=32), :]
            columns[pl.ds(2 * group, 64, stride=8), :] = jnp.where(
                low, near, pltpu.roll(far, 64, 1)
            )
            columns[pl.ds(2 * group + 1, 64, stride=8), :] = jnp.where(
                low, pltpu.roll(near, 64, 1), far
            )
        out[jj] = layer_norm(columns[...].T, gains, biases).astype(bf16)


def factors(own, mate, own_far, mate_far, vectors, out, late, field, weights, rows):
    mine, chip = position(), lax.axis_index("xl")
    for step, block in enumerate((own, mate, own_far, mate_far)):
        first = pl.multiple_of((mine ^ step) * 32, 32)
        start = pl.multiple_of(176 * chip if step < 2 else 48 * chip, 16)
        for ii in range(4):
            field[ii, pl.ds(first, 32), :] = block[
                pl.ds(pl.multiple_of(start + 32 * ii, 16), 32), :
            ].astype(f32)
        start = 128 if step < 2 else pl.multiple_of(128 * (1 - chip), 128)
        weights[pl.ds(first, 32), :] = block[pl.ds(start, 32), :]
        after = block[pl.ds(start + 32, 16), :]
        late[pl.ds(first, 16), :] = after[:, 0:256]
        late[pl.ds(pl.multiple_of(first + 16, 16), 16), :] = after[:, 256:512]
    gains, biases = column(vectors[0:1]), column(vectors[1:2])
    for ii in range(4):
        normed = layer_norm(field[ii], gains, biases).astype(bf16)

        def project(which):
            return jnp.dot(
                weights[:, 128 * which : 128 * (which + 1)], normed, preferred_element_type=f32
            )

        for side in range(2):
            factor = jax.nn.sigmoid(project(2 * side + 1)) * project(2 * side)
            for lane in range(4):
                rows[pl.ds(16 * side + 4 * ii + lane, 128, stride=32), :] = factor[
                    :, 128 * lane : 128 * (lane + 1)
                ]
    out[...] = rows[...].reshape(128, 32, 128).astype(bf16)


def products(got, out, received, left, right, rows):
    received[...] = got[...].astype(f32).reshape(4096, 128)
    for lane in range(4):
        for ii in range(4):
            left[lane, pl.ds(ii, 128, stride=4), :] = received[
                pl.ds(4 * ii + lane, 128, stride=32), :
            ]
            right[128 * ii : 128 * (ii + 1), 128 * lane : 128 * (lane + 1)] = received[
                pl.ds(16 + 4 * ii + lane, 128, stride=32), :
            ].astype(bf16)
    whole = jnp.concatenate([left[lane].astype(bf16) for lane in range(4)], axis=1)
    for jj in range(4):
        total = lax.dot_general(
            right[128 * jj : 128 * (jj + 1), :],
            whole,
            (((1,), (1,)), ((), ())),
            preferred_element_type=f32,
        )
        for lane in range(4):
            rows[pl.ds(4 * jj + lane, 128, stride=16), :] = total[
                :, 128 * lane : 128 * (lane + 1)
            ]
    out[...] = rows[...].reshape(128, 16, 128).astype(bf16)


def updates(got, normed_field, late, vectors, out0, out1, out2, out3, rows, update):
    mine = position()
    rows[...] = got[...].astype(f32).reshape(2048, 128)
    gains, biases = column(vectors[2:3]), column(vectors[3:4])
    gate, final = late[:, 0:128], late[:, 128:256]
    for jj in range(4):
        gating = jax.nn.sigmoid(
            jnp.dot(gate, normed_field[jj], preferred_element_type=f32)
        ).astype(bf16)
        for lane in range(4):
            hidden = rows[pl.ds(4 * jj + lane, 128, stride=16), :]
            normed = layer_norm(hidden, gains, biases).astype(bf16)
            value = jnp.dot(final, normed, preferred_element_type=f32)
            at = slice(128 * lane, 128 * (lane + 1))
            update[jj, :, at] = (value * gating[:, at].astype(f32)).astype(bf16)
    for step, out in enumerate((out0, out1, out2, out3)):
        out[...] = update[:, pl.ds(pl.multiple_of((mine ^ step) * 32, 32), 32), :]


def arrange(own, in1, in2, in3, out, rows):
    first = lax.axis_index("core") == 0
    near = 4 * lax.axis_index("xl")
    order = residue_order()
    for lane in range(4):
        at = slice(128 * lane, 128 * (lane + 1))
        for jj in range(4):
            rows[lane, pl.ds(near + jj, 32, stride=8), :] = jnp.where(
                first, own[jj, :, at].astype(f32), in1[jj, :, at].astype(f32)
            )
            rows[lane, pl.ds(4 - near + jj, 32, stride=8), :] = jnp.where(
                first, in2[jj, :, at].astype(f32), in3[jj, :, at].astype(f32)
            )
        placed = jnp.dot(rows[lane].astype(bf16), order, preferred_element_type=f32)
        out[:, :, at] = placed.reshape(32, 8, 128).astype(bf16)


def send(array, *pairs):
    return lax.ppermute(array, ("xl", "core"), pairs)


def unused(*outs):
    return call(lambda *refs: None, "unused", outs, [])()


def body(
    pair_field,
    input_gain,
    input_bias,
    left_weight,
    left_gate,
    right_weight,
    right_gate,
    gate_weight,
    output_gain,
    output_bias,
    final_weight,
):
    same_core = ("y", "z", "xh", "xl")
    first = lax.axis_index("core") == 0
    chip = lax.axis_index("xl")
    weights = (left_weight, left_gate, right_weight, right_gate, gate_weight, final_weight)
    vectors = (input_gain, input_bias, output_gain, output_bias)
    whole, vectors = call(
        lay_out,
        "lay_out",
        (
            pltpu.VMEM((304, 512), bf16),
            pltpu.VMEM((4, 128), f32),
        ),
        [
            pltpu.VMEM((32, 8, 512), bf16),
            pltpu.VMEM((6, 32, 128), bf16),
            pltpu.VMEM((4, 256, 128), f32),
            pltpu.SemaphoreType.DMA((11,)),
        ],
        limit=60 * 1024 * 1024,
        in_specs=[pl.BlockSpec(memory_space=pltpu.HBM)] * 11,
    )(pair_field, *[w.T for w in weights], *[v.reshape(1, 128) for v in vectors])
    mate = send(whole, (0, 1), (1, 0), (2, 3), (3, 2))
    own_far, mate_far = (
        send(lax.dynamic_slice(part, (128 * (1 - chip), 0), (176, 512)), (0, 2), (2, 0))
        for part in (whole, mate)
    )

    def move_field(own, mate, vectors):
        sent = call(
            scatter_field,
            "scatter_field",
            shape(128, 16, 128),
            [
                pltpu.VMEM((512, 512), bf16),
                pltpu.VMEM((512, 128), f32),
                pltpu.VMEM((2048, 128), f32),
            ],
        )(own, mate)
        got = lax.all_to_all(sent, same_core, 0, 0, tiled=True)
        return call(
            gather_field,
            "gather_field",
            shape(4, 128, 512),
            [pltpu.VMEM((2048, 128), f32), pltpu.VMEM((512, 128), f32)],
        )(got, vectors)

    def multiply(own, mate, own_far, mate_far, vectors):
        sent, late = call(
            factors,
            "factors",
            (shape(128, 32, 128), shape(128, 256)),
            [
                pltpu.VMEM((4, 128, 512), f32),
                pltpu.VMEM((128, 512), bf16),
                pltpu.VMEM((4096, 128), f32),
            ],
        )(own, mate, own_far, mate_far, vectors)
        got = lax.all_to_all(sent, same_core, 0, 0, tiled=True)
        sent = call(
            products,
            "products",
            shape(128, 16, 128),
            [
                pltpu.VMEM((4096, 128), f32),
                pltpu.VMEM((4, 512, 128), f32),
                pltpu.VMEM((512, 512), bf16),
                pltpu.VMEM((2048, 128), f32),
            ],
        )(got)
        return sent, late

    def exchange(sent):
        return lax.all_to_all(sent, same_core, 0, 0, tiled=True)

    def update(got, normed_field, late, vectors):
        return call(
            updates,
            "updates",
            (shape(4, 32, 512),) * 4,
            [pltpu.VMEM((2048, 128), f32), pltpu.VMEM((4, 128, 512), bf16)],
        )(got, normed_field, late, vectors)

    normed_field = lax.cond(
        first, lambda *_: unused(shape(4, 128, 512))[0], move_field, whole, mate, vectors
    )
    sent, late = lax.cond(
        first,
        multiply,
        lambda *_: unused(shape(128, 16, 128), shape(128, 256)),
        whole,
        mate,
        own_far,
        mate_far,
        vectors,
    )
    normed_field, sent = lax.optimization_barrier((normed_field, sent))
    normed_field = send(normed_field, (1, 0), (3, 2))
    got = lax.cond(first, exchange, lambda _: unused(shape(128, 16, 128))[0], sent)
    parts = lax.cond(
        first,
        update,
        lambda *_: unused(*(shape(4, 32, 512),) * 4),
        got,
        normed_field,
        late,
        vectors,
    )
    return call(arrange, "arrange", shape(32, 8, 512), [pltpu.VMEM((4, 256, 128), f32)])(
        parts[0],
        send(parts[1], (0, 1), (2, 3)),
        send(parts[2], (0, 2), (2, 0)),
        send(parts[3], (0, 3), (2, 1)),
    )


def solution(mesh):
    mesh = Mesh(mesh.devices.reshape(4, 2, 8, 2, 2), ("y", "xh", "z", "xl", "core"))
    row, ch = ("y", "xh", "z"), ("xl", "core")
    placed = (
        P(ch, row, None),
        P(),
        P(),
        P(None, ch),
        P(None, ch),
        P(None, ch),
        P(None, ch),
        P(None, ch),
        P(),
        P(),
        P(None, ch),
    )
    return jax.shard_map(
        body, mesh=mesh, in_specs=placed, out_specs=P(ch, row, None), check_vma=False
    )
```

time: 341 us -> 88.1 us (0.26)
  waiting for transfers between devices: 276 us -> 28.6 us
  starting transfers between devices: 0.08 us -> 27 us
  between operations: 13.4 us -> 0.11 us
  matrix products: 12.6 us -> 0 us
  other arithmetic: 6.98 us -> 0 us
  local copies, waits for them, and re-layouts: 5.68 us -> 0.03 us
  Pallas kernels: 0 us -> 4.31 us
    all_gather x3 -> x0, waiting for transfers between devices: 275 us -> none  [the longest x1 224 us: body(): lax.all_gather(right_factor, 'row', axis=1, tiled=True)]
    ppermute x0 -> x7, waiting for transfers between devices: none -> 28.6 us  [send(): return lax.ppermute(array, ('xl', 'core'), pairs)]
    ppermute x0 -> x7, starting transfers between devices: none -> 27 us  [send(): return lax.ppermute(array, ('xl', 'core'), pairs)]
    dot_general x7 -> x0, matrix products: 12.6 us -> none  [the longest x1 10.9 us: contract(): jnp.einsum(form, first.astype(jnp.float32), second.astype(jnp.float32), p...]
    reduce_sum x4 -> x0, other arithmetic: 6.13 us -> none  [the longest x2 3.11 us: layer_norm(): variance = jnp.mean(centred * centred, axis=0, keepdims=True)]
    pallas_call x0 -> x7, Pallas kernels: none -> 4.31 us  [the longest x1 1.35 us: move_field(): call(gather_field, 'gather_field', shape(4, 128, 512), [pltpu.VMEM((2048,...]
  transfers between devices with their start and end apart: 3 -> 7, of which waited for: 3 -> 4; matrix products, arithmetic and copies ran while one was open for 0% -> 0% of each run, Pallas kernels for 0% -> 2%
where the time goes in v7:
time: 88.1 us; the launch traced here: 87.8 us
  waiting for transfers between devices  28.6 us (32%)
  blocking collectives  27.7 us (31%)
  starting transfers between devices  27 us (31%)
  Pallas kernels  4.31 us (5%)
    ppermute x7, waiting for transfers between devices, send(): return lax.ppermute(array, ('xl', 'core'), pairs)  28.6 us
    all_to_all x1, blocking collectives, move_field(): got = lax.all_to_all(sent, same_core, 0, 0, tiled=True)  27.7 us
    ppermute x7, starting transfers between devices, send(): return lax.ppermute(array, ('xl', 'core'), pairs)  27 us
  transfers between devices with their start and end apart: 7, of which 4 were waited for; matrix products, arithmetic and copies ran while one was open for 0% of the time, Pallas kernels for 2%

profile of v7, /device:TPU:1, one launch (start us, length us, event | category | flops | bytes accessed | tf_op | source)
XLA Modules:
  0.0 87.8 jit_solution(5152018226654991121)
XLA Ops:
  0.0 1.2 %lay_out.1 = (bf16[304,512]{1,0:T(8,128)(2,1)S(1)}, f32[4,128]{1,0:T(4,128)S(1)}) custom-call(bf16[32,8,512]{2,1,0:T(8,128)(2,1)} %refs_0_.1, bf16[32,128]{1,0:T(8,128)(2,1)} %bitcast.10, bf16[32,128]{1,0:T(8,128)(2,1)} %bitcast.11, bf16[32,128]{1,0:T(8,128)(2,1)} %bitcast.12, bf16[32,128]{1,0:T(8,128)(2,1)} %bitcast.13, bf16[32,128]{1,0:T(8,128)(2,1)} %bitcast.14, ...), custom_call_target="tpu_custom_call" | custom-call | bytes 1048576 | tf_op jit(solution)/shard_map/lay_out/pallas_call | solution.py:241
  1.2 3.3 %collective-permute-start = (bf16[304,512]{1,0:T(8,128)(2,1)S(1)}, bf16[304,512]{1,0:T(8,128)(2,1)S(1)}, u32[]{:S(2)}, u32[]{:S(2)}) collective-permute-start(bf16[304,512]{1,0:T(8,128)(2,1)S(1)} %get-tuple-element.60), channel_id=1, source_target_pairs={{0,1},{1,0},{2,3},{3,2},{4,5},{5,4},{6,7},{7,6},{8,9},{9,8},{10,11... | collective-permute-start | bytes 933896 | tf_op jit(solution)/shard_map/ppermute | solution.py:216
  4.6 0.7 collective-permute-start.1
  5.2 0.5 collective-permute-done
  5.8 0.7 collective-permute-start.2
  6.5 29.7 %conditional.4 = (bf16[4,128,512]{2,1,0:T(8,128)(2,1)S(1)}) conditional(s32[]{:T(128)} %convert_element_type.2, (bf16[304,512]{1,0:T(8,128)(2,1)S(1)}, bf16[304,512]{1,0:T(8,128)(2,1)S(1)}, f32[4,128]{1,0:T(4,128)S(1)}) %tuple.33, () %tuple.34), branch_computations={%region_0.0_spmd, %region_1.0_spmd} | conditional | bytes 3145736 | solution.py:318
  6.5 0.7 scatter_field.1
  7.2 27.7 %all_to_all.12.got = bf16[128,16,128]{2,1,0:T(8,128)(2,1)S(1)} all-to-all(bf16[128,16,128]{2,1,0:T(8,128)(2,1)S(1)} %scatter_field.1), channel_id=1, replica_groups=mesh['y'=4,'xh'=2,'z'=8,'xl'=2,'core'=2] {'y','z','xh','xl'}, dimensions={0} | all-to-all | bytes 1048576 | tf_op jit(solution)/shard_map/cond/branch_0_fun/all_to_all | solution.py:274
  34.9 1.4 %gather_field.1 = bf16[4,128,512]{2,1,0:T(8,128)(2,1)S(1)} custom-call(bf16[128,16,128]{2,1,0:T(8,128)(2,1)S(1)} %all_to_all.12.got, f32[4,128]{1,0:T(4,128)S(1)} %get-tuple-element.38.vectors), custom_call_target="tpu_custom_call" | custom-call | bytes 1048576 | tf_op jit(solution)/shard_map/cond/branch_0_fun/gather_field/pallas_call | solution.py:275
  36.2 0.0 collective-permute-done.1
  36.2 0.0 collective-permute-done.2
  36.3 19.1 %collective-permute-start.3 = (bf16[4,128,512]{2,1,0:T(8,128)(2,1)S(1)}, bf16[4,128,512]{2,1,0:T(8,128)(2,1)S(1)}, u32[]{:S(2)}, u32[]{:S(2)}) collective-permute-start(bf16[4,128,512]{2,1,0:T(8,128)(2,1)S(1)} %get-tuple-element.82), channel_id=1, source_target_pairs={{1,0},{3,2},{5,4},{7,6},{9,8},{11,10},{13,12},{15,14},{17,16},{19,... | collective-permute-start | bytes 1572872 | tf_op jit(solution)/shard_map/ppermute | solution.py:216
  55.4 1.5 %collective-permute-done.3 = bf16[4,128,512]{2,1,0:T(8,128)(2,1)S(1)} collective-permute-done((bf16[4,128,512]{2,1,0:T(8,128)(2,1)S(1)}, bf16[4,128,512]{2,1,0:T(8,128)(2,1)S(1)}, u32[]{:S(2)}, u32[]{:S(2)}) %collective-permute-start.3) | collective-permute-done | bytes 524320 | tf_op jit(solution)/shard_map/ppermute | solution.py:216
  56.8 1.3 %collective-permute-start.4 = (bf16[4,32,512]{2,1,0:T(8,128)(2,1)S(1)}, bf16[4,32,512]{2,1,0:T(8,128)(2,1)S(1)}, u32[]{:S(2)}, u32[]{:S(2)}) collective-permute-start(bf16[4,32,512]{2,1,0:T(8,128)(2,1)S(1)} %get-tuple-element.67), channel_id=1, source_target_pairs={{0,1},{2,3},{4,5},{6,7},{8,9},{10,11},{12,13},{14,15},{16,17},{18,... | collective-permute-start | bytes 393224 | tf_op jit(solution)/shard_map/ppermute | solution.py:216
  58.1 0.7 collective-permute-start.5
  58.8 1.3 %collective-permute-start.6 = (bf16[4,32,512]{2,1,0:T(8,128)(2,1)S(1)}, bf16[4,32,512]{2,1,0:T(8,128)(2,1)S(1)}, u32[]{:S(2)}, u32[]{:S(2)}) collective-permute-start(bf16[4,32,512]{2,1,0:T(8,128)(2,1)S(1)} %get-tuple-element.69), channel_id=1, source_target_pairs={{0,3},{2,1},{4,7},{6,5},{8,11},{10,9},{12,15},{14,13},{16,19},{18,... | collective-permute-start | bytes 393224 | tf_op jit(solution)/shard_map/ppermute | solution.py:216
  60.1 19.9 %collective-permute-done.4.in1 = bf16[4,32,512]{2,1,0:T(8,128)(2,1)S(1)} collective-permute-done((bf16[4,32,512]{2,1,0:T(8,128)(2,1)S(1)}, bf16[4,32,512]{2,1,0:T(8,128)(2,1)S(1)}, u32[]{:S(2)}, u32[]{:S(2)}) %collective-permute-start.4) | collective-permute-done | bytes 131104 | tf_op jit(solution)/shard_map/ppermute | solution.py:216
  80.0 0.0 collective-permute-done.5.in2
  80.0 6.8 %collective-permute-done.6.in3 = bf16[4,32,512]{2,1,0:T(8,128)(2,1)S(1)} collective-permute-done((bf16[4,32,512]{2,1,0:T(8,128)(2,1)S(1)}, bf16[4,32,512]{2,1,0:T(8,128)(2,1)S(1)}, u32[]{:S(2)}, u32[]{:S(2)}) %collective-permute-start.6) | collective-permute-done | bytes 131104 | tf_op jit(solution)/shard_map/ppermute | solution.py:216
  86.7 1.1 %arrange.1 = bf16[32,8,512]{2,1,0:T(8,128)(2,1)} custom-call(bf16[4,32,512]{2,1,0:T(8,128)(2,1)S(1)} %get-tuple-element.66.own, bf16[4,32,512]{2,1,0:T(8,128)(2,1)S(1)} %collective-permute-done.4.in1, bf16[4,32,512]{2,1,0:T(8,128)(2,1)S(1)} %collective-permute-done.5.in2, bf16[4,32,512]{2,1,0:T(8,128)(2,1)S(1)} %collective-permute-done.6.in3), custom_call_target="tpu_custom_call" | custom-call | bytes 1048576 | tf_op jit(solution)/shard_map/arrange/pallas_call | solution.py:343
  (8 shorter events, 0.1 us)
Async XLA Ops:
  1.2 4.6 %collective-permute-start = (bf16[304,512]{1,0:T(8,128)(2,1)S(1)}, bf16[304,512]{1,0:T(8,128)(2,1)S(1)}, u32[]{:S(2)}, u32[]{:S(2)}) collective-permute-start(bf16[304,512]{1,0:T(8,128)(2,1)S(1)} %get-tuple-element.60), channel_id=1, source_target_pairs={{0,1},{1,0},{2,3},{3,2},{4,5},{5,4},{6,7},{7,6},{8,9},{9,8},{10,11... | collective-permute-start | bytes 933896 | tf_op jit(solution)/shard_map/ppermute | solution.py:216
  4.6 31.7 %collective-permute-start.1 = (bf16[176,512]{1,0:T(8,128)(2,1)S(1)}, bf16[176,512]{1,0:T(8,128)(2,1)S(1)}, u32[]{:S(2)}, u32[]{:S(2)}) collective-permute-start(bf16[176,512]{1,0:T(8,128)(2,1)S(1)} %constant_dynamic-slice_fusion.1), channel_id=1, source_target_pairs={{0,2},{2,0},{4,6},{6,4},{8,10},{10,8},{12,14},{14,12},{16,18},{18,... | collective-permute-start | bytes 540680 | tf_op jit(solution)/shard_map/ppermute | solution.py:216
  5.8 30.5 %collective-permute-start.2 = (bf16[176,512]{1,0:T(8,128)(2,1)S(1)}, bf16[176,512]{1,0:T(8,128)(2,1)S(1)}, u32[]{:S(2)}, u32[]{:S(2)}) collective-permute-start(bf16[176,512]{1,0:T(8,128)(2,1)S(1)} %constant_dynamic-slice_fusion), channel_id=1, source_target_pairs={{0,2},{2,0},{4,6},{6,4},{8,10},{10,8},{12,14},{14,12},{16,18},{18,... | collective-permute-start | bytes 540680 | tf_op jit(solution)/shard_map/ppermute | solution.py:216
  36.3 20.6 %collective-permute-start.3 = (bf16[4,128,512]{2,1,0:T(8,128)(2,1)S(1)}, bf16[4,128,512]{2,1,0:T(8,128)(2,1)S(1)}, u32[]{:S(2)}, u32[]{:S(2)}) collective-permute-start(bf16[4,128,512]{2,1,0:T(8,128)(2,1)S(1)} %get-tuple-element.82), channel_id=1, source_target_pairs={{1,0},{3,2},{5,4},{7,6},{9,8},{11,10},{13,12},{15,14},{17,16},{19,... | collective-permute-start | bytes 1572872 | tf_op jit(solution)/shard_map/ppermute | solution.py:216
  56.8 23.1 %collective-permute-start.4 = (bf16[4,32,512]{2,1,0:T(8,128)(2,1)S(1)}, bf16[4,32,512]{2,1,0:T(8,128)(2,1)S(1)}, u32[]{:S(2)}, u32[]{:S(2)}) collective-permute-start(bf16[4,32,512]{2,1,0:T(8,128)(2,1)S(1)} %get-tuple-element.67), channel_id=1, source_target_pairs={{0,1},{2,3},{4,5},{6,7},{8,9},{10,11},{12,13},{14,15},{16,17},{18,... | collective-permute-start | bytes 393224 | tf_op jit(solution)/shard_map/ppermute | solution.py:216
  58.1 21.9 %collective-permute-start.5 = (bf16[4,32,512]{2,1,0:T(8,128)(2,1)S(1)}, bf16[4,32,512]{2,1,0:T(8,128)(2,1)S(1)}, u32[]{:S(2)}, u32[]{:S(2)}) collective-permute-start(bf16[4,32,512]{2,1,0:T(8,128)(2,1)S(1)} %get-tuple-element.68), channel_id=1, source_target_pairs={{0,2},{2,0},{4,6},{6,4},{8,10},{10,8},{12,14},{14,12},{16,18},{18,... | collective-permute-start | bytes 393224 | tf_op jit(solution)/shard_map/ppermute | solution.py:216
  58.8 27.9 %collective-permute-start.6 = (bf16[4,32,512]{2,1,0:T(8,128)(2,1)S(1)}, bf16[4,32,512]{2,1,0:T(8,128)(2,1)S(1)}, u32[]{:S(2)}, u32[]{:S(2)}) collective-permute-start(bf16[4,32,512]{2,1,0:T(8,128)(2,1)S(1)} %get-tuple-element.69), channel_id=1, source_target_pairs={{0,3},{2,1},{4,7},{6,5},{8,11},{10,9},{12,15},{14,13},{16,19},{18,... | collective-permute-start | bytes 393224 | tf_op jit(solution)/shard_map/ppermute | solution.py:216

commit v8 on v6

--- a/solution.py
+++ b/solution.py
@@ -1,5 +1,6 @@
 import jax
 import jax.numpy as jnp
+import numpy as np
 from jax import lax
 from jax.experimental import pallas as pl
 from jax.experimental.pallas import tpu as pltpu
@@ -7,6 +8,7 @@
 from jax.sharding import PartitionSpec as P
 
 epsilon = 1e-05
+first_y, first_z, first_x = 2, 5, 2
 bf16, f32 = jnp.bfloat16, jnp.float32
 vmem_bytes = 16 * 1024 * 1024
 
@@ -41,10 +43,24 @@
     return jnp.broadcast_to(row, (128, 128)).T
 
 
+def peers(core):
+    device = np.arange(256).reshape(4, 2, 8, 2, 2)[..., core]
+    chips = device.transpose(0, 2, 1, 3).reshape(4, 8, 4)
+    chips = np.roll(chips, (-first_y, -first_z, -first_x), (0, 1, 2))
+    return chips.reshape(-1).tolist()
+
+
+def block_of(y):
+    at = 128 * ((y - first_y) % 4)
+    return slice(at, at + 128)
+
+
 def residue_order():
     taken = lax.broadcasted_iota(jnp.int32, (128, 128), 0)
     given = lax.broadcasted_iota(jnp.int32, (128, 128), 1)
-    matches = taken == given % 64 // 8 * 16 + given // 64 * 8 + given % 8
+    z = (given // 8 + 8 - first_z) % 8
+    x = (given // 64 * 2 + given // 4 % 2 + 4 - first_x) % 4
+    matches = taken == 16 * z + 4 * x + given % 4
     return matches.astype(f32).astype(bf16)
 
 
@@ -127,7 +143,7 @@
         ).astype(bf16)
         for lane in range(4):
             at = slice(128 * lane, 128 * (lane + 1))
-            rows[at] = lax.dot_general(
+            rows[block_of(lane)] = lax.dot_general(
                 order, value[:, at], (((1,), (1,)), ((), ())), preferred_element_type=f32
             )
         for jj in range(2):
@@ -191,6 +207,7 @@
 def arrange(in0, in1, in2, in3, out, rows):
     mine = position()
     order = residue_order()
+    natural = {block_of(y).start // 128: slice(128 * y, 128 * (y + 1)) for y in range(4)}
     for lane in range(4):
         at = slice(128 * lane, 128 * (lane + 1))
         for step, block in enumerate((in0, in1, in2, in3)):
@@ -199,7 +216,7 @@
                     jj, :, at
                 ].astype(f32)
         placed = jnp.dot(rows[lane].astype(bf16), order, preferred_element_type=f32)
-        out[:, :, at] = placed.reshape(32, 8, 128).astype(bf16)
+        out[:, :, natural[lane]] = placed.reshape(32, 8, 128).astype(bf16)
 
 
 def swap(array, step):
@@ -209,6 +226,17 @@
 def around(array, step):
     pairs = [(s, s ^ (4 + step)) for s in range(8)]
     return lax.ppermute(array, ("xh", "xl", "core"), pairs)
+
+
+def scatter(messages):
+    return lax.all_to_all(
+        messages,
+        ("y", "xh", "z", "xl", "core"),
+        0,
+        0,
+        axis_index_groups=[peers(0), peers(1)],
+        tiled=True,
+    )
 
 
 def exchange(parts):
@@ -228,7 +256,6 @@
     output_bias,
     final_weight,
 ):
-    same_core = ("y", "z", "xh", "xl")
     weights = (left_weight, left_gate, right_weight, right_gate, gate_weight, final_weight)
     vectors = (input_gain, input_bias, output_gain, output_bias)
     *parts, shared, vectors = call(
@@ -255,7 +282,7 @@
             pltpu.VMEM((2048, 128), f32),
         ],
     )(*exchange(parts), around(shared, 2), around(shared, 3), vectors)
-    own = lax.all_to_all(sent, same_core, 0, 0, tiled=True)
+    own = scatter(sent)
     kept, given = call(
         gates,
         "gates",
@@ -274,7 +301,7 @@
             pltpu.VMEM((2048, 128), f32),
         ],
     )(own, swap(own[:, :8], 1), kept, swap(given, 1))
-    got = lax.all_to_all(sent, same_core, 0, 0, tiled=True)
+    got = scatter(sent)
     parts = call(
         updates,
         "updates",

time: 83 us -> 78.3 us (0.943)
  blocking collectives: 54.3 us -> 51.2 us
  starting transfers between devices: 15.4 us -> 13.8 us
    all_to_all x2, blocking collectives: 54.3 us -> 51.2 us  [scatter(): lax.all_to_all(messages, ('y', 'xh', 'z', 'xl', 'core'), 0, 0, axis_index...]
    ppermute x8, starting transfers between devices: 12.7 us -> 11.1 us  [swap(): lax.ppermute(array, ('xl', 'core'), [(s, s ^ step) for s in range(4)])]
where the time goes in v8:
time: 78.3 us; the launch traced here: 78.1 us
  blocking collectives  51.2 us (65%)
  starting transfers between devices  13.8 us (18%)
  waiting for transfers between devices  7.76 us (10%)
  Pallas kernels  5.35 us (7%)
    all_to_all x2, blocking collectives, scatter(): lax.all_to_all(messages, ('y', 'xh', 'z', 'xl', 'core'), 0, 0, axis_index...  51.2 us
    ppermute x8, starting transfers between devices, swap(): lax.ppermute(array, ('xl', 'core'), [(s, s ^ step) for s in range(4)])  11.1 us
    ppermute x8, waiting for transfers between devices, swap(): lax.ppermute(array, ('xl', 'core'), [(s, s ^ step) for s in range(4)])  4.88 us
    ppermute x2, waiting for transfers between devices, around(): return lax.ppermute(array, ('xh', 'xl', 'core'), pairs)  2.88 us
    ppermute x2, starting transfers between devices, around(): return lax.ppermute(array, ('xh', 'xl', 'core'), pairs)  2.72 us
  transfers between devices with their start and end apart: 10, of which 5 were waited for; matrix products, arithmetic and copies ran while one was open for 0% of the time, Pallas kernels for 1%

profile of v8, /device:TPU:1, one launch (start us, length us, event | category | flops | bytes accessed | tf_op | source)
XLA Modules:
  0.0 78.1 jit_solution(2437319139692198540)
XLA Ops:
  0.0 1.2 %lay_out.1 = (bf16[112,512]{1,0:T(8,128)(2,1)S(1)}, bf16[112,512]{1,0:T(8,128)(2,1)S(1)}, bf16[64,512]{1,0:T(8,128)(2,1)S(1)}, bf16[64,512]{1,0:T(8,128)(2,1)S(1...) custom-call(bf16[32,8,512]{2,1,0:T(8,128)(2,1)} %refs_0_.1, bf16[32,128]{1,0:T(8,128)(2,1)} %bitcast.10, ...), custom_call_target="tpu_custom_call" | custom-call | bytes 1048576 | tf_op jit(solution)/shard_map/lay_out/pallas_call | solution.py:261
  1.2 3.3 %collective-permute-start = (bf16[112,512]{1,0:T(8,128)(2,1)S(1)}, bf16[112,512]{1,0:T(8,128)(2,1)S(1)}, u32[]{:S(2)}, u32[]{:S(2)}) collective-permute-start(bf16[112,512]{1,0:T(8,128)(2,1)S(1)} %get-tuple-element.21), channel_id=1, source_target_pairs={{0,1},{1,0},{2,3},{3,2},{4,5},{5,4},{6,7},{7,6},{8,9},{9,8},{10,11... | collective-permute-start | bytes 344072 | tf_op jit(solution)/shard_map/ppermute | solution.py:223
  4.6 0.0 collective-permute-start.1
  4.6 1.7 %collective-permute-start.2 = (bf16[64,512]{1,0:T(8,128)(2,1)S(1)}, bf16[64,512]{1,0:T(8,128)(2,1)S(1)}, u32[]{:S(2)}, u32[]{:S(2)}) collective-permute-start(bf16[64,512]{1,0:T(8,128)(2,1)S(1)} %get-tuple-element.23), channel_id=1, source_target_pairs={{0,3},{1,2},{2,1},{3,0},{4,7},{5,6},{6,5},{7,4},{8,11},{9,10},{10,... | collective-permute-start | bytes 196616 | tf_op jit(solution)/shard_map/ppermute | solution.py:223
  6.3 0.8 %collective-permute-start.4 = (bf16[48,512]{1,0:T(8,128)(2,1)S(1)}, bf16[48,512]{1,0:T(8,128)(2,1)S(1)}, u32[]{:S(2)}, u32[]{:S(2)}) collective-permute-start(bf16[48,512]{1,0:T(8,128)(2,1)S(1)} %get-tuple-element.24), channel_id=1, source_target_pairs={{0,35},{1,34},{2,33},{3,32},{32,3},{33,2},{34,1},{35,0},{4,39},{5,... | collective-permute-start | bytes 147464 | tf_op jit(solution)/shard_map/ppermute | solution.py:228
  7.1 1.9 %collective-permute-start.3 = (bf16[48,512]{1,0:T(8,128)(2,1)S(1)}, bf16[48,512]{1,0:T(8,128)(2,1)S(1)}, u32[]{:S(2)}, u32[]{:S(2)}) collective-permute-start(bf16[48,512]{1,0:T(8,128)(2,1)S(1)} %get-tuple-element.24), channel_id=1, source_target_pairs={{0,34},{1,35},{2,32},{3,33},{32,2},{33,3},{34,0},{35,1},{4,38},{5,... | collective-permute-start | bytes 147464 | tf_op jit(solution)/shard_map/ppermute | solution.py:228
  9.0 2.3 %collective-permute-done.4.shared3 = bf16[48,512]{1,0:T(8,128)(2,1)S(1)} collective-permute-done((bf16[48,512]{1,0:T(8,128)(2,1)S(1)}, bf16[48,512]{1,0:T(8,128)(2,1)S(1)}, u32[]{:S(2)}, u32[]{:S(2)}) %collective-permute-start.4) | collective-permute-done | bytes 49184 | tf_op jit(solution)/shard_map/ppermute | solution.py:228
  11.3 0.6 collective-permute-done.3.shared2
  11.9 0.0 collective-permute-done.1.in2
  11.9 0.0 collective-permute-done.2.in3
  11.9 0.0 collective-permute-done.in1
  11.9 0.8 factors.1
  12.7 26.3 %all_to_all.10.own = bf16[128,16,128]{2,1,0:T(8,128)(2,1)S(1)} all-to-all(bf16[128,16,128]{2,1,0:T(8,128)(2,1)S(1)} %get-tuple-element.26), channel_id=1, replica_groups={{180,182,148,150,184,186,152,154,188,190,156,158,160,162,128,130,164,16..., dimensions={0} | all-to-all | bytes 1048576 | tf_op jit(solution)/shard_map/all_to_all | solution.py:232
  39.0 2.7 %collective-permute-start.5 = (bf16[128,8,128]{2,1,0:T(8,128)(2,1)S(1)}, bf16[128,8,128]{2,1,0:T(8,128)(2,1)S(1)}, u32[]{:S(2)}, u32[]{:S(2)}) collective-permute-start(bf16[128,8,128]{2,1,0:T(8,128)(2,1)S(1)} %slice.4), channel_id=1, source_target_pairs={{0,1},{1,0},{2,3},{3,2},{4,5},{5,4},{6,7},{7,6},{8,9},{9,8},{10,11... | collective-permute-start | bytes 786440 | tf_op jit(solution)/shard_map/ppermute | solution.py:223
  41.7 0.6 gates.1
  42.3 0.1 collective-permute-start.6
  42.4 1.3 %collective-permute-done.6.given = bf16[4,128,128]{2,1,0:T(8,128)(2,1)S(1)} collective-permute-done((bf16[4,128,128]{2,1,0:T(8,128)(2,1)S(1)}, bf16[4,128,128]{2,1,0:T(8,128)(2,1)S(1)}, u32[]{:S(2)}, u32[]{:S(2)}) %collective-permute-start.6) | collective-permute-done | bytes 131104 | tf_op jit(solution)/shard_map/ppermute | solution.py:223
  43.7 0.0 collective-permute-done.5.other
  43.7 1.0 %products.1 = bf16[128,16,128]{2,1,0:T(8,128)(2,1)S(1)} custom-call(bf16[128,16,128]{2,1,0:T(8,128)(2,1)S(1)} %all_to_all.10.own, bf16[128,8,128]{2,1,0:T(8,128)(2,1)S(1)} %collective-permute-done.5.other, bf16[4,128,128]{2,1,0:T(8,128)(2,1)S(1)} %get-tuple-element.29.kept, bf16[4,128,128]{2,1,0:T(8,128)(2,1)S(1)} %collective-permute-done.6.given), custom_call_target="tpu_custom_call" | custom-call | bytes 1048576 | tf_op jit(solution)/shard_map/products/pallas_call | solution.py:293
  44.8 24.9 %all_to_all.11.got = bf16[128,16,128]{2,1,0:T(8,128)(2,1)S(1)} all-to-all(bf16[128,16,128]{2,1,0:T(8,128)(2,1)S(1)} %products.1), channel_id=1, replica_groups={{180,182,148,150,184,186,152,154,188,190,156,158,160,162,128,130,164,16..., dimensions={0} | all-to-all | bytes 1048576 | tf_op jit(solution)/shard_map/all_to_all | solution.py:232
  69.7 0.7 updates.1
  70.4 1.5 %collective-permute-start.7 = (bf16[2,32,512]{2,1,0:T(8,128)(2,1)S(1)}, bf16[2,32,512]{2,1,0:T(8,128)(2,1)S(1)}, u32[]{:S(2)}, u32[]{:S(2)}) collective-permute-start(bf16[2,32,512]{2,1,0:T(8,128)(2,1)S(1)} %get-tuple-element.32), channel_id=1, source_target_pairs={{0,1},{1,0},{2,3},{3,2},{4,5},{5,4},{6,7},{7,6},{8,9},{9,8},{10,11... | collective-permute-start | bytes 196616 | tf_op jit(solution)/shard_map/ppermute | solution.py:223
  71.8 1.0 %collective-permute-start.8 = (bf16[2,32,512]{2,1,0:T(8,128)(2,1)S(1)}, bf16[2,32,512]{2,1,0:T(8,128)(2,1)S(1)}, u32[]{:S(2)}, u32[]{:S(2)}) collective-permute-start(bf16[2,32,512]{2,1,0:T(8,128)(2,1)S(1)} %get-tuple-element.33), channel_id=1, source_target_pairs={{0,2},{1,3},{2,0},{3,1},{4,6},{5,7},{6,4},{7,5},{8,10},{9,11},{10,... | collective-permute-start | bytes 196616 | tf_op jit(solution)/shard_map/ppermute | solution.py:223
  72.8 0.8 collective-permute-start.9
  73.6 0.0 collective-permute-done.7.in1
  73.6 1.9 %collective-permute-done.8.in2 = bf16[2,32,512]{2,1,0:T(8,128)(2,1)S(1)} collective-permute-done((bf16[2,32,512]{2,1,0:T(8,128)(2,1)S(1)}, bf16[2,32,512]{2,1,0:T(8,128)(2,1)S(1)}, u32[]{:S(2)}, u32[]{:S(2)}) %collective-permute-start.8) | collective-permute-done | bytes 65568 | tf_op jit(solution)/shard_map/ppermute | solution.py:223
  75.5 1.6 %collective-permute-done.9.in3 = bf16[2,32,512]{2,1,0:T(8,128)(2,1)S(1)} collective-permute-done((bf16[2,32,512]{2,1,0:T(8,128)(2,1)S(1)}, bf16[2,32,512]{2,1,0:T(8,128)(2,1)S(1)}, u32[]{:S(2)}, u32[]{:S(2)}) %collective-permute-start.9) | collective-permute-done | bytes 65568 | tf_op jit(solution)/shard_map/ppermute | solution.py:223
  77.1 1.0 %arrange.1 = bf16[32,8,512]{2,1,0:T(8,128)(2,1)} custom-call(bf16[2,32,512]{2,1,0:T(8,128)(2,1)S(1)} %get-tuple-element.31.in0, bf16[2,32,512]{2,1,0:T(8,128)(2,1)S(1)} %collective-permute-done.7.in1, bf16[2,32,512]{2,1,0:T(8,128)(2,1)S(1)} %collective-permute-done.8.in2, bf16[2,32,512]{2,1,0:T(8,128)(2,1)S(1)} %collective-permute-done.9.in3), custom_call_target="tpu_custom_call" | custom-call | bytes 1048576 | tf_op jit(solution)/shard_map/arrange/pallas_call | solution.py:315
  (1 shorter events, 0.0 us)
Async XLA Ops:
  1.2 10.7 %collective-permute-start = (bf16[112,512]{1,0:T(8,128)(2,1)S(1)}, bf16[112,512]{1,0:T(8,128)(2,1)S(1)}, u32[]{:S(2)}, u32[]{:S(2)}) collective-permute-start(bf16[112,512]{1,0:T(8,128)(2,1)S(1)} %get-tuple-element.21), channel_id=1, source_target_pairs={{0,1},{1,0},{2,3},{3,2},{4,5},{5,4},{6,7},{7,6},{8,9},{9,8},{10,11... | collective-permute-start | bytes 344072 | tf_op jit(solution)/shard_map/ppermute | solution.py:223
  4.6 7.3 %collective-permute-start.1 = (bf16[64,512]{1,0:T(8,128)(2,1)S(1)}, bf16[64,512]{1,0:T(8,128)(2,1)S(1)}, u32[]{:S(2)}, u32[]{:S(2)}) collective-permute-start(bf16[64,512]{1,0:T(8,128)(2,1)S(1)} %get-tuple-element.22), channel_id=1, source_target_pairs={{0,2},{1,3},{2,0},{3,1},{4,6},{5,7},{6,4},{7,5},{8,10},{9,11},{10,... | collective-permute-start | bytes 196616 | tf_op jit(solution)/shard_map/ppermute | solution.py:223
  4.6 7.3 %collective-permute-start.2 = (bf16[64,512]{1,0:T(8,128)(2,1)S(1)}, bf16[64,512]{1,0:T(8,128)(2,1)S(1)}, u32[]{:S(2)}, u32[]{:S(2)}) collective-permute-start(bf16[64,512]{1,0:T(8,128)(2,1)S(1)} %get-tuple-element.23), channel_id=1, source_target_pairs={{0,3},{1,2},{2,1},{3,0},{4,7},{5,6},{6,5},{7,4},{8,11},{9,10},{10,... | collective-permute-start | bytes 196616 | tf_op jit(solution)/shard_map/ppermute | solution.py:223
  6.3 5.0 %collective-permute-start.4 = (bf16[48,512]{1,0:T(8,128)(2,1)S(1)}, bf16[48,512]{1,0:T(8,128)(2,1)S(1)}, u32[]{:S(2)}, u32[]{:S(2)}) collective-permute-start(bf16[48,512]{1,0:T(8,128)(2,1)S(1)} %get-tuple-element.24), channel_id=1, source_target_pairs={{0,35},{1,34},{2,33},{3,32},{32,3},{33,2},{34,1},{35,0},{4,39},{5,... | collective-permute-start | bytes 147464 | tf_op jit(solution)/shard_map/ppermute | solution.py:228
  7.1 4.8 %collective-permute-start.3 = (bf16[48,512]{1,0:T(8,128)(2,1)S(1)}, bf16[48,512]{1,0:T(8,128)(2,1)S(1)}, u32[]{:S(2)}, u32[]{:S(2)}) collective-permute-start(bf16[48,512]{1,0:T(8,128)(2,1)S(1)} %get-tuple-element.24), channel_id=1, source_target_pairs={{0,34},{1,35},{2,32},{3,33},{32,2},{33,3},{34,0},{35,1},{4,38},{5,... | collective-permute-start | bytes 147464 | tf_op jit(solution)/shard_map/ppermute | solution.py:228
  39.0 4.7 %collective-permute-start.5 = (bf16[128,8,128]{2,1,0:T(8,128)(2,1)S(1)}, bf16[128,8,128]{2,1,0:T(8,128)(2,1)S(1)}, u32[]{:S(2)}, u32[]{:S(2)}) collective-permute-start(bf16[128,8,128]{2,1,0:T(8,128)(2,1)S(1)} %slice.4), channel_id=1, source_target_pairs={{0,1},{1,0},{2,3},{3,2},{4,5},{5,4},{6,7},{7,6},{8,9},{9,8},{10,11... | collective-permute-start | bytes 786440 | tf_op jit(solution)/shard_map/ppermute | solution.py:223
  42.3 1.4 %collective-permute-start.6 = (bf16[4,128,128]{2,1,0:T(8,128)(2,1)S(1)}, bf16[4,128,128]{2,1,0:T(8,128)(2,1)S(1)}, u32[]{:S(2)}, u32[]{:S(2)}) collective-permute-start(bf16[4,128,128]{2,1,0:T(8,128)(2,1)S(1)} %get-tuple-element.30), channel_id=1, source_target_pairs={{0,1},{1,0},{2,3},{3,2},{4,5},{5,4},{6,7},{7,6},{8,9},{9,8},{10,11... | collective-permute-start | bytes 393224 | tf_op jit(solution)/shard_map/ppermute | solution.py:223
  70.4 3.2 %collective-permute-start.7 = (bf16[2,32,512]{2,1,0:T(8,128)(2,1)S(1)}, bf16[2,32,512]{2,1,0:T(8,128)(2,1)S(1)}, u32[]{:S(2)}, u32[]{:S(2)}) collective-permute-start(bf16[2,32,512]{2,1,0:T(8,128)(2,1)S(1)} %get-tuple-element.32), channel_id=1, source_target_pairs={{0,1},{1,0},{2,3},{3,2},{4,5},{5,4},{6,7},{7,6},{8,9},{9,8},{10,11... | collective-permute-start | bytes 196616 | tf_op jit(solution)/shard_map/ppermute | solution.py:223
  71.8 3.7 %collective-permute-start.8 = (bf16[2,32,512]{2,1,0:T(8,128)(2,1)S(1)}, bf16[2,32,512]{2,1,0:T(8,128)(2,1)S(1)}, u32[]{:S(2)}, u32[]{:S(2)}) collective-permute-start(bf16[2,32,512]{2,1,0:T(8,128)(2,1)S(1)} %get-tuple-element.33), channel_id=1, source_target_pairs={{0,2},{1,3},{2,0},{3,1},{4,6},{5,7},{6,4},{7,5},{8,10},{9,11},{10,... | collective-permute-start | bytes 196616 | tf_op jit(solution)/shard_map/ppermute | solution.py:223
  72.8 4.3 %collective-permute-start.9 = (bf16[2,32,512]{2,1,0:T(8,128)(2,1)S(1)}, bf16[2,32,512]{2,1,0:T(8,128)(2,1)S(1)}, u32[]{:S(2)}, u32[]{:S(2)}) collective-permute-start(bf16[2,32,512]{2,1,0:T(8,128)(2,1)S(1)} %get-tuple-element.34), channel_id=1, source_target_pairs={{0,3},{1,2},{2,1},{3,0},{4,7},{5,6},{6,5},{7,4},{8,11},{9,10},{10,... | collective-permute-start | bytes 196616 | tf_op jit(solution)/shard_map/ppermute | solution.py:223

commit v9 on v8

--- a/solution.py
+++ b/solution.py
@@ -1,6 +1,5 @@
 import jax
 import jax.numpy as jnp
-import numpy as np
 from jax import lax
 from jax.experimental import pallas as pl
 from jax.experimental.pallas import tpu as pltpu
@@ -8,7 +7,7 @@
 from jax.sharding import PartitionSpec as P
 
 epsilon = 1e-05
-first_y, first_z, first_x = 2, 5, 2
+far_chip = 90
 bf16, f32 = jnp.bfloat16, jnp.float32
 vmem_bytes = 16 * 1024 * 1024
 
@@ -44,24 +43,16 @@
 
 
 def peers(core):
-    device = np.arange(256).reshape(4, 2, 8, 2, 2)[..., core]
-    chips = device.transpose(0, 2, 1, 3).reshape(4, 8, 4)
-    chips = np.roll(chips, (-first_y, -first_z, -first_x), (0, 1, 2))
-    return chips.reshape(-1).tolist()
-
-
-def block_of(y):
-    at = 128 * ((y - first_y) % 4)
-    return slice(at, at + 128)
-
-
-def residue_order():
-    taken = lax.broadcasted_iota(jnp.int32, (128, 128), 0)
-    given = lax.broadcasted_iota(jnp.int32, (128, 128), 1)
-    z = (given // 8 + 8 - first_z) % 8
-    x = (given // 64 * 2 + given // 4 % 2 + 4 - first_x) % 4
-    matches = taken == 16 * z + 4 * x + given % 4
-    return matches.astype(f32).astype(bf16)
+    devices = list(range(core, 256, 2))
+    devices[0], devices[far_chip] = devices[far_chip], devices[0]
+    return devices
+
+
+def restore(rows):
+    first, far = slice(0, 4), slice(4 * far_chip, 4 * far_chip + 4)
+    kept = rows[first, :]
+    rows[first, :] = rows[far, :]
+    rows[far, :] = kept
 
 
 def position():
@@ -96,7 +87,7 @@
                 out[32 * ii : 32 * (ii + 1), at] = rows[
                     lane, pl.ds(2 * (mine ^ step) + ii, 32, stride=8), :
                 ].astype(bf16)
-    for out, first in ((outs[0], 64), (outs[1], 64), (shared, 0)):
+    for out, first in ((outs[0], 64), (outs[1], 64), (outs[2], 64), (shared, 0)):
         for lane in range(4):
             at = slice(128 * lane, 128 * (lane + 1))
             out[first : first + 32, at] = weights[lane]
@@ -105,13 +96,13 @@
             ]
 
 
-def factors(in0, in1, in2, in3, shared2, shared3, vectors, out, normed_out, late, field, weights, rows):
+def factors(in0, in1, in2, in3, shared3, vectors, out, normed_out, late, field, weights, rows):
     mine = position()
     for step, block in enumerate((in0, in1, in2, in3)):
         first = pl.multiple_of((mine ^ step) * 32, 32)
         for ii in range(2):
             field[ii, pl.ds(first, 32), :] = block[32 * ii : 32 * (ii + 1), :].astype(f32)
-        block = (in0.at[64:112], in1.at[64:112], shared2, shared3)[step]
+        block = (in0.at[64:112], in1.at[64:112], in2.at[64:112], shared3)[step]
         weights[pl.ds(first, 32), :] = block[0:32, :]
         late[pl.ds(first, 16), :] = block[32:48, 0:256]
         late[pl.ds(pl.multiple_of(first + 16, 16), 16), :] = block[32:48, 256:512]
@@ -136,16 +127,10 @@
 
 def gates(normed, late, kept, given, rows):
     core = lax.axis_index("core")
-    order = residue_order()
     for ii in range(2):
-        value = jax.nn.sigmoid(
-            jnp.dot(late[:, 0:128], normed[ii], preferred_element_type=f32)
-        ).astype(bf16)
-        for lane in range(4):
-            at = slice(128 * lane, 128 * (lane + 1))
-            rows[block_of(lane)] = lax.dot_general(
-                order, value[:, at], (((1,), (1,)), ((), ())), preferred_element_type=f32
-            )
+        value = jax.nn.sigmoid(jnp.dot(late[:, 0:128], normed[ii], preferred_element_type=f32))
+        rows[...] = value.T
+        restore(rows)
         for jj in range(2):
             kept[2 * ii + jj] = rows[pl.ds(2 * core + jj, 128, stride=4), :].astype(bf16)
             given[2 * ii + jj] = rows[pl.ds(2 * (1 - core) + jj, 128, stride=4), :].astype(bf16)
@@ -164,6 +149,7 @@
             left[lane, pl.ds(2 * (1 - core) + ii, 128, stride=4), :] = other_rows[
                 pl.ds(4 * ii + lane, 128, stride=8), :
             ]
+        restore(left.at[lane])
         right = jnp.concatenate(
             [mine_rows[pl.ds(8 + 4 * jj + lane, 128, stride=16), :] for jj in range(2)], axis=0
         ).astype(bf16)
@@ -193,6 +179,7 @@
             gate_rows[pl.ds(ii, 128, stride=4), :] = rows[
                 pl.ds(8 + 4 * jj + ii, 128, stride=16), :
             ]
+        restore(gate_rows)
         gating = gate_rows[...].T
         for lane in range(4):
             hidden = rows[pl.ds(4 * jj + lane, 128, stride=16), :]
@@ -206,8 +193,6 @@
 
 def arrange(in0, in1, in2, in3, out, rows):
     mine = position()
-    order = residue_order()
-    natural = {block_of(y).start // 128: slice(128 * y, 128 * (y + 1)) for y in range(4)}
     for lane in range(4):
         at = slice(128 * lane, 128 * (lane + 1))
         for step, block in enumerate((in0, in1, in2, in3)):
@@ -215,8 +200,7 @@
                 rows[lane, pl.ds(2 * (mine ^ step) + jj, 32, stride=8), :] = block[
                     jj, :, at
                 ].astype(f32)
-        placed = jnp.dot(rows[lane].astype(bf16), order, preferred_element_type=f32)
-        out[:, :, natural[lane]] = placed.reshape(32, 8, 128).astype(bf16)
+        out[:, :, at] = rows[lane].reshape(32, 8, 128).astype(bf16)
 
 
 def swap(array, step):
@@ -261,7 +245,7 @@
     *parts, shared, vectors = call(
         lay_out,
         "lay_out",
-        tuple(pltpu.VMEM((high, 512), bf16) for high in (112, 112, 64, 64, 48))
+        tuple(pltpu.VMEM((high, 512), bf16) for high in (112, 112, 112, 64, 48))
         + (pltpu.VMEM((4, 128), f32),),
         [
             pltpu.VMEM((32, 8, 512), bf16),
@@ -281,7 +265,7 @@
             pltpu.VMEM((128, 512), bf16),
             pltpu.VMEM((2048, 128), f32),
         ],
-    )(*exchange(parts), around(shared, 2), around(shared, 3), vectors)
+    )(*exchange(parts), around(shared, 3), vectors)
     own = scatter(sent)
     kept, given = call(
         gates,

time: 78.3 us -> 77 us (0.983)
  starting transfers between devices: 13.8 us -> 10.8 us
  waiting for transfers between devices: 7.76 us -> 8.79 us
  blocking collectives: 51.2 us -> 52.2 us
    ppermute x2 -> x1, starting transfers between devices: 2.72 us -> 0.79 us  [around(): return lax.ppermute(array, ('xh', 'xl', 'core'), pairs)]
    ppermute x2 -> x1, waiting for transfers between devices: 2.88 us -> 3.94 us  [around(): return lax.ppermute(array, ('xh', 'xl', 'core'), pairs)]
    ppermute x8, starting transfers between devices: 11.1 us -> 10 us  [swap(): lax.ppermute(array, ('xl', 'core'), [(s, s ^ step) for s in range(4)])]
    all_to_all x2, blocking collectives: 51.2 us -> 52.2 us  [scatter(): lax.all_to_all(messages, ('y', 'xh', 'z', 'xl', 'core'), 0, 0, axis_index...]
  transfers between devices with their start and end apart: 10 -> 9, of which waited for: 5 -> 4; matrix products, arithmetic and copies ran while one was open for 0% -> 0% of each run, Pallas kernels for 1% -> 0%
where the time goes in v9:
time: 77 us; the launch traced here: 76.8 us
  blocking collectives  52.2 us (68%)
  starting transfers between devices  10.8 us (14%)
  waiting for transfers between devices  8.79 us (11%)
  Pallas kernels  4.94 us (6%)
    all_to_all x2, blocking collectives, scatter(): lax.all_to_all(messages, ('y', 'xh', 'z', 'xl', 'core'), 0, 0, axis_index...  52.2 us
    ppermute x8, starting transfers between devices, swap(): lax.ppermute(array, ('xl', 'core'), [(s, s ^ step) for s in range(4)])  10 us
    ppermute x8, waiting for transfers between devices, swap(): lax.ppermute(array, ('xl', 'core'), [(s, s ^ step) for s in range(4)])  4.85 us
    ppermute x1, waiting for transfers between devices, around(): return lax.ppermute(array, ('xh', 'xl', 'core'), pairs)  3.94 us
  transfers between devices with their start and end apart: 9, of which 4 were waited for; matrix products, arithmetic and copies ran while one was open for 0% of the time, Pallas kernels for 0%

profile of v9, /device:TPU:1, one launch (start us, length us, event | category | flops | bytes accessed | tf_op | source)
XLA Modules:
  0.0 76.8 jit_solution(6740114342687799514)
XLA Ops:
  0.0 1.2 %lay_out.1 = (bf16[112,512]{1,0:T(8,128)(2,1)S(1)}, bf16[112,512]{1,0:T(8,128)(2,1)S(1)}, bf16[112,512]{1,0:T(8,128)(2,1)S(1)}, bf16[64,512]{1,0:T(8,128)(2,1)S(...) custom-call(bf16[32,8,512]{2,1,0:T(8,128)(2,1)} %refs_0_.1, bf16[32,128]{1,0:T(8,128)(2,1)} %bitcast.10, ...), custom_call_target="tpu_custom_call" | custom-call | bytes 1048576 | tf_op jit(solution)/shard_map/lay_out/pallas_call | solution.py:245
  1.2 3.3 %collective-permute-start = (bf16[112,512]{1,0:T(8,128)(2,1)S(1)}, bf16[112,512]{1,0:T(8,128)(2,1)S(1)}, u32[]{:S(2)}, u32[]{:S(2)}) collective-permute-start(bf16[112,512]{1,0:T(8,128)(2,1)S(1)} %get-tuple-element.21), channel_id=1, source_target_pairs={{0,1},{1,0},{2,3},{3,2},{4,5},{5,4},{6,7},{7,6},{8,9},{9,8},{10,11... | collective-permute-start | bytes 344072 | tf_op jit(solution)/shard_map/ppermute | solution.py:207
  4.6 0.0 collective-permute-start.1
  4.6 1.7 %collective-permute-start.2 = (bf16[64,512]{1,0:T(8,128)(2,1)S(1)}, bf16[64,512]{1,0:T(8,128)(2,1)S(1)}, u32[]{:S(2)}, u32[]{:S(2)}) collective-permute-start(bf16[64,512]{1,0:T(8,128)(2,1)S(1)} %get-tuple-element.23), channel_id=1, source_target_pairs={{0,3},{1,2},{2,1},{3,0},{4,7},{5,6},{6,5},{7,4},{8,11},{9,10},{10,... | collective-permute-start | bytes 196616 | tf_op jit(solution)/shard_map/ppermute | solution.py:207
  6.3 0.8 %collective-permute-start.3 = (bf16[48,512]{1,0:T(8,128)(2,1)S(1)}, bf16[48,512]{1,0:T(8,128)(2,1)S(1)}, u32[]{:S(2)}, u32[]{:S(2)}) collective-permute-start(bf16[48,512]{1,0:T(8,128)(2,1)S(1)} %get-tuple-element.24), channel_id=1, source_target_pairs={{0,35},{1,34},{2,33},{3,32},{32,3},{33,2},{34,1},{35,0},{4,39},{5,... | collective-permute-start | bytes 147464 | tf_op jit(solution)/shard_map/ppermute | solution.py:212
  7.1 3.9 %collective-permute-done.3.shared3 = bf16[48,512]{1,0:T(8,128)(2,1)S(1)} collective-permute-done((bf16[48,512]{1,0:T(8,128)(2,1)S(1)}, bf16[48,512]{1,0:T(8,128)(2,1)S(1)}, u32[]{:S(2)}, u32[]{:S(2)}) %collective-permute-start.3) | collective-permute-done | bytes 49184 | tf_op jit(solution)/shard_map/ppermute | solution.py:212
  11.0 0.0 collective-permute-done.2.in3
  11.0 0.0 collective-permute-done.in1
  11.0 0.0 collective-permute-done.1.in2
  11.0 0.8 %factors.1 = (bf16[128,16,128]{2,1,0:T(8,128)(2,1)S(1)}, bf16[2,128,512]{2,1,0:T(8,128)(2,1)S(1)}, bf16[128,256]{1,0:T(8,128)(2,1)S(1)}) custom-call(bf16[112,512]{1,0:T(8,128)(2,1)S(1)} %get-tuple-element.20.in0, bf16[112,512]{1,0:T(8,128)(2,1)S(1)} %collective-permute-done.in1, bf16[112,512]{1,0:T(8,128)(2,1)S(1)} %collective-permute-done.1.in2, ...), custom_call_target="tpu_custom_call" | custom-call | bytes 1048576 | tf_op jit(solution)/shard_map/factors/pallas_call | solution.py:259
  11.8 27.2 %all_to_all.10.own = bf16[128,16,128]{2,1,0:T(8,128)(2,1)S(1)} all-to-all(bf16[128,16,128]{2,1,0:T(8,128)(2,1)S(1)} %get-tuple-element.26), channel_id=1, replica_groups={{180,2,4,6,8,10,12,14,16,18,20,22,24,26,28,30,32,34,36,38,40,42,44,46,4..., dimensions={0} | all-to-all | bytes 1048576 | tf_op jit(solution)/shard_map/all_to_all | solution.py:216
  39.0 1.6 %collective-permute-start.4 = (bf16[128,8,128]{2,1,0:T(8,128)(2,1)S(1)}, bf16[128,8,128]{2,1,0:T(8,128)(2,1)S(1)}, u32[]{:S(2)}, u32[]{:S(2)}) collective-permute-start(bf16[128,8,128]{2,1,0:T(8,128)(2,1)S(1)} %slice.4), channel_id=1, source_target_pairs={{0,1},{1,0},{2,3},{3,2},{4,5},{5,4},{6,7},{7,6},{8,9},{9,8},{10,11... | collective-permute-start | bytes 786440 | tf_op jit(solution)/shard_map/ppermute | solution.py:207
  40.6 0.4 gates.1
  41.0 0.1 collective-permute-start.5
  41.1 1.3 %collective-permute-done.5.given = bf16[4,128,128]{2,1,0:T(8,128)(2,1)S(1)} collective-permute-done((bf16[4,128,128]{2,1,0:T(8,128)(2,1)S(1)}, bf16[4,128,128]{2,1,0:T(8,128)(2,1)S(1)}, u32[]{:S(2)}, u32[]{:S(2)}) %collective-permute-start.5) | collective-permute-done | bytes 131104 | tf_op jit(solution)/shard_map/ppermute | solution.py:207
  42.4 0.0 collective-permute-done.4.other
  42.4 1.0 %products.1 = bf16[128,16,128]{2,1,0:T(8,128)(2,1)S(1)} custom-call(bf16[128,16,128]{2,1,0:T(8,128)(2,1)S(1)} %all_to_all.10.own, bf16[128,8,128]{2,1,0:T(8,128)(2,1)S(1)} %collective-permute-done.4.other, bf16[4,128,128]{2,1,0:T(8,128)(2,1)S(1)} %get-tuple-element.29.kept, bf16[4,128,128]{2,1,0:T(8,128)(2,1)S(1)} %collective-permute-done.5.given), custom_call_target="tpu_custom_call" | custom-call | bytes 1048576 | tf_op jit(solution)/shard_map/products/pallas_call | solution.py:277
  43.4 25.1 %all_to_all.11.got = bf16[128,16,128]{2,1,0:T(8,128)(2,1)S(1)} all-to-all(bf16[128,16,128]{2,1,0:T(8,128)(2,1)S(1)} %products.1), channel_id=1, replica_groups={{180,2,4,6,8,10,12,14,16,18,20,22,24,26,28,30,32,34,36,38,40,42,44,46,4..., dimensions={0} | all-to-all | bytes 1048576 | tf_op jit(solution)/shard_map/all_to_all | solution.py:216
  68.5 0.7 updates.1
  69.2 1.6 %collective-permute-start.6 = (bf16[2,32,512]{2,1,0:T(8,128)(2,1)S(1)}, bf16[2,32,512]{2,1,0:T(8,128)(2,1)S(1)}, u32[]{:S(2)}, u32[]{:S(2)}) collective-permute-start(bf16[2,32,512]{2,1,0:T(8,128)(2,1)S(1)} %get-tuple-element.32), channel_id=1, source_target_pairs={{0,1},{1,0},{2,3},{3,2},{4,5},{5,4},{6,7},{7,6},{8,9},{9,8},{10,11... | collective-permute-start | bytes 196616 | tf_op jit(solution)/shard_map/ppermute | solution.py:207
  70.8 0.9 %collective-permute-start.7 = (bf16[2,32,512]{2,1,0:T(8,128)(2,1)S(1)}, bf16[2,32,512]{2,1,0:T(8,128)(2,1)S(1)}, u32[]{:S(2)}, u32[]{:S(2)}) collective-permute-start(bf16[2,32,512]{2,1,0:T(8,128)(2,1)S(1)} %get-tuple-element.33), channel_id=1, source_target_pairs={{0,2},{1,3},{2,0},{3,1},{4,6},{5,7},{6,4},{7,5},{8,10},{9,11},{10,... | collective-permute-start | bytes 196616 | tf_op jit(solution)/shard_map/ppermute | solution.py:207
  71.7 0.8 %collective-permute-start.8 = (bf16[2,32,512]{2,1,0:T(8,128)(2,1)S(1)}, bf16[2,32,512]{2,1,0:T(8,128)(2,1)S(1)}, u32[]{:S(2)}, u32[]{:S(2)}) collective-permute-start(bf16[2,32,512]{2,1,0:T(8,128)(2,1)S(1)} %get-tuple-element.34), channel_id=1, source_target_pairs={{0,3},{1,2},{2,1},{3,0},{4,7},{5,6},{6,5},{7,4},{8,11},{9,10},{10,... | collective-permute-start | bytes 196616 | tf_op jit(solution)/shard_map/ppermute | solution.py:207
  72.5 0.0 collective-permute-done.6.in1
  72.5 1.9 %collective-permute-done.7.in2 = bf16[2,32,512]{2,1,0:T(8,128)(2,1)S(1)} collective-permute-done((bf16[2,32,512]{2,1,0:T(8,128)(2,1)S(1)}, bf16[2,32,512]{2,1,0:T(8,128)(2,1)S(1)}, u32[]{:S(2)}, u32[]{:S(2)}) %collective-permute-start.7) | collective-permute-done | bytes 65568 | tf_op jit(solution)/shard_map/ppermute | solution.py:207
  74.4 1.6 %collective-permute-done.8.in3 = bf16[2,32,512]{2,1,0:T(8,128)(2,1)S(1)} collective-permute-done((bf16[2,32,512]{2,1,0:T(8,128)(2,1)S(1)}, bf16[2,32,512]{2,1,0:T(8,128)(2,1)S(1)}, u32[]{:S(2)}, u32[]{:S(2)}) %collective-permute-start.8) | collective-permute-done | bytes 65568 | tf_op jit(solution)/shard_map/ppermute | solution.py:207
  76.0 0.8 %arrange.1 = bf16[32,8,512]{2,1,0:T(8,128)(2,1)} custom-call(bf16[2,32,512]{2,1,0:T(8,128)(2,1)S(1)} %get-tuple-element.31.in0, bf16[2,32,512]{2,1,0:T(8,128)(2,1)S(1)} %collective-permute-done.6.in1, bf16[2,32,512]{2,1,0:T(8,128)(2,1)S(1)} %collective-permute-done.7.in2, bf16[2,32,512]{2,1,0:T(8,128)(2,1)S(1)} %collective-permute-done.8.in3), custom_call_target="tpu_custom_call" | custom-call | bytes 1048576 | tf_op jit(solution)/shard_map/arrange/pallas_call | solution.py:299
  (1 shorter events, 0.0 us)
Async XLA Ops:
  1.2 9.8 %collective-permute-start = (bf16[112,512]{1,0:T(8,128)(2,1)S(1)}, bf16[112,512]{1,0:T(8,128)(2,1)S(1)}, u32[]{:S(2)}, u32[]{:S(2)}) collective-permute-start(bf16[112,512]{1,0:T(8,128)(2,1)S(1)} %get-tuple-element.21), channel_id=1, source_target_pairs={{0,1},{1,0},{2,3},{3,2},{4,5},{5,4},{6,7},{7,6},{8,9},{9,8},{10,11... | collective-permute-start | bytes 344072 | tf_op jit(solution)/shard_map/ppermute | solution.py:207
  4.6 6.5 %collective-permute-start.1 = (bf16[112,512]{1,0:T(8,128)(2,1)S(1)}, bf16[112,512]{1,0:T(8,128)(2,1)S(1)}, u32[]{:S(2)}, u32[]{:S(2)}) collective-permute-start(bf16[112,512]{1,0:T(8,128)(2,1)S(1)} %get-tuple-element.22), channel_id=1, source_target_pairs={{0,2},{1,3},{2,0},{3,1},{4,6},{5,7},{6,4},{7,5},{8,10},{9,11},{10,... | collective-permute-start | bytes 344072 | tf_op jit(solution)/shard_map/ppermute | solution.py:207
  4.6 6.5 %collective-permute-start.2 = (bf16[64,512]{1,0:T(8,128)(2,1)S(1)}, bf16[64,512]{1,0:T(8,128)(2,1)S(1)}, u32[]{:S(2)}, u32[]{:S(2)}) collective-permute-start(bf16[64,512]{1,0:T(8,128)(2,1)S(1)} %get-tuple-element.23), channel_id=1, source_target_pairs={{0,3},{1,2},{2,1},{3,0},{4,7},{5,6},{6,5},{7,4},{8,11},{9,10},{10,... | collective-permute-start | bytes 196616 | tf_op jit(solution)/shard_map/ppermute | solution.py:207
  6.3 4.7 %collective-permute-start.3 = (bf16[48,512]{1,0:T(8,128)(2,1)S(1)}, bf16[48,512]{1,0:T(8,128)(2,1)S(1)}, u32[]{:S(2)}, u32[]{:S(2)}) collective-permute-start(bf16[48,512]{1,0:T(8,128)(2,1)S(1)} %get-tuple-element.24), channel_id=1, source_target_pairs={{0,35},{1,34},{2,33},{3,32},{32,3},{33,2},{34,1},{35,0},{4,39},{5,... | collective-permute-start | bytes 147464 | tf_op jit(solution)/shard_map/ppermute | solution.py:212
  39.0 3.4 %collective-permute-start.4 = (bf16[128,8,128]{2,1,0:T(8,128)(2,1)S(1)}, bf16[128,8,128]{2,1,0:T(8,128)(2,1)S(1)}, u32[]{:S(2)}, u32[]{:S(2)}) collective-permute-start(bf16[128,8,128]{2,1,0:T(8,128)(2,1)S(1)} %slice.4), channel_id=1, source_target_pairs={{0,1},{1,0},{2,3},{3,2},{4,5},{5,4},{6,7},{7,6},{8,9},{9,8},{10,11... | collective-permute-start | bytes 786440 | tf_op jit(solution)/shard_map/ppermute | solution.py:207
  41.0 1.4 %collective-permute-start.5 = (bf16[4,128,128]{2,1,0:T(8,128)(2,1)S(1)}, bf16[4,128,128]{2,1,0:T(8,128)(2,1)S(1)}, u32[]{:S(2)}, u32[]{:S(2)}) collective-permute-start(bf16[4,128,128]{2,1,0:T(8,128)(2,1)S(1)} %get-tuple-element.30), channel_id=1, source_target_pairs={{0,1},{1,0},{2,3},{3,2},{4,5},{5,4},{6,7},{7,6},{8,9},{9,8},{10,11... | collective-permute-start | bytes 393224 | tf_op jit(solution)/shard_map/ppermute | solution.py:207
  69.2 3.3 %collective-permute-start.6 = (bf16[2,32,512]{2,1,0:T(8,128)(2,1)S(1)}, bf16[2,32,512]{2,1,0:T(8,128)(2,1)S(1)}, u32[]{:S(2)}, u32[]{:S(2)}) collective-permute-start(bf16[2,32,512]{2,1,0:T(8,128)(2,1)S(1)} %get-tuple-element.32), channel_id=1, source_target_pairs={{0,1},{1,0},{2,3},{3,2},{4,5},{5,4},{6,7},{7,6},{8,9},{9,8},{10,11... | collective-permute-start | bytes 196616 | tf_op jit(solution)/shard_map/ppermute | solution.py:207
  70.8 3.7 %collective-permute-start.7 = (bf16[2,32,512]{2,1,0:T(8,128)(2,1)S(1)}, bf16[2,32,512]{2,1,0:T(8,128)(2,1)S(1)}, u32[]{:S(2)}, u32[]{:S(2)}) collective-permute-start(bf16[2,32,512]{2,1,0:T(8,128)(2,1)S(1)} %get-tuple-element.33), channel_id=1, source_target_pairs={{0,2},{1,3},{2,0},{3,1},{4,6},{5,7},{6,4},{7,5},{8,10},{9,11},{10,... | collective-permute-start | bytes 196616 | tf_op jit(solution)/shard_map/ppermute | solution.py:207
  71.7 4.3 %collective-permute-start.8 = (bf16[2,32,512]{2,1,0:T(8,128)(2,1)S(1)}, bf16[2,32,512]{2,1,0:T(8,128)(2,1)S(1)}, u32[]{:S(2)}, u32[]{:S(2)}) collective-permute-start(bf16[2,32,512]{2,1,0:T(8,128)(2,1)S(1)} %get-tuple-element.34), channel_id=1, source_target_pairs={{0,3},{1,2},{2,1},{3,0},{4,7},{5,6},{6,5},{7,4},{8,11},{9,10},{10,... | collective-permute-start | bytes 196616 | tf_op jit(solution)/shard_map/ppermute | solution.py:207

commit v10 on v9

--- a/solution.py
+++ b/solution.py
@@ -7,7 +7,7 @@
 from jax.sharding import PartitionSpec as P
 
 epsilon = 1e-05
-far_chip = 90
+far_pair = 45
 bf16, f32 = jnp.bfloat16, jnp.float32
 vmem_bytes = 16 * 1024 * 1024
 
@@ -42,17 +42,25 @@
     return jnp.broadcast_to(row, (128, 128)).T
 
 
+def pair_order():
+    def distance(pair):
+        y, z = pair // 16, pair % 8
+        return min(z, 8 - z)
+
+    return [far_pair] + [pair for pair in sorted(range(64), key=distance) if pair != far_pair]
+
+
 def peers(core):
-    devices = list(range(core, 256, 2))
-    devices[0], devices[far_chip] = devices[far_chip], devices[0]
-    return devices
-
-
-def restore(rows):
-    first, far = slice(0, 4), slice(4 * far_chip, 4 * far_chip + 4)
-    kept = rows[first, :]
-    rows[first, :] = rows[far, :]
-    rows[far, :] = kept
+    return [4 * pair + 2 * xl + core for pair in pair_order() for xl in range(2)]
+
+
+def to_peers(rows):
+    return jnp.concatenate([rows[8 * pair : 8 * pair + 8, :] for pair in pair_order()], axis=0)
+
+
+def from_peers(rows):
+    places = [pair_order().index(pair) for pair in range(64)]
+    return jnp.concatenate([rows[8 * place : 8 * place + 8, :] for place in places], axis=0)
 
 
 def position():
@@ -130,7 +138,7 @@
     for ii in range(2):
         value = jax.nn.sigmoid(jnp.dot(late[:, 0:128], normed[ii], preferred_element_type=f32))
         rows[...] = value.T
-        restore(rows)
+        rows[...] = to_peers(rows)
         for jj in range(2):
             kept[2 * ii + jj] = rows[pl.ds(2 * core + jj, 128, stride=4), :].astype(bf16)
             given[2 * ii + jj] = rows[pl.ds(2 * (1 - core) + jj, 128, stride=4), :].astype(bf16)
@@ -149,12 +157,11 @@
             left[lane, pl.ds(2 * (1 - core) + ii, 128, stride=4), :] = other_rows[
                 pl.ds(4 * ii + lane, 128, stride=8), :
             ]
-        restore(left.at[lane])
         right = jnp.concatenate(
             [mine_rows[pl.ds(8 + 4 * jj + lane, 128, stride=16), :] for jj in range(2)], axis=0
         ).astype(bf16)
         part = lax.dot_general(
-            right, left[lane].astype(bf16), (((1,), (1,)), ((), ())), preferred_element_type=f32
+            right, from_peers(left.at[lane]).astype(bf16), (((1,), (1,)), ((), ())), preferred_element_type=f32
         )
         total = part if total is None else total + part
     for jj in range(2):
@@ -179,8 +186,7 @@
             gate_rows[pl.ds(ii, 128, stride=4), :] = rows[
                 pl.ds(8 + 4 * jj + ii, 128, stride=16), :
             ]
-        restore(gate_rows)
-        gating = gate_rows[...].T
+        gating = from_peers(gate_rows).T
         for lane in range(4):
             hidden = rows[pl.ds(4 * jj + lane, 128, stride=16), :]
             normed = layer_norm(hidden, gains, biases).astype(bf16)

time: 77 us -> 75.9 us (0.986)
  blocking collectives: 52.2 us -> 51.2 us
    all_to_all x2, blocking collectives: 52.2 us -> 51.2 us  [scatter(): lax.all_to_all(messages, ('y', 'xh', 'z', 'xl', 'core'), 0, 0, axis_index...]
  transfers between devices with their start and end apart: 9 -> 9, of which waited for: 4 -> 4; matrix products, arithmetic and copies ran while one was open for 0% -> 0% of each run, Pallas kernels for 0% -> 1%
where the time goes in v10:
time: 75.9 us; the launch traced here: 75.8 us
  blocking collectives  51.2 us (67%)
  starting transfers between devices  10.7 us (14%)
  waiting for transfers between devices  8.79 us (12%)
  Pallas kernels  4.96 us (7%)
    all_to_all x2, blocking collectives, scatter(): lax.all_to_all(messages, ('y', 'xh', 'z', 'xl', 'core'), 0, 0, axis_index...  51.2 us
    ppermute x8, starting transfers between devices, swap(): lax.ppermute(array, ('xl', 'core'), [(s, s ^ step) for s in range(4)])  9.91 us
    ppermute x8, waiting for transfers between devices, swap(): lax.ppermute(array, ('xl', 'core'), [(s, s ^ step) for s in range(4)])  4.85 us
    ppermute x1, waiting for transfers between devices, around(): return lax.ppermute(array, ('xh', 'xl', 'core'), pairs)  3.94 us
  transfers between devices with their start and end apart: 9, of which 4 were waited for; matrix products, arithmetic and copies ran while one was open for 0% of the time, Pallas kernels for 1%

profile of v10, /device:TPU:1, one launch (start us, length us, event | category | flops | bytes accessed | tf_op | source)
XLA Modules:
  0.0 75.8 jit_solution(11637122313559708068)
XLA Ops:
  0.0 1.2 %lay_out.1 = (bf16[112,512]{1,0:T(8,128)(2,1)S(1)}, bf16[112,512]{1,0:T(8,128)(2,1)S(1)}, bf16[112,512]{1,0:T(8,128)(2,1)S(1)}, bf16[64,512]{1,0:T(8,128)(2,1)S(...) custom-call(bf16[32,8,512]{2,1,0:T(8,128)(2,1)} %refs_0_.1, bf16[32,128]{1,0:T(8,128)(2,1)} %bitcast.10, ...), custom_call_target="tpu_custom_call" | custom-call | bytes 1048576 | tf_op jit(solution)/shard_map/lay_out/pallas_call | solution.py:251
  1.2 3.3 %collective-permute-start = (bf16[112,512]{1,0:T(8,128)(2,1)S(1)}, bf16[112,512]{1,0:T(8,128)(2,1)S(1)}, u32[]{:S(2)}, u32[]{:S(2)}) collective-permute-start(bf16[112,512]{1,0:T(8,128)(2,1)S(1)} %get-tuple-element.21), channel_id=1, source_target_pairs={{0,1},{1,0},{2,3},{3,2},{4,5},{5,4},{6,7},{7,6},{8,9},{9,8},{10,11... | collective-permute-start | bytes 344072 | tf_op jit(solution)/shard_map/ppermute | solution.py:213
  4.6 0.0 collective-permute-start.1
  4.6 1.7 %collective-permute-start.2 = (bf16[64,512]{1,0:T(8,128)(2,1)S(1)}, bf16[64,512]{1,0:T(8,128)(2,1)S(1)}, u32[]{:S(2)}, u32[]{:S(2)}) collective-permute-start(bf16[64,512]{1,0:T(8,128)(2,1)S(1)} %get-tuple-element.23), channel_id=1, source_target_pairs={{0,3},{1,2},{2,1},{3,0},{4,7},{5,6},{6,5},{7,4},{8,11},{9,10},{10,... | collective-permute-start | bytes 196616 | tf_op jit(solution)/shard_map/ppermute | solution.py:213
  6.3 0.8 %collective-permute-start.3 = (bf16[48,512]{1,0:T(8,128)(2,1)S(1)}, bf16[48,512]{1,0:T(8,128)(2,1)S(1)}, u32[]{:S(2)}, u32[]{:S(2)}) collective-permute-start(bf16[48,512]{1,0:T(8,128)(2,1)S(1)} %get-tuple-element.24), channel_id=1, source_target_pairs={{0,35},{1,34},{2,33},{3,32},{32,3},{33,2},{34,1},{35,0},{4,39},{5,... | collective-permute-start | bytes 147464 | tf_op jit(solution)/shard_map/ppermute | solution.py:218
  7.1 3.9 %collective-permute-done.3.shared3 = bf16[48,512]{1,0:T(8,128)(2,1)S(1)} collective-permute-done((bf16[48,512]{1,0:T(8,128)(2,1)S(1)}, bf16[48,512]{1,0:T(8,128)(2,1)S(1)}, u32[]{:S(2)}, u32[]{:S(2)}) %collective-permute-start.3) | collective-permute-done | bytes 49184 | tf_op jit(solution)/shard_map/ppermute | solution.py:218
  11.0 0.0 collective-permute-done.2.in3
  11.0 0.0 collective-permute-done.in1
  11.0 0.0 collective-permute-done.1.in2
  11.0 0.8 %factors.1 = (bf16[128,16,128]{2,1,0:T(8,128)(2,1)S(1)}, bf16[2,128,512]{2,1,0:T(8,128)(2,1)S(1)}, bf16[128,256]{1,0:T(8,128)(2,1)S(1)}) custom-call(bf16[112,512]{1,0:T(8,128)(2,1)S(1)} %get-tuple-element.20.in0, bf16[112,512]{1,0:T(8,128)(2,1)S(1)} %collective-permute-done.in1, bf16[112,512]{1,0:T(8,128)(2,1)S(1)} %collective-permute-done.1.in2, ...), custom_call_target="tpu_custom_call" | custom-call | bytes 1048576 | tf_op jit(solution)/shard_map/factors/pallas_call | solution.py:265
  11.8 26.7 %all_to_all.10.own = bf16[128,16,128]{2,1,0:T(8,128)(2,1)S(1)} all-to-all(bf16[128,16,128]{2,1,0:T(8,128)(2,1)S(1)} %get-tuple-element.26), channel_id=1, replica_groups={{180,182,0,2,32,34,64,66,96,98,128,130,160,162,192,194,224,226,4,6,28,3..., dimensions={0} | all-to-all | bytes 1048576 | tf_op jit(solution)/shard_map/all_to_all | solution.py:222
  38.5 1.5 %collective-permute-start.4 = (bf16[128,8,128]{2,1,0:T(8,128)(2,1)S(1)}, bf16[128,8,128]{2,1,0:T(8,128)(2,1)S(1)}, u32[]{:S(2)}, u32[]{:S(2)}) collective-permute-start(bf16[128,8,128]{2,1,0:T(8,128)(2,1)S(1)} %slice.4), channel_id=1, source_target_pairs={{0,1},{1,0},{2,3},{3,2},{4,5},{5,4},{6,7},{7,6},{8,9},{9,8},{10,11... | collective-permute-start | bytes 786440 | tf_op jit(solution)/shard_map/ppermute | solution.py:213
  40.0 0.4 gates.1
  40.4 0.1 collective-permute-start.5
  40.5 1.3 %collective-permute-done.5.given = bf16[4,128,128]{2,1,0:T(8,128)(2,1)S(1)} collective-permute-done((bf16[4,128,128]{2,1,0:T(8,128)(2,1)S(1)}, bf16[4,128,128]{2,1,0:T(8,128)(2,1)S(1)}, u32[]{:S(2)}, u32[]{:S(2)}) %collective-permute-start.5) | collective-permute-done | bytes 131104 | tf_op jit(solution)/shard_map/ppermute | solution.py:213
  41.8 0.0 collective-permute-done.4.other
  41.8 1.0 %products.1 = bf16[128,16,128]{2,1,0:T(8,128)(2,1)S(1)} custom-call(bf16[128,16,128]{2,1,0:T(8,128)(2,1)S(1)} %all_to_all.10.own, bf16[128,8,128]{2,1,0:T(8,128)(2,1)S(1)} %collective-permute-done.4.other, bf16[4,128,128]{2,1,0:T(8,128)(2,1)S(1)} %get-tuple-element.29.kept, bf16[4,128,128]{2,1,0:T(8,128)(2,1)S(1)} %collective-permute-done.5.given), custom_call_target="tpu_custom_call" | custom-call | bytes 1048576 | tf_op jit(solution)/shard_map/products/pallas_call | solution.py:283
  42.9 24.6 %all_to_all.11.got = bf16[128,16,128]{2,1,0:T(8,128)(2,1)S(1)} all-to-all(bf16[128,16,128]{2,1,0:T(8,128)(2,1)S(1)} %products.1), channel_id=1, replica_groups={{180,182,0,2,32,34,64,66,96,98,128,130,160,162,192,194,224,226,4,6,28,3..., dimensions={0} | all-to-all | bytes 1048576 | tf_op jit(solution)/shard_map/all_to_all | solution.py:222
  67.5 0.7 updates.1
  68.2 1.5 %collective-permute-start.6 = (bf16[2,32,512]{2,1,0:T(8,128)(2,1)S(1)}, bf16[2,32,512]{2,1,0:T(8,128)(2,1)S(1)}, u32[]{:S(2)}, u32[]{:S(2)}) collective-permute-start(bf16[2,32,512]{2,1,0:T(8,128)(2,1)S(1)} %get-tuple-element.32), channel_id=1, source_target_pairs={{0,1},{1,0},{2,3},{3,2},{4,5},{5,4},{6,7},{7,6},{8,9},{9,8},{10,11... | collective-permute-start | bytes 196616 | tf_op jit(solution)/shard_map/ppermute | solution.py:213
  69.7 0.6 collective-permute-start.7
  70.3 1.1 %collective-permute-start.8 = (bf16[2,32,512]{2,1,0:T(8,128)(2,1)S(1)}, bf16[2,32,512]{2,1,0:T(8,128)(2,1)S(1)}, u32[]{:S(2)}, u32[]{:S(2)}) collective-permute-start(bf16[2,32,512]{2,1,0:T(8,128)(2,1)S(1)} %get-tuple-element.34), channel_id=1, source_target_pairs={{0,3},{1,2},{2,1},{3,0},{4,7},{5,6},{6,5},{7,4},{8,11},{9,10},{10,... | collective-permute-start | bytes 196616 | tf_op jit(solution)/shard_map/ppermute | solution.py:213
  71.4 0.0 collective-permute-done.6.in1
  71.4 1.9 %collective-permute-done.7.in2 = bf16[2,32,512]{2,1,0:T(8,128)(2,1)S(1)} collective-permute-done((bf16[2,32,512]{2,1,0:T(8,128)(2,1)S(1)}, bf16[2,32,512]{2,1,0:T(8,128)(2,1)S(1)}, u32[]{:S(2)}, u32[]{:S(2)}) %collective-permute-start.7) | collective-permute-done | bytes 65568 | tf_op jit(solution)/shard_map/ppermute | solution.py:213
  73.4 1.6 %collective-permute-done.8.in3 = bf16[2,32,512]{2,1,0:T(8,128)(2,1)S(1)} collective-permute-done((bf16[2,32,512]{2,1,0:T(8,128)(2,1)S(1)}, bf16[2,32,512]{2,1,0:T(8,128)(2,1)S(1)}, u32[]{:S(2)}, u32[]{:S(2)}) %collective-permute-start.8) | collective-permute-done | bytes 65568 | tf_op jit(solution)/shard_map/ppermute | solution.py:213
  74.9 0.8 %arrange.1 = bf16[32,8,512]{2,1,0:T(8,128)(2,1)} custom-call(bf16[2,32,512]{2,1,0:T(8,128)(2,1)S(1)} %get-tuple-element.31.in0, bf16[2,32,512]{2,1,0:T(8,128)(2,1)S(1)} %collective-permute-done.6.in1, bf16[2,32,512]{2,1,0:T(8,128)(2,1)S(1)} %collective-permute-done.7.in2, bf16[2,32,512]{2,1,0:T(8,128)(2,1)S(1)} %collective-permute-done.8.in3), custom_call_target="tpu_custom_call" | custom-call | bytes 1048576 | tf_op jit(solution)/shard_map/arrange/pallas_call | solution.py:305
  (1 shorter events, 0.0 us)
Async XLA Ops:
  1.2 9.8 %collective-permute-start = (bf16[112,512]{1,0:T(8,128)(2,1)S(1)}, bf16[112,512]{1,0:T(8,128)(2,1)S(1)}, u32[]{:S(2)}, u32[]{:S(2)}) collective-permute-start(bf16[112,512]{1,0:T(8,128)(2,1)S(1)} %get-tuple-element.21), channel_id=1, source_target_pairs={{0,1},{1,0},{2,3},{3,2},{4,5},{5,4},{6,7},{7,6},{8,9},{9,8},{10,11... | collective-permute-start | bytes 344072 | tf_op jit(solution)/shard_map/ppermute | solution.py:213
  4.6 6.5 %collective-permute-start.1 = (bf16[112,512]{1,0:T(8,128)(2,1)S(1)}, bf16[112,512]{1,0:T(8,128)(2,1)S(1)}, u32[]{:S(2)}, u32[]{:S(2)}) collective-permute-start(bf16[112,512]{1,0:T(8,128)(2,1)S(1)} %get-tuple-element.22), channel_id=1, source_target_pairs={{0,2},{1,3},{2,0},{3,1},{4,6},{5,7},{6,4},{7,5},{8,10},{9,11},{10,... | collective-permute-start | bytes 344072 | tf_op jit(solution)/shard_map/ppermute | solution.py:213
  4.6 6.5 %collective-permute-start.2 = (bf16[64,512]{1,0:T(8,128)(2,1)S(1)}, bf16[64,512]{1,0:T(8,128)(2,1)S(1)}, u32[]{:S(2)}, u32[]{:S(2)}) collective-permute-start(bf16[64,512]{1,0:T(8,128)(2,1)S(1)} %get-tuple-element.23), channel_id=1, source_target_pairs={{0,3},{1,2},{2,1},{3,0},{4,7},{5,6},{6,5},{7,4},{8,11},{9,10},{10,... | collective-permute-start | bytes 196616 | tf_op jit(solution)/shard_map/ppermute | solution.py:213
  6.3 4.7 %collective-permute-start.3 = (bf16[48,512]{1,0:T(8,128)(2,1)S(1)}, bf16[48,512]{1,0:T(8,128)(2,1)S(1)}, u32[]{:S(2)}, u32[]{:S(2)}) collective-permute-start(bf16[48,512]{1,0:T(8,128)(2,1)S(1)} %get-tuple-element.24), channel_id=1, source_target_pairs={{0,35},{1,34},{2,33},{3,32},{32,3},{33,2},{34,1},{35,0},{4,39},{5,... | collective-permute-start | bytes 147464 | tf_op jit(solution)/shard_map/ppermute | solution.py:218
  38.5 3.3 %collective-permute-start.4 = (bf16[128,8,128]{2,1,0:T(8,128)(2,1)S(1)}, bf16[128,8,128]{2,1,0:T(8,128)(2,1)S(1)}, u32[]{:S(2)}, u32[]{:S(2)}) collective-permute-start(bf16[128,8,128]{2,1,0:T(8,128)(2,1)S(1)} %slice.4), channel_id=1, source_target_pairs={{0,1},{1,0},{2,3},{3,2},{4,5},{5,4},{6,7},{7,6},{8,9},{9,8},{10,11... | collective-permute-start | bytes 786440 | tf_op jit(solution)/shard_map/ppermute | solution.py:213
  40.4 1.4 %collective-permute-start.5 = (bf16[4,128,128]{2,1,0:T(8,128)(2,1)S(1)}, bf16[4,128,128]{2,1,0:T(8,128)(2,1)S(1)}, u32[]{:S(2)}, u32[]{:S(2)}) collective-permute-start(bf16[4,128,128]{2,1,0:T(8,128)(2,1)S(1)} %get-tuple-element.30), channel_id=1, source_target_pairs={{0,1},{1,0},{2,3},{3,2},{4,5},{5,4},{6,7},{7,6},{8,9},{9,8},{10,11... | collective-permute-start | bytes 393224 | tf_op jit(solution)/shard_map/ppermute | solution.py:213
  68.2 3.2 %collective-permute-start.6 = (bf16[2,32,512]{2,1,0:T(8,128)(2,1)S(1)}, bf16[2,32,512]{2,1,0:T(8,128)(2,1)S(1)}, u32[]{:S(2)}, u32[]{:S(2)}) collective-permute-start(bf16[2,32,512]{2,1,0:T(8,128)(2,1)S(1)} %get-tuple-element.32), channel_id=1, source_target_pairs={{0,1},{1,0},{2,3},{3,2},{4,5},{5,4},{6,7},{7,6},{8,9},{9,8},{10,11... | collective-permute-start | bytes 196616 | tf_op jit(solution)/shard_map/ppermute | solution.py:213
  69.7 3.7 %collective-permute-start.7 = (bf16[2,32,512]{2,1,0:T(8,128)(2,1)S(1)}, bf16[2,32,512]{2,1,0:T(8,128)(2,1)S(1)}, u32[]{:S(2)}, u32[]{:S(2)}) collective-permute-start(bf16[2,32,512]{2,1,0:T(8,128)(2,1)S(1)} %get-tuple-element.33), channel_id=1, source_target_pairs={{0,2},{1,3},{2,0},{3,1},{4,6},{5,7},{6,4},{7,5},{8,10},{9,11},{10,... | collective-permute-start | bytes 196616 | tf_op jit(solution)/shard_map/ppermute | solution.py:213
  70.3 4.6 %collective-permute-start.8 = (bf16[2,32,512]{2,1,0:T(8,128)(2,1)S(1)}, bf16[2,32,512]{2,1,0:T(8,128)(2,1)S(1)}, u32[]{:S(2)}, u32[]{:S(2)}) collective-permute-start(bf16[2,32,512]{2,1,0:T(8,128)(2,1)S(1)} %get-tuple-element.34), channel_id=1, source_target_pairs={{0,3},{1,2},{2,1},{3,0},{4,7},{5,6},{6,5},{7,4},{8,11},{9,10},{10,... | collective-permute-start | bytes 196616 | tf_op jit(solution)/shard_map/ppermute | solution.py:213

commit v11 on v10

--- a/solution.py
+++ b/solution.py
@@ -144,26 +144,37 @@
             given[2 * ii + jj] = rows[pl.ds(2 * (1 - core) + jj, 128, stride=4), :].astype(bf16)
 
 
-def products(own, other, kept, given, out, mine_rows, other_rows, left, rows):
+def prepare(own, left, right, received):
     core = lax.axis_index("core")
-    mine_rows[...] = own[...].astype(f32).reshape(2048, 128)
-    other_rows[...] = other[...].astype(f32).reshape(1024, 128)
-    total = None
+    received[...] = own[...].astype(f32).reshape(2048, 128)
     for lane in range(4):
         for ii in range(2):
-            left[lane, pl.ds(2 * core + ii, 128, stride=4), :] = mine_rows[
+            left[lane, pl.ds(2 * core + ii, 128, stride=4), :] = received[
                 pl.ds(4 * ii + lane, 128, stride=16), :
             ]
-            left[lane, pl.ds(2 * (1 - core) + ii, 128, stride=4), :] = other_rows[
+            right[128 * ii : 128 * (ii + 1), 128 * lane : 128 * (lane + 1)] = received[
+                pl.ds(8 + 4 * ii + lane, 128, stride=16), :
+            ].astype(bf16)
+
+
+def products(own_left, right, other, kept, given, out, received, left, rows):
+    core = lax.axis_index("core")
+    mine = lax.broadcasted_iota(jnp.int32, (512, 128), 0) // 2 % 2 == core
+    received[...] = other[...].astype(f32).reshape(1024, 128)
+    whole = []
+    for lane in range(4):
+        for ii in range(2):
+            left[pl.ds(2 * (1 - core) + ii, 128, stride=4), :] = received[
                 pl.ds(4 * ii + lane, 128, stride=8), :
             ]
-        right = jnp.concatenate(
-            [mine_rows[pl.ds(8 + 4 * jj + lane, 128, stride=16), :] for jj in range(2)], axis=0
-        ).astype(bf16)
-        part = lax.dot_general(
-            right, from_peers(left.at[lane]).astype(bf16), (((1,), (1,)), ((), ())), preferred_element_type=f32
-        )
-        total = part if total is None else total + part
+        left[...] = jnp.where(mine, own_left[lane], left[...])
+        whole.append(from_peers(left).astype(bf16))
+    total = lax.dot_general(
+        right[...],
+        jnp.concatenate(whole, axis=1),
+        (((1,), (1,)), ((), ())),
+        preferred_element_type=f32,
+    )
     for jj in range(2):
         for lane in range(4):
             rows[pl.ds(4 * jj + lane, 128, stride=16), :] = total[
@@ -280,17 +291,23 @@
         [pltpu.VMEM((512, 128), f32)],
         flops=1 << 30,
     )(normed, late)
+    left, right = call(
+        prepare,
+        "prepare",
+        (jax.ShapeDtypeStruct((4, 512, 128), f32), shape(256, 512)),
+        [pltpu.VMEM((2048, 128), f32)],
+        flops=1 << 30,
+    )(own)
     sent = call(
         products,
         "products",
         shape(128, 16, 128),
         [
-            pltpu.VMEM((2048, 128), f32),
             pltpu.VMEM((1024, 128), f32),
-            pltpu.VMEM((4, 512, 128), f32),
+            pltpu.VMEM((512, 128), f32),
             pltpu.VMEM((2048, 128), f32),
         ],
-    )(own, swap(own[:, :8], 1), kept, swap(given, 1))
+    )(left, right, swap(own[:, :8], 1), kept, swap(given, 1))
     got = scatter(sent)
     parts = call(
         updates,

time: 75.9 us -> 75.7 us (level)
  no operation moved by 1% of the time
where the time goes in v11:
time: 75.7 us; the launch traced here: 75.5 us
  blocking collectives  51.2 us (68%)
  starting transfers between devices  10.7 us (14%)
  waiting for transfers between devices  8.37 us (11%)
  Pallas kernels  5.13 us (7%)
    all_to_all x2, blocking collectives, scatter(): lax.all_to_all(messages, ('y', 'xh', 'z', 'xl', 'core'), 0, 0, axis_index...  51.2 us
    ppermute x8, starting transfers between devices, swap(): lax.ppermute(array, ('xl', 'core'), [(s, s ^ step) for s in range(4)])  9.91 us
    ppermute x8, waiting for transfers between devices, swap(): lax.ppermute(array, ('xl', 'core'), [(s, s ^ step) for s in range(4)])  4.43 us
    ppermute x1, waiting for transfers between devices, around(): return lax.ppermute(array, ('xh', 'xl', 'core'), pairs)  3.94 us
  transfers between devices with their start and end apart: 9, of which 4 were waited for; matrix products, arithmetic and copies ran while one was open for 0% of the time, Pallas kernels for 1%

profile of v11, /device:TPU:1, one launch (start us, length us, event | category | flops | bytes accessed | tf_op | source)
XLA Modules:
  0.0 75.5 jit_solution(10069852922265371711)
XLA Ops:
  0.0 1.2 %lay_out.1 = (bf16[112,512]{1,0:T(8,128)(2,1)S(1)}, bf16[112,512]{1,0:T(8,128)(2,1)S(1)}, bf16[112,512]{1,0:T(8,128)(2,1)S(1)}, bf16[64,512]{1,0:T(8,128)(2,1)S(...) custom-call(bf16[32,8,512]{2,1,0:T(8,128)(2,1)} %refs_0_.1, bf16[32,128]{1,0:T(8,128)(2,1)} %bitcast.10, ...), custom_call_target="tpu_custom_call" | custom-call | bytes 1048576 | tf_op jit(solution)/shard_map/lay_out/pallas_call | solution.py:262
  1.2 3.3 %collective-permute-start = (bf16[112,512]{1,0:T(8,128)(2,1)S(1)}, bf16[112,512]{1,0:T(8,128)(2,1)S(1)}, u32[]{:S(2)}, u32[]{:S(2)}) collective-permute-start(bf16[112,512]{1,0:T(8,128)(2,1)S(1)} %get-tuple-element.23), channel_id=1, source_target_pairs={{0,1},{1,0},{2,3},{3,2},{4,5},{5,4},{6,7},{7,6},{8,9},{9,8},{10,11... | collective-permute-start | bytes 344072 | tf_op jit(solution)/shard_map/ppermute | solution.py:224
  4.6 0.0 collective-permute-start.1
  4.6 1.7 %collective-permute-start.2 = (bf16[64,512]{1,0:T(8,128)(2,1)S(1)}, bf16[64,512]{1,0:T(8,128)(2,1)S(1)}, u32[]{:S(2)}, u32[]{:S(2)}) collective-permute-start(bf16[64,512]{1,0:T(8,128)(2,1)S(1)} %get-tuple-element.25), channel_id=1, source_target_pairs={{0,3},{1,2},{2,1},{3,0},{4,7},{5,6},{6,5},{7,4},{8,11},{9,10},{10,... | collective-permute-start | bytes 196616 | tf_op jit(solution)/shard_map/ppermute | solution.py:224
  6.3 0.8 %collective-permute-start.3 = (bf16[48,512]{1,0:T(8,128)(2,1)S(1)}, bf16[48,512]{1,0:T(8,128)(2,1)S(1)}, u32[]{:S(2)}, u32[]{:S(2)}) collective-permute-start(bf16[48,512]{1,0:T(8,128)(2,1)S(1)} %get-tuple-element.26), channel_id=1, source_target_pairs={{0,35},{1,34},{2,33},{3,32},{32,3},{33,2},{34,1},{35,0},{4,39},{5,... | collective-permute-start | bytes 147464 | tf_op jit(solution)/shard_map/ppermute | solution.py:229
  7.1 3.9 %collective-permute-done.3.shared3 = bf16[48,512]{1,0:T(8,128)(2,1)S(1)} collective-permute-done((bf16[48,512]{1,0:T(8,128)(2,1)S(1)}, bf16[48,512]{1,0:T(8,128)(2,1)S(1)}, u32[]{:S(2)}, u32[]{:S(2)}) %collective-permute-start.3) | collective-permute-done | bytes 49184 | tf_op jit(solution)/shard_map/ppermute | solution.py:229
  11.0 0.0 collective-permute-done.2.in3
  11.0 0.0 collective-permute-done.in1
  11.0 0.0 collective-permute-done.1.in2
  11.0 0.8 %factors.1 = (bf16[128,16,128]{2,1,0:T(8,128)(2,1)S(1)}, bf16[2,128,512]{2,1,0:T(8,128)(2,1)S(1)}, bf16[128,256]{1,0:T(8,128)(2,1)S(1)}) custom-call(bf16[112,512]{1,0:T(8,128)(2,1)S(1)} %get-tuple-element.22.in0, bf16[112,512]{1,0:T(8,128)(2,1)S(1)} %collective-permute-done.in1, bf16[112,512]{1,0:T(8,128)(2,1)S(1)} %collective-permute-done.1.in2, ...), custom_call_target="tpu_custom_call" | custom-call | bytes 1048576 | tf_op jit(solution)/shard_map/factors/pallas_call | solution.py:276
  11.8 26.7 %all_to_all.10.own = bf16[128,16,128]{2,1,0:T(8,128)(2,1)S(1)} all-to-all(bf16[128,16,128]{2,1,0:T(8,128)(2,1)S(1)} %get-tuple-element.28), channel_id=1, replica_groups={{180,182,0,2,32,34,64,66,96,98,128,130,160,162,192,194,224,226,4,6,28,3..., dimensions={0} | all-to-all | bytes 1048576 | tf_op jit(solution)/shard_map/all_to_all | solution.py:233
  38.5 1.5 %collective-permute-start.4 = (bf16[128,8,128]{2,1,0:T(8,128)(2,1)S(1)}, bf16[128,8,128]{2,1,0:T(8,128)(2,1)S(1)}, u32[]{:S(2)}, u32[]{:S(2)}) collective-permute-start(bf16[128,8,128]{2,1,0:T(8,128)(2,1)S(1)} %slice.4), channel_id=1, source_target_pairs={{0,1},{1,0},{2,3},{3,2},{4,5},{5,4},{6,7},{7,6},{8,9},{9,8},{10,11... | collective-permute-start | bytes 786440 | tf_op jit(solution)/shard_map/ppermute | solution.py:224
  40.0 0.4 gates.1
  40.4 0.1 collective-permute-start.5
  40.5 0.4 prepare.1
  40.9 0.9 %collective-permute-done.5.given = bf16[4,128,128]{2,1,0:T(8,128)(2,1)S(1)} collective-permute-done((bf16[4,128,128]{2,1,0:T(8,128)(2,1)S(1)}, bf16[4,128,128]{2,1,0:T(8,128)(2,1)S(1)}, u32[]{:S(2)}, u32[]{:S(2)}) %collective-permute-start.5) | collective-permute-done | bytes 131104 | tf_op jit(solution)/shard_map/ppermute | solution.py:224
  41.8 0.0 collective-permute-done.4.other
  41.8 0.8 %products.1 = bf16[128,16,128]{2,1,0:T(8,128)(2,1)S(1)} custom-call(f32[4,512,128]{2,1,0:T(8,128)S(1)} %get-tuple-element.29.own_left, bf16[256,512]{1,0:T(8,128)(2,1)S(1)} %get-tuple-element.30.right, bf16[128,8,128]{2,1,0:T(8,128)(2,1)S(1)} %collective-permute-done.4.other, bf16[4,128,128]{2,1,0:T(8,128)(2,1)S(1)} %get-tuple-element.33.kept, ...), custom_call_target="tpu_custom_call" | custom-call | bytes 1048576 | tf_op jit(solution)/shard_map/products/pallas_call | solution.py:301
  42.6 24.6 %all_to_all.11.got = bf16[128,16,128]{2,1,0:T(8,128)(2,1)S(1)} all-to-all(bf16[128,16,128]{2,1,0:T(8,128)(2,1)S(1)} %products.1), channel_id=1, replica_groups={{180,182,0,2,32,34,64,66,96,98,128,130,160,162,192,194,224,226,4,6,28,3..., dimensions={0} | all-to-all | bytes 1048576 | tf_op jit(solution)/shard_map/all_to_all | solution.py:233
  67.2 0.7 updates.1
  67.9 1.5 %collective-permute-start.6 = (bf16[2,32,512]{2,1,0:T(8,128)(2,1)S(1)}, bf16[2,32,512]{2,1,0:T(8,128)(2,1)S(1)}, u32[]{:S(2)}, u32[]{:S(2)}) collective-permute-start(bf16[2,32,512]{2,1,0:T(8,128)(2,1)S(1)} %get-tuple-element.36), channel_id=1, source_target_pairs={{0,1},{1,0},{2,3},{3,2},{4,5},{5,4},{6,7},{7,6},{8,9},{9,8},{10,11... | collective-permute-start | bytes 196616 | tf_op jit(solution)/shard_map/ppermute | solution.py:224
  69.4 0.6 collective-permute-start.7
  70.1 1.1 %collective-permute-start.8 = (bf16[2,32,512]{2,1,0:T(8,128)(2,1)S(1)}, bf16[2,32,512]{2,1,0:T(8,128)(2,1)S(1)}, u32[]{:S(2)}, u32[]{:S(2)}) collective-permute-start(bf16[2,32,512]{2,1,0:T(8,128)(2,1)S(1)} %get-tuple-element.38), channel_id=1, source_target_pairs={{0,3},{1,2},{2,1},{3,0},{4,7},{5,6},{6,5},{7,4},{8,11},{9,10},{10,... | collective-permute-start | bytes 196616 | tf_op jit(solution)/shard_map/ppermute | solution.py:224
  71.2 0.0 collective-permute-done.6.in1
  71.2 1.9 %collective-permute-done.7.in2 = bf16[2,32,512]{2,1,0:T(8,128)(2,1)S(1)} collective-permute-done((bf16[2,32,512]{2,1,0:T(8,128)(2,1)S(1)}, bf16[2,32,512]{2,1,0:T(8,128)(2,1)S(1)}, u32[]{:S(2)}, u32[]{:S(2)}) %collective-permute-start.7) | collective-permute-done | bytes 65568 | tf_op jit(solution)/shard_map/ppermute | solution.py:224
  73.1 1.6 %collective-permute-done.8.in3 = bf16[2,32,512]{2,1,0:T(8,128)(2,1)S(1)} collective-permute-done((bf16[2,32,512]{2,1,0:T(8,128)(2,1)S(1)}, bf16[2,32,512]{2,1,0:T(8,128)(2,1)S(1)}, u32[]{:S(2)}, u32[]{:S(2)}) %collective-permute-start.8) | collective-permute-done | bytes 65568 | tf_op jit(solution)/shard_map/ppermute | solution.py:224
  74.7 0.8 %arrange.1 = bf16[32,8,512]{2,1,0:T(8,128)(2,1)} custom-call(bf16[2,32,512]{2,1,0:T(8,128)(2,1)S(1)} %get-tuple-element.35.in0, bf16[2,32,512]{2,1,0:T(8,128)(2,1)S(1)} %collective-permute-done.6.in1, bf16[2,32,512]{2,1,0:T(8,128)(2,1)S(1)} %collective-permute-done.7.in2, bf16[2,32,512]{2,1,0:T(8,128)(2,1)S(1)} %collective-permute-done.8.in3), custom_call_target="tpu_custom_call" | custom-call | bytes 1048576 | tf_op jit(solution)/shard_map/arrange/pallas_call | solution.py:322
  (1 shorter events, 0.0 us)
Async XLA Ops:
  1.2 9.8 %collective-permute-start = (bf16[112,512]{1,0:T(8,128)(2,1)S(1)}, bf16[112,512]{1,0:T(8,128)(2,1)S(1)}, u32[]{:S(2)}, u32[]{:S(2)}) collective-permute-start(bf16[112,512]{1,0:T(8,128)(2,1)S(1)} %get-tuple-element.23), channel_id=1, source_target_pairs={{0,1},{1,0},{2,3},{3,2},{4,5},{5,4},{6,7},{7,6},{8,9},{9,8},{10,11... | collective-permute-start | bytes 344072 | tf_op jit(solution)/shard_map/ppermute | solution.py:224
  4.6 6.5 %collective-permute-start.1 = (bf16[112,512]{1,0:T(8,128)(2,1)S(1)}, bf16[112,512]{1,0:T(8,128)(2,1)S(1)}, u32[]{:S(2)}, u32[]{:S(2)}) collective-permute-start(bf16[112,512]{1,0:T(8,128)(2,1)S(1)} %get-tuple-element.24), channel_id=1, source_target_pairs={{0,2},{1,3},{2,0},{3,1},{4,6},{5,7},{6,4},{7,5},{8,10},{9,11},{10,... | collective-permute-start | bytes 344072 | tf_op jit(solution)/shard_map/ppermute | solution.py:224
  4.6 6.5 %collective-permute-start.2 = (bf16[64,512]{1,0:T(8,128)(2,1)S(1)}, bf16[64,512]{1,0:T(8,128)(2,1)S(1)}, u32[]{:S(2)}, u32[]{:S(2)}) collective-permute-start(bf16[64,512]{1,0:T(8,128)(2,1)S(1)} %get-tuple-element.25), channel_id=1, source_target_pairs={{0,3},{1,2},{2,1},{3,0},{4,7},{5,6},{6,5},{7,4},{8,11},{9,10},{10,... | collective-permute-start | bytes 196616 | tf_op jit(solution)/shard_map/ppermute | solution.py:224
  6.3 4.7 %collective-permute-start.3 = (bf16[48,512]{1,0:T(8,128)(2,1)S(1)}, bf16[48,512]{1,0:T(8,128)(2,1)S(1)}, u32[]{:S(2)}, u32[]{:S(2)}) collective-permute-start(bf16[48,512]{1,0:T(8,128)(2,1)S(1)} %get-tuple-element.26), channel_id=1, source_target_pairs={{0,35},{1,34},{2,33},{3,32},{32,3},{33,2},{34,1},{35,0},{4,39},{5,... | collective-permute-start | bytes 147464 | tf_op jit(solution)/shard_map/ppermute | solution.py:229
  38.5 3.3 %collective-permute-start.4 = (bf16[128,8,128]{2,1,0:T(8,128)(2,1)S(1)}, bf16[128,8,128]{2,1,0:T(8,128)(2,1)S(1)}, u32[]{:S(2)}, u32[]{:S(2)}) collective-permute-start(bf16[128,8,128]{2,1,0:T(8,128)(2,1)S(1)} %slice.4), channel_id=1, source_target_pairs={{0,1},{1,0},{2,3},{3,2},{4,5},{5,4},{6,7},{7,6},{8,9},{9,8},{10,11... | collective-permute-start | bytes 786440 | tf_op jit(solution)/shard_map/ppermute | solution.py:224
  40.4 1.4 %collective-permute-start.5 = (bf16[4,128,128]{2,1,0:T(8,128)(2,1)S(1)}, bf16[4,128,128]{2,1,0:T(8,128)(2,1)S(1)}, u32[]{:S(2)}, u32[]{:S(2)}) collective-permute-start(bf16[4,128,128]{2,1,0:T(8,128)(2,1)S(1)} %get-tuple-element.34), channel_id=1, source_target_pairs={{0,1},{1,0},{2,3},{3,2},{4,5},{5,4},{6,7},{7,6},{8,9},{9,8},{10,11... | collective-permute-start | bytes 393224 | tf_op jit(solution)/shard_map/ppermute | solution.py:224
  67.9 3.2 %collective-permute-start.6 = (bf16[2,32,512]{2,1,0:T(8,128)(2,1)S(1)}, bf16[2,32,512]{2,1,0:T(8,128)(2,1)S(1)}, u32[]{:S(2)}, u32[]{:S(2)}) collective-permute-start(bf16[2,32,512]{2,1,0:T(8,128)(2,1)S(1)} %get-tuple-element.36), channel_id=1, source_target_pairs={{0,1},{1,0},{2,3},{3,2},{4,5},{5,4},{6,7},{7,6},{8,9},{9,8},{10,11... | collective-permute-start | bytes 196616 | tf_op jit(solution)/shard_map/ppermute | solution.py:224
  69.4 3.7 %collective-permute-start.7 = (bf16[2,32,512]{2,1,0:T(8,128)(2,1)S(1)}, bf16[2,32,512]{2,1,0:T(8,128)(2,1)S(1)}, u32[]{:S(2)}, u32[]{:S(2)}) collective-permute-start(bf16[2,32,512]{2,1,0:T(8,128)(2,1)S(1)} %get-tuple-element.37), channel_id=1, source_target_pairs={{0,2},{1,3},{2,0},{3,1},{4,6},{5,7},{6,4},{7,5},{8,10},{9,11},{10,... | collective-permute-start | bytes 196616 | tf_op jit(solution)/shard_map/ppermute | solution.py:224
  70.1 4.6 %collective-permute-start.8 = (bf16[2,32,512]{2,1,0:T(8,128)(2,1)S(1)}, bf16[2,32,512]{2,1,0:T(8,128)(2,1)S(1)}, u32[]{:S(2)}, u32[]{:S(2)}) collective-permute-start(bf16[2,32,512]{2,1,0:T(8,128)(2,1)S(1)} %get-tuple-element.38), channel_id=1, source_target_pairs={{0,3},{1,2},{2,1},{3,0},{4,7},{5,6},{6,5},{7,4},{8,11},{9,10},{10,... | collective-permute-start | bytes 196616 | tf_op jit(solution)/shard_map/ppermute | solution.py:224

commit v12 on v11

--- a/solution.py
+++ b/solution.py
@@ -187,25 +187,33 @@
     out[...] = rows[...].reshape(128, 16, 128).astype(bf16)
 
 
-def updates(got, late, vectors, out0, out1, out2, out3, rows, gate_rows, update):
-    mine = position()
+def finish(late, normed, gating, *outs):
+    for out, step in outs:
+        some = pl.ds(pl.multiple_of((position() ^ step) * 32, 32), 32)
+        final = late[some, 128:256]
+        for jj in range(2):
+            value = jnp.dot(final, normed[jj], preferred_element_type=f32)
+            out[jj] = (value * gating[jj, some, :].astype(f32)).astype(bf16)
+
+
+def updates(got, late, vectors, out1, out2, out3, normed, gating, rows, gate_rows):
     rows[...] = got[...].astype(f32).reshape(2048, 128)
     gains, biases = column(vectors[2:3]), column(vectors[3:4])
-    final = late[:, 128:256]
     for jj in range(2):
         for ii in range(4):
             gate_rows[pl.ds(ii, 128, stride=4), :] = rows[
                 pl.ds(8 + 4 * jj + ii, 128, stride=16), :
             ]
-        gating = from_peers(gate_rows).T
+        gating[jj] = from_peers(gate_rows).T.astype(bf16)
         for lane in range(4):
             hidden = rows[pl.ds(4 * jj + lane, 128, stride=16), :]
-            normed = layer_norm(hidden, gains, biases).astype(bf16)
-            value = jnp.dot(final, normed, preferred_element_type=f32)
             at = slice(128 * lane, 128 * (lane + 1))
-            update[jj, :, at] = (value * gating[:, at]).astype(bf16)
-    for step, out in enumerate((out0, out1, out2, out3)):
-        out[...] = update[:, pl.ds(pl.multiple_of((mine ^ step) * 32, 32), 32), :]
+            normed[jj, :, at] = layer_norm(hidden, gains, biases).astype(bf16)
+    finish(late, normed, gating, (out1, 1), (out2, 2), (out3, 3))
+
+
+def updates_near(late, normed, gating, out0):
+    finish(late, normed, gating, (out0, 0))
 
 
 def arrange(in0, in1, in2, in3, out, rows):
@@ -240,8 +248,8 @@
     )
 
 
-def exchange(parts):
-    return [parts[0]] + [swap(parts[step], step) for step in (1, 2, 3)]
+def exchange(parts, *steps):
+    return [parts[0]] + [swap(parts[step], step) for step in steps]
 
 
 def body(
@@ -282,7 +290,7 @@
             pltpu.VMEM((128, 512), bf16),
             pltpu.VMEM((2048, 128), f32),
         ],
-    )(*exchange(parts), around(shared, 3), vectors)
+    )(*exchange(parts, 1, 2, 3), around(shared, 3), vectors)
     own = scatter(sent)
     kept, given = call(
         gates,
@@ -309,18 +317,18 @@
         ],
     )(left, right, swap(own[:, :8], 1), kept, swap(given, 1))
     got = scatter(sent)
-    parts = call(
+    out1, out2, out3, normed, gating = call(
         updates,
         "updates",
-        (shape(2, 32, 512),) * 4,
-        [
-            pltpu.VMEM((2048, 128), f32),
-            pltpu.VMEM((512, 128), f32),
-            pltpu.VMEM((2, 128, 512), bf16),
-        ],
+        (shape(2, 32, 512),) * 3 + (shape(2, 128, 512),) * 2,
+        [pltpu.VMEM((2048, 128), f32), pltpu.VMEM((512, 128), f32)],
     )(got, late, vectors)
+    near = call(updates_near, "updates_near", shape(2, 32, 512), [], flops=1 << 30)(
+        late, normed, gating
+    )
+    parts = (near, out1, out2, out3)
     return call(arrange, "arrange", shape(32, 8, 512), [pltpu.VMEM((4, 256, 128), f32)])(
-        *exchange(parts)
+        *exchange(parts, 1, 2, 3)
     )
 
 

time: 75.7 us -> 75.8 us (level)
  no operation moved by 1% of the time
where the time goes in v12:
time: 75.8 us; the launch traced here: 75.6 us
  blocking collectives  51.2 us (68%)
  starting transfers between devices  10.7 us (14%)
  waiting for transfers between devices  8.21 us (11%)
  Pallas kernels  5.33 us (7%)
    all_to_all x2, blocking collectives, scatter(): lax.all_to_all(messages, ('y', 'xh', 'z', 'xl', 'core'), 0, 0, axis_index...  51.2 us
    ppermute x8, starting transfers between devices, swap(): lax.ppermute(array, ('xl', 'core'), [(s, s ^ step) for s in range(4)])  9.91 us
    ppermute x8, waiting for transfers between devices, swap(): lax.ppermute(array, ('xl', 'core'), [(s, s ^ step) for s in range(4)])  4.27 us
    ppermute x1, waiting for transfers between devices, around(): return lax.ppermute(array, ('xh', 'xl', 'core'), pairs)  3.94 us
  transfers between devices with their start and end apart: 9, of which 4 were waited for; matrix products, arithmetic and copies ran while one was open for 0% of the time, Pallas kernels for 1%

profile of v12, /device:TPU:1, one launch (start us, length us, event | category | flops | bytes accessed | tf_op | source)
XLA Modules:
  0.0 75.6 jit_solution(8903977429446383473)
XLA Ops:
  0.0 1.2 %lay_out.1 = (bf16[112,512]{1,0:T(8,128)(2,1)S(1)}, bf16[112,512]{1,0:T(8,128)(2,1)S(1)}, bf16[112,512]{1,0:T(8,128)(2,1)S(1)}, bf16[64,512]{1,0:T(8,128)(2,1)S(...) custom-call(bf16[32,8,512]{2,1,0:T(8,128)(2,1)} %refs_0_.1, bf16[32,128]{1,0:T(8,128)(2,1)} %bitcast.10, ...), custom_call_target="tpu_custom_call" | custom-call | bytes 1048576 | tf_op jit(solution)/shard_map/lay_out/pallas_call | solution.py:270
  1.2 3.3 %collective-permute-start = (bf16[112,512]{1,0:T(8,128)(2,1)S(1)}, bf16[112,512]{1,0:T(8,128)(2,1)S(1)}, u32[]{:S(2)}, u32[]{:S(2)}) collective-permute-start(bf16[112,512]{1,0:T(8,128)(2,1)S(1)} %get-tuple-element.24), channel_id=1, source_target_pairs={{0,1},{1,0},{2,3},{3,2},{4,5},{5,4},{6,7},{7,6},{8,9},{9,8},{10,11... | collective-permute-start | bytes 344072 | tf_op jit(solution)/shard_map/ppermute | solution.py:232
  4.6 0.0 collective-permute-start.1
  4.6 1.7 %collective-permute-start.2 = (bf16[64,512]{1,0:T(8,128)(2,1)S(1)}, bf16[64,512]{1,0:T(8,128)(2,1)S(1)}, u32[]{:S(2)}, u32[]{:S(2)}) collective-permute-start(bf16[64,512]{1,0:T(8,128)(2,1)S(1)} %get-tuple-element.26), channel_id=1, source_target_pairs={{0,3},{1,2},{2,1},{3,0},{4,7},{5,6},{6,5},{7,4},{8,11},{9,10},{10,... | collective-permute-start | bytes 196616 | tf_op jit(solution)/shard_map/ppermute | solution.py:232
  6.3 0.8 %collective-permute-start.3 = (bf16[48,512]{1,0:T(8,128)(2,1)S(1)}, bf16[48,512]{1,0:T(8,128)(2,1)S(1)}, u32[]{:S(2)}, u32[]{:S(2)}) collective-permute-start(bf16[48,512]{1,0:T(8,128)(2,1)S(1)} %get-tuple-element.27), channel_id=1, source_target_pairs={{0,35},{1,34},{2,33},{3,32},{32,3},{33,2},{34,1},{35,0},{4,39},{5,... | collective-permute-start | bytes 147464 | tf_op jit(solution)/shard_map/ppermute | solution.py:237
  7.1 3.9 %collective-permute-done.3.shared3 = bf16[48,512]{1,0:T(8,128)(2,1)S(1)} collective-permute-done((bf16[48,512]{1,0:T(8,128)(2,1)S(1)}, bf16[48,512]{1,0:T(8,128)(2,1)S(1)}, u32[]{:S(2)}, u32[]{:S(2)}) %collective-permute-start.3) | collective-permute-done | bytes 49184 | tf_op jit(solution)/shard_map/ppermute | solution.py:237
  11.0 0.0 collective-permute-done.2.in3
  11.0 0.0 collective-permute-done.in1
  11.0 0.0 collective-permute-done.1.in2
  11.0 0.8 %factors.1 = (bf16[128,16,128]{2,1,0:T(8,128)(2,1)S(1)}, bf16[2,128,512]{2,1,0:T(8,128)(2,1)S(1)}, bf16[128,256]{1,0:T(8,128)(2,1)S(1)}) custom-call(bf16[112,512]{1,0:T(8,128)(2,1)S(1)} %get-tuple-element.23.in0, bf16[112,512]{1,0:T(8,128)(2,1)S(1)} %collective-permute-done.in1, bf16[112,512]{1,0:T(8,128)(2,1)S(1)} %collective-permute-done.1.in2, ...), custom_call_target="tpu_custom_call" | custom-call | bytes 1048576 | tf_op jit(solution)/shard_map/factors/pallas_call | solution.py:284
  11.8 26.7 %all_to_all.10.own = bf16[128,16,128]{2,1,0:T(8,128)(2,1)S(1)} all-to-all(bf16[128,16,128]{2,1,0:T(8,128)(2,1)S(1)} %get-tuple-element.30), channel_id=1, replica_groups={{180,182,0,2,32,34,64,66,96,98,128,130,160,162,192,194,224,226,4,6,28,3..., dimensions={0} | all-to-all | bytes 1048576 | tf_op jit(solution)/shard_map/all_to_all | solution.py:241
  38.5 1.5 %collective-permute-start.4 = (bf16[128,8,128]{2,1,0:T(8,128)(2,1)S(1)}, bf16[128,8,128]{2,1,0:T(8,128)(2,1)S(1)}, u32[]{:S(2)}, u32[]{:S(2)}) collective-permute-start(bf16[128,8,128]{2,1,0:T(8,128)(2,1)S(1)} %slice.4), channel_id=1, source_target_pairs={{0,1},{1,0},{2,3},{3,2},{4,5},{5,4},{6,7},{7,6},{8,9},{9,8},{10,11... | collective-permute-start | bytes 786440 | tf_op jit(solution)/shard_map/ppermute | solution.py:232
  40.0 0.4 gates.1
  40.4 0.1 collective-permute-start.5
  40.5 0.4 prepare.1
  40.9 0.9 %collective-permute-done.5.given = bf16[4,128,128]{2,1,0:T(8,128)(2,1)S(1)} collective-permute-done((bf16[4,128,128]{2,1,0:T(8,128)(2,1)S(1)}, bf16[4,128,128]{2,1,0:T(8,128)(2,1)S(1)}, u32[]{:S(2)}, u32[]{:S(2)}) %collective-permute-start.5) | collective-permute-done | bytes 131104 | tf_op jit(solution)/shard_map/ppermute | solution.py:232
  41.8 0.0 collective-permute-done.4.other
  41.8 0.8 %products.1 = bf16[128,16,128]{2,1,0:T(8,128)(2,1)S(1)} custom-call(f32[4,512,128]{2,1,0:T(8,128)S(1)} %get-tuple-element.31.own_left, bf16[256,512]{1,0:T(8,128)(2,1)S(1)} %get-tuple-element.32.right, bf16[128,8,128]{2,1,0:T(8,128)(2,1)S(1)} %collective-permute-done.4.other, bf16[4,128,128]{2,1,0:T(8,128)(2,1)S(1)} %get-tuple-element.34.kept, ...), custom_call_target="tpu_custom_call" | custom-call | bytes 1048576 | tf_op jit(solution)/shard_map/products/pallas_call | solution.py:309
  42.6 24.6 %all_to_all.11.got = bf16[128,16,128]{2,1,0:T(8,128)(2,1)S(1)} all-to-all(bf16[128,16,128]{2,1,0:T(8,128)(2,1)S(1)} %products.1), channel_id=1, replica_groups={{180,182,0,2,32,34,64,66,96,98,128,130,160,162,192,194,224,226,4,6,28,3..., dimensions={0} | all-to-all | bytes 1048576 | tf_op jit(solution)/shard_map/all_to_all | solution.py:241
  67.2 0.8 %updates.1 = (bf16[2,32,512]{2,1,0:T(8,128)(2,1)S(1)}, bf16[2,32,512]{2,1,0:T(8,128)(2,1)S(1)}, bf16[2,32,512]{2,1,0:T(8,128)(2,1)S(1)}, bf16[2,128,512]{2,1,0:T(8,128)(2,1)S(1)}, bf16[2,128,512]{2,1,0:T(8,128)(2,1)S(1)}) custom-call(bf16[128,16,128]{2,1,0:T(8,128)(2,1)S(1)} %all_to_all.11.got, bf16[128,256]{1,0:T(8,128)(2,1)S(1)} %get-tuple-element.29.late, ...), custom_call_target="tpu_custom_call" | custom-call | bytes 1048576 | tf_op jit(solution)/shard_map/updates/pallas_call | solution.py:320
  68.0 1.5 %collective-permute-start.6 = (bf16[2,32,512]{2,1,0:T(8,128)(2,1)S(1)}, bf16[2,32,512]{2,1,0:T(8,128)(2,1)S(1)}, u32[]{:S(2)}, u32[]{:S(2)}) collective-permute-start(bf16[2,32,512]{2,1,0:T(8,128)(2,1)S(1)} %get-tuple-element.38), channel_id=1, source_target_pairs={{0,1},{1,0},{2,3},{3,2},{4,5},{5,4},{6,7},{7,6},{8,9},{9,8},{10,11... | collective-permute-start | bytes 196616 | tf_op jit(solution)/shard_map/ppermute | solution.py:232
  69.5 0.6 collective-permute-start.7
  70.1 1.1 %collective-permute-start.8 = (bf16[2,32,512]{2,1,0:T(8,128)(2,1)S(1)}, bf16[2,32,512]{2,1,0:T(8,128)(2,1)S(1)}, u32[]{:S(2)}, u32[]{:S(2)}) collective-permute-start(bf16[2,32,512]{2,1,0:T(8,128)(2,1)S(1)} %get-tuple-element.40), channel_id=1, source_target_pairs={{0,3},{1,2},{2,1},{3,0},{4,7},{5,6},{6,5},{7,4},{8,11},{9,10},{10,... | collective-permute-start | bytes 196616 | tf_op jit(solution)/shard_map/ppermute | solution.py:232
  71.2 0.1 updates_near.1.in0
  71.4 0.0 collective-permute-done.6.in1
  71.4 1.8 %collective-permute-done.7.in2 = bf16[2,32,512]{2,1,0:T(8,128)(2,1)S(1)} collective-permute-done((bf16[2,32,512]{2,1,0:T(8,128)(2,1)S(1)}, bf16[2,32,512]{2,1,0:T(8,128)(2,1)S(1)}, u32[]{:S(2)}, u32[]{:S(2)}) %collective-permute-start.7) | collective-permute-done | bytes 65568 | tf_op jit(solution)/shard_map/ppermute | solution.py:232
  73.2 1.6 %collective-permute-done.8.in3 = bf16[2,32,512]{2,1,0:T(8,128)(2,1)S(1)} collective-permute-done((bf16[2,32,512]{2,1,0:T(8,128)(2,1)S(1)}, bf16[2,32,512]{2,1,0:T(8,128)(2,1)S(1)}, u32[]{:S(2)}, u32[]{:S(2)}) %collective-permute-start.8) | collective-permute-done | bytes 65568 | tf_op jit(solution)/shard_map/ppermute | solution.py:232
  74.7 0.8 %arrange.1 = bf16[32,8,512]{2,1,0:T(8,128)(2,1)} custom-call(bf16[2,32,512]{2,1,0:T(8,128)(2,1)S(1)} %updates_near.1.in0, bf16[2,32,512]{2,1,0:T(8,128)(2,1)S(1)} %collective-permute-done.6.in1, bf16[2,32,512]{2,1,0:T(8,128)(2,1)S(1)} %collective-permute-done.7.in2, bf16[2,32,512]{2,1,0:T(8,128)(2,1)S(1)} %collective-permute-done.8.in3), custom_call_target="tpu_custom_call" | custom-call | bytes 1048576 | tf_op jit(solution)/shard_map/arrange/pallas_call | solution.py:330
  (1 shorter events, 0.0 us)
Async XLA Ops:
  1.2 9.8 %collective-permute-start = (bf16[112,512]{1,0:T(8,128)(2,1)S(1)}, bf16[112,512]{1,0:T(8,128)(2,1)S(1)}, u32[]{:S(2)}, u32[]{:S(2)}) collective-permute-start(bf16[112,512]{1,0:T(8,128)(2,1)S(1)} %get-tuple-element.24), channel_id=1, source_target_pairs={{0,1},{1,0},{2,3},{3,2},{4,5},{5,4},{6,7},{7,6},{8,9},{9,8},{10,11... | collective-permute-start | bytes 344072 | tf_op jit(solution)/shard_map/ppermute | solution.py:232
  4.6 6.5 %collective-permute-start.1 = (bf16[112,512]{1,0:T(8,128)(2,1)S(1)}, bf16[112,512]{1,0:T(8,128)(2,1)S(1)}, u32[]{:S(2)}, u32[]{:S(2)}) collective-permute-start(bf16[112,512]{1,0:T(8,128)(2,1)S(1)} %get-tuple-element.25), channel_id=1, source_target_pairs={{0,2},{1,3},{2,0},{3,1},{4,6},{5,7},{6,4},{7,5},{8,10},{9,11},{10,... | collective-permute-start | bytes 344072 | tf_op jit(solution)/shard_map/ppermute | solution.py:232
  4.6 6.5 %collective-permute-start.2 = (bf16[64,512]{1,0:T(8,128)(2,1)S(1)}, bf16[64,512]{1,0:T(8,128)(2,1)S(1)}, u32[]{:S(2)}, u32[]{:S(2)}) collective-permute-start(bf16[64,512]{1,0:T(8,128)(2,1)S(1)} %get-tuple-element.26), channel_id=1, source_target_pairs={{0,3},{1,2},{2,1},{3,0},{4,7},{5,6},{6,5},{7,4},{8,11},{9,10},{10,... | collective-permute-start | bytes 196616 | tf_op jit(solution)/shard_map/ppermute | solution.py:232
  6.3 4.7 %collective-permute-start.3 = (bf16[48,512]{1,0:T(8,128)(2,1)S(1)}, bf16[48,512]{1,0:T(8,128)(2,1)S(1)}, u32[]{:S(2)}, u32[]{:S(2)}) collective-permute-start(bf16[48,512]{1,0:T(8,128)(2,1)S(1)} %get-tuple-element.27), channel_id=1, source_target_pairs={{0,35},{1,34},{2,33},{3,32},{32,3},{33,2},{34,1},{35,0},{4,39},{5,... | collective-permute-start | bytes 147464 | tf_op jit(solution)/shard_map/ppermute | solution.py:237
  38.5 3.3 %collective-permute-start.4 = (bf16[128,8,128]{2,1,0:T(8,128)(2,1)S(1)}, bf16[128,8,128]{2,1,0:T(8,128)(2,1)S(1)}, u32[]{:S(2)}, u32[]{:S(2)}) collective-permute-start(bf16[128,8,128]{2,1,0:T(8,128)(2,1)S(1)} %slice.4), channel_id=1, source_target_pairs={{0,1},{1,0},{2,3},{3,2},{4,5},{5,4},{6,7},{7,6},{8,9},{9,8},{10,11... | collective-permute-start | bytes 786440 | tf_op jit(solution)/shard_map/ppermute | solution.py:232
  40.4 1.4 %collective-permute-start.5 = (bf16[4,128,128]{2,1,0:T(8,128)(2,1)S(1)}, bf16[4,128,128]{2,1,0:T(8,128)(2,1)S(1)}, u32[]{:S(2)}, u32[]{:S(2)}) collective-permute-start(bf16[4,128,128]{2,1,0:T(8,128)(2,1)S(1)} %get-tuple-element.35), channel_id=1, source_target_pairs={{0,1},{1,0},{2,3},{3,2},{4,5},{5,4},{6,7},{7,6},{8,9},{9,8},{10,11... | collective-permute-start | bytes 393224 | tf_op jit(solution)/shard_map/ppermute | solution.py:232
  68.0 3.4 %collective-permute-start.6 = (bf16[2,32,512]{2,1,0:T(8,128)(2,1)S(1)}, bf16[2,32,512]{2,1,0:T(8,128)(2,1)S(1)}, u32[]{:S(2)}, u32[]{:S(2)}) collective-permute-start(bf16[2,32,512]{2,1,0:T(8,128)(2,1)S(1)} %get-tuple-element.38), channel_id=1, source_target_pairs={{0,1},{1,0},{2,3},{3,2},{4,5},{5,4},{6,7},{7,6},{8,9},{9,8},{10,11... | collective-permute-start | bytes 196616 | tf_op jit(solution)/shard_map/ppermute | solution.py:232
  69.5 3.7 %collective-permute-start.7 = (bf16[2,32,512]{2,1,0:T(8,128)(2,1)S(1)}, bf16[2,32,512]{2,1,0:T(8,128)(2,1)S(1)}, u32[]{:S(2)}, u32[]{:S(2)}) collective-permute-start(bf16[2,32,512]{2,1,0:T(8,128)(2,1)S(1)} %get-tuple-element.39), channel_id=1, source_target_pairs={{0,2},{1,3},{2,0},{3,1},{4,6},{5,7},{6,4},{7,5},{8,10},{9,11},{10,... | collective-permute-start | bytes 196616 | tf_op jit(solution)/shard_map/ppermute | solution.py:232
  70.1 4.6 %collective-permute-start.8 = (bf16[2,32,512]{2,1,0:T(8,128)(2,1)S(1)}, bf16[2,32,512]{2,1,0:T(8,128)(2,1)S(1)}, u32[]{:S(2)}, u32[]{:S(2)}) collective-permute-start(bf16[2,32,512]{2,1,0:T(8,128)(2,1)S(1)} %get-tuple-element.40), channel_id=1, source_target_pairs={{0,3},{1,2},{2,1},{3,0},{4,7},{5,6},{6,5},{7,4},{8,11},{9,10},{10,... | collective-permute-start | bytes 196616 | tf_op jit(solution)/shard_map/ppermute | solution.py:232

commit v13 on v12

--- a/solution.py
+++ b/solution.py
@@ -125,7 +125,8 @@
             )
 
         for side in range(2):
-            factor = jax.nn.sigmoid(project(2 * side + 1)) * project(2 * side)
+            gate = 0.5 * jnp.tanh(0.5 * project(2 * side + 1)) + 0.5
+            factor = gate * project(2 * side)
             for lane in range(4):
                 rows[pl.ds(8 * side + 4 * ii + lane, 128, stride=16), :] = factor[
                     :, 128 * lane : 128 * (lane + 1)

time: 75.8 us -> 75.8 us (level)
  no operation moved by 1% of the time
where the time goes in v13:
time: 75.8 us; the launch traced here: 75.6 us
  blocking collectives  51.2 us (68%)
  starting transfers between devices  10.7 us (14%)
  waiting for transfers between devices  8.21 us (11%)
  Pallas kernels  5.37 us (7%)
    all_to_all x2, blocking collectives, scatter(): lax.all_to_all(messages, ('y', 'xh', 'z', 'xl', 'core'), 0, 0, axis_index...  51.2 us
    ppermute x8, starting transfers between devices, swap(): lax.ppermute(array, ('xl', 'core'), [(s, s ^ step) for s in range(4)])  9.91 us
    ppermute x8, waiting for transfers between devices, swap(): lax.ppermute(array, ('xl', 'core'), [(s, s ^ step) for s in range(4)])  4.27 us
    ppermute x1, waiting for transfers between devices, around(): return lax.ppermute(array, ('xh', 'xl', 'core'), pairs)  3.94 us
  transfers between devices with their start and end apart: 9, of which 4 were waited for; matrix products, arithmetic and copies ran while one was open for 0% of the time, Pallas kernels for 1%

profile of v13, /device:TPU:1, one launch (start us, length us, event | category | flops | bytes accessed | tf_op | source)
XLA Modules:
  0.0 75.6 jit_solution(15852548645576582462)
XLA Ops:
  0.0 1.2 %lay_out.1 = (bf16[112,512]{1,0:T(8,128)(2,1)S(1)}, bf16[112,512]{1,0:T(8,128)(2,1)S(1)}, bf16[112,512]{1,0:T(8,128)(2,1)S(1)}, bf16[64,512]{1,0:T(8,128)(2,1)S(...) custom-call(bf16[32,8,512]{2,1,0:T(8,128)(2,1)} %refs_0_.1, bf16[32,128]{1,0:T(8,128)(2,1)} %bitcast.10, ...), custom_call_target="tpu_custom_call" | custom-call | bytes 1048576 | tf_op jit(solution)/shard_map/lay_out/pallas_call | solution.py:271
  1.2 3.3 %collective-permute-start = (bf16[112,512]{1,0:T(8,128)(2,1)S(1)}, bf16[112,512]{1,0:T(8,128)(2,1)S(1)}, u32[]{:S(2)}, u32[]{:S(2)}) collective-permute-start(bf16[112,512]{1,0:T(8,128)(2,1)S(1)} %get-tuple-element.24), channel_id=1, source_target_pairs={{0,1},{1,0},{2,3},{3,2},{4,5},{5,4},{6,7},{7,6},{8,9},{9,8},{10,11... | collective-permute-start | bytes 344072 | tf_op jit(solution)/shard_map/ppermute | solution.py:233
  4.6 0.0 collective-permute-start.1
  4.6 1.7 %collective-permute-start.2 = (bf16[64,512]{1,0:T(8,128)(2,1)S(1)}, bf16[64,512]{1,0:T(8,128)(2,1)S(1)}, u32[]{:S(2)}, u32[]{:S(2)}) collective-permute-start(bf16[64,512]{1,0:T(8,128)(2,1)S(1)} %get-tuple-element.26), channel_id=1, source_target_pairs={{0,3},{1,2},{2,1},{3,0},{4,7},{5,6},{6,5},{7,4},{8,11},{9,10},{10,... | collective-permute-start | bytes 196616 | tf_op jit(solution)/shard_map/ppermute | solution.py:233
  6.3 0.8 %collective-permute-start.3 = (bf16[48,512]{1,0:T(8,128)(2,1)S(1)}, bf16[48,512]{1,0:T(8,128)(2,1)S(1)}, u32[]{:S(2)}, u32[]{:S(2)}) collective-permute-start(bf16[48,512]{1,0:T(8,128)(2,1)S(1)} %get-tuple-element.27), channel_id=1, source_target_pairs={{0,35},{1,34},{2,33},{3,32},{32,3},{33,2},{34,1},{35,0},{4,39},{5,... | collective-permute-start | bytes 147464 | tf_op jit(solution)/shard_map/ppermute | solution.py:238
  7.1 3.9 %collective-permute-done.3.shared3 = bf16[48,512]{1,0:T(8,128)(2,1)S(1)} collective-permute-done((bf16[48,512]{1,0:T(8,128)(2,1)S(1)}, bf16[48,512]{1,0:T(8,128)(2,1)S(1)}, u32[]{:S(2)}, u32[]{:S(2)}) %collective-permute-start.3) | collective-permute-done | bytes 49184 | tf_op jit(solution)/shard_map/ppermute | solution.py:238
  11.0 0.0 collective-permute-done.2.in3
  11.0 0.0 collective-permute-done.in1
  11.0 0.0 collective-permute-done.1.in2
  11.0 0.8 %factors.1 = (bf16[128,16,128]{2,1,0:T(8,128)(2,1)S(1)}, bf16[2,128,512]{2,1,0:T(8,128)(2,1)S(1)}, bf16[128,256]{1,0:T(8,128)(2,1)S(1)}) custom-call(bf16[112,512]{1,0:T(8,128)(2,1)S(1)} %get-tuple-element.23.in0, bf16[112,512]{1,0:T(8,128)(2,1)S(1)} %collective-permute-done.in1, bf16[112,512]{1,0:T(8,128)(2,1)S(1)} %collective-permute-done.1.in2, ...), custom_call_target="tpu_custom_call" | custom-call | bytes 1048576 | tf_op jit(solution)/shard_map/factors/pallas_call | solution.py:285
  11.9 26.6 %all_to_all.10.own = bf16[128,16,128]{2,1,0:T(8,128)(2,1)S(1)} all-to-all(bf16[128,16,128]{2,1,0:T(8,128)(2,1)S(1)} %get-tuple-element.30), channel_id=1, replica_groups={{180,182,0,2,32,34,64,66,96,98,128,130,160,162,192,194,224,226,4,6,28,3..., dimensions={0} | all-to-all | bytes 1048576 | tf_op jit(solution)/shard_map/all_to_all | solution.py:242
  38.5 1.5 %collective-permute-start.4 = (bf16[128,8,128]{2,1,0:T(8,128)(2,1)S(1)}, bf16[128,8,128]{2,1,0:T(8,128)(2,1)S(1)}, u32[]{:S(2)}, u32[]{:S(2)}) collective-permute-start(bf16[128,8,128]{2,1,0:T(8,128)(2,1)S(1)} %slice.4), channel_id=1, source_target_pairs={{0,1},{1,0},{2,3},{3,2},{4,5},{5,4},{6,7},{7,6},{8,9},{9,8},{10,11... | collective-permute-start | bytes 786440 | tf_op jit(solution)/shard_map/ppermute | solution.py:233
  40.0 0.4 gates.1
  40.4 0.1 collective-permute-start.5
  40.5 0.4 prepare.1
  41.0 0.9 %collective-permute-done.5.given = bf16[4,128,128]{2,1,0:T(8,128)(2,1)S(1)} collective-permute-done((bf16[4,128,128]{2,1,0:T(8,128)(2,1)S(1)}, bf16[4,128,128]{2,1,0:T(8,128)(2,1)S(1)}, u32[]{:S(2)}, u32[]{:S(2)}) %collective-permute-start.5) | collective-permute-done | bytes 131104 | tf_op jit(solution)/shard_map/ppermute | solution.py:233
  41.9 0.0 collective-permute-done.4.other
  41.9 0.8 %products.1 = bf16[128,16,128]{2,1,0:T(8,128)(2,1)S(1)} custom-call(f32[4,512,128]{2,1,0:T(8,128)S(1)} %get-tuple-element.31.own_left, bf16[256,512]{1,0:T(8,128)(2,1)S(1)} %get-tuple-element.32.right, bf16[128,8,128]{2,1,0:T(8,128)(2,1)S(1)} %collective-permute-done.4.other, bf16[4,128,128]{2,1,0:T(8,128)(2,1)S(1)} %get-tuple-element.34.kept, ...), custom_call_target="tpu_custom_call" | custom-call | bytes 1048576 | tf_op jit(solution)/shard_map/products/pallas_call | solution.py:310
  42.7 24.6 %all_to_all.11.got = bf16[128,16,128]{2,1,0:T(8,128)(2,1)S(1)} all-to-all(bf16[128,16,128]{2,1,0:T(8,128)(2,1)S(1)} %products.1), channel_id=1, replica_groups={{180,182,0,2,32,34,64,66,96,98,128,130,160,162,192,194,224,226,4,6,28,3..., dimensions={0} | all-to-all | bytes 1048576 | tf_op jit(solution)/shard_map/all_to_all | solution.py:242
  67.3 0.8 %updates.1 = (bf16[2,32,512]{2,1,0:T(8,128)(2,1)S(1)}, bf16[2,32,512]{2,1,0:T(8,128)(2,1)S(1)}, bf16[2,32,512]{2,1,0:T(8,128)(2,1)S(1)}, bf16[2,128,512]{2,1,0:T(8,128)(2,1)S(1)}, bf16[2,128,512]{2,1,0:T(8,128)(2,1)S(1)}) custom-call(bf16[128,16,128]{2,1,0:T(8,128)(2,1)S(1)} %all_to_all.11.got, bf16[128,256]{1,0:T(8,128)(2,1)S(1)} %get-tuple-element.29.late, ...), custom_call_target="tpu_custom_call" | custom-call | bytes 1048576 | tf_op jit(solution)/shard_map/updates/pallas_call | solution.py:321
  68.0 1.5 %collective-permute-start.6 = (bf16[2,32,512]{2,1,0:T(8,128)(2,1)S(1)}, bf16[2,32,512]{2,1,0:T(8,128)(2,1)S(1)}, u32[]{:S(2)}, u32[]{:S(2)}) collective-permute-start(bf16[2,32,512]{2,1,0:T(8,128)(2,1)S(1)} %get-tuple-element.38), channel_id=1, source_target_pairs={{0,1},{1,0},{2,3},{3,2},{4,5},{5,4},{6,7},{7,6},{8,9},{9,8},{10,11... | collective-permute-start | bytes 196616 | tf_op jit(solution)/shard_map/ppermute | solution.py:233
  69.5 0.6 collective-permute-start.7
  70.2 1.1 %collective-permute-start.8 = (bf16[2,32,512]{2,1,0:T(8,128)(2,1)S(1)}, bf16[2,32,512]{2,1,0:T(8,128)(2,1)S(1)}, u32[]{:S(2)}, u32[]{:S(2)}) collective-permute-start(bf16[2,32,512]{2,1,0:T(8,128)(2,1)S(1)} %get-tuple-element.40), channel_id=1, source_target_pairs={{0,3},{1,2},{2,1},{3,0},{4,7},{5,6},{6,5},{7,4},{8,11},{9,10},{10,... | collective-permute-start | bytes 196616 | tf_op jit(solution)/shard_map/ppermute | solution.py:233
  71.3 0.1 updates_near.1.in0
  71.4 0.0 collective-permute-done.6.in1
  71.4 1.8 %collective-permute-done.7.in2 = bf16[2,32,512]{2,1,0:T(8,128)(2,1)S(1)} collective-permute-done((bf16[2,32,512]{2,1,0:T(8,128)(2,1)S(1)}, bf16[2,32,512]{2,1,0:T(8,128)(2,1)S(1)}, u32[]{:S(2)}, u32[]{:S(2)}) %collective-permute-start.7) | collective-permute-done | bytes 65568 | tf_op jit(solution)/shard_map/ppermute | solution.py:233
  73.2 1.6 %collective-permute-done.8.in3 = bf16[2,32,512]{2,1,0:T(8,128)(2,1)S(1)} collective-permute-done((bf16[2,32,512]{2,1,0:T(8,128)(2,1)S(1)}, bf16[2,32,512]{2,1,0:T(8,128)(2,1)S(1)}, u32[]{:S(2)}, u32[]{:S(2)}) %collective-permute-start.8) | collective-permute-done | bytes 65568 | tf_op jit(solution)/shard_map/ppermute | solution.py:233
  74.8 0.8 %arrange.1 = bf16[32,8,512]{2,1,0:T(8,128)(2,1)} custom-call(bf16[2,32,512]{2,1,0:T(8,128)(2,1)S(1)} %updates_near.1.in0, bf16[2,32,512]{2,1,0:T(8,128)(2,1)S(1)} %collective-permute-done.6.in1, bf16[2,32,512]{2,1,0:T(8,128)(2,1)S(1)} %collective-permute-done.7.in2, bf16[2,32,512]{2,1,0:T(8,128)(2,1)S(1)} %collective-permute-done.8.in3), custom_call_target="tpu_custom_call" | custom-call | bytes 1048576 | tf_op jit(solution)/shard_map/arrange/pallas_call | solution.py:331
  (1 shorter events, 0.0 us)
Async XLA Ops:
  1.2 9.8 %collective-permute-start = (bf16[112,512]{1,0:T(8,128)(2,1)S(1)}, bf16[112,512]{1,0:T(8,128)(2,1)S(1)}, u32[]{:S(2)}, u32[]{:S(2)}) collective-permute-start(bf16[112,512]{1,0:T(8,128)(2,1)S(1)} %get-tuple-element.24), channel_id=1, source_target_pairs={{0,1},{1,0},{2,3},{3,2},{4,5},{5,4},{6,7},{7,6},{8,9},{9,8},{10,11... | collective-permute-start | bytes 344072 | tf_op jit(solution)/shard_map/ppermute | solution.py:233
  4.6 6.5 %collective-permute-start.1 = (bf16[112,512]{1,0:T(8,128)(2,1)S(1)}, bf16[112,512]{1,0:T(8,128)(2,1)S(1)}, u32[]{:S(2)}, u32[]{:S(2)}) collective-permute-start(bf16[112,512]{1,0:T(8,128)(2,1)S(1)} %get-tuple-element.25), channel_id=1, source_target_pairs={{0,2},{1,3},{2,0},{3,1},{4,6},{5,7},{6,4},{7,5},{8,10},{9,11},{10,... | collective-permute-start | bytes 344072 | tf_op jit(solution)/shard_map/ppermute | solution.py:233
  4.6 6.5 %collective-permute-start.2 = (bf16[64,512]{1,0:T(8,128)(2,1)S(1)}, bf16[64,512]{1,0:T(8,128)(2,1)S(1)}, u32[]{:S(2)}, u32[]{:S(2)}) collective-permute-start(bf16[64,512]{1,0:T(8,128)(2,1)S(1)} %get-tuple-element.26), channel_id=1, source_target_pairs={{0,3},{1,2},{2,1},{3,0},{4,7},{5,6},{6,5},{7,4},{8,11},{9,10},{10,... | collective-permute-start | bytes 196616 | tf_op jit(solution)/shard_map/ppermute | solution.py:233
  6.3 4.7 %collective-permute-start.3 = (bf16[48,512]{1,0:T(8,128)(2,1)S(1)}, bf16[48,512]{1,0:T(8,128)(2,1)S(1)}, u32[]{:S(2)}, u32[]{:S(2)}) collective-permute-start(bf16[48,512]{1,0:T(8,128)(2,1)S(1)} %get-tuple-element.27), channel_id=1, source_target_pairs={{0,35},{1,34},{2,33},{3,32},{32,3},{33,2},{34,1},{35,0},{4,39},{5,... | collective-permute-start | bytes 147464 | tf_op jit(solution)/shard_map/ppermute | solution.py:238
  38.5 3.3 %collective-permute-start.4 = (bf16[128,8,128]{2,1,0:T(8,128)(2,1)S(1)}, bf16[128,8,128]{2,1,0:T(8,128)(2,1)S(1)}, u32[]{:S(2)}, u32[]{:S(2)}) collective-permute-start(bf16[128,8,128]{2,1,0:T(8,128)(2,1)S(1)} %slice.4), channel_id=1, source_target_pairs={{0,1},{1,0},{2,3},{3,2},{4,5},{5,4},{6,7},{7,6},{8,9},{9,8},{10,11... | collective-permute-start | bytes 786440 | tf_op jit(solution)/shard_map/ppermute | solution.py:233
  40.4 1.4 %collective-permute-start.5 = (bf16[4,128,128]{2,1,0:T(8,128)(2,1)S(1)}, bf16[4,128,128]{2,1,0:T(8,128)(2,1)S(1)}, u32[]{:S(2)}, u32[]{:S(2)}) collective-permute-start(bf16[4,128,128]{2,1,0:T(8,128)(2,1)S(1)} %get-tuple-element.35), channel_id=1, source_target_pairs={{0,1},{1,0},{2,3},{3,2},{4,5},{5,4},{6,7},{7,6},{8,9},{9,8},{10,11... | collective-permute-start | bytes 393224 | tf_op jit(solution)/shard_map/ppermute | solution.py:233
  68.0 3.4 %collective-permute-start.6 = (bf16[2,32,512]{2,1,0:T(8,128)(2,1)S(1)}, bf16[2,32,512]{2,1,0:T(8,128)(2,1)S(1)}, u32[]{:S(2)}, u32[]{:S(2)}) collective-permute-start(bf16[2,32,512]{2,1,0:T(8,128)(2,1)S(1)} %get-tuple-element.38), channel_id=1, source_target_pairs={{0,1},{1,0},{2,3},{3,2},{4,5},{5,4},{6,7},{7,6},{8,9},{9,8},{10,11... | collective-permute-start | bytes 196616 | tf_op jit(solution)/shard_map/ppermute | solution.py:233
  69.5 3.7 %collective-permute-start.7 = (bf16[2,32,512]{2,1,0:T(8,128)(2,1)S(1)}, bf16[2,32,512]{2,1,0:T(8,128)(2,1)S(1)}, u32[]{:S(2)}, u32[]{:S(2)}) collective-permute-start(bf16[2,32,512]{2,1,0:T(8,128)(2,1)S(1)} %get-tuple-element.39), channel_id=1, source_target_pairs={{0,2},{1,3},{2,0},{3,1},{4,6},{5,7},{6,4},{7,5},{8,10},{9,11},{10,... | collective-permute-start | bytes 196616 | tf_op jit(solution)/shard_map/ppermute | solution.py:233
  70.2 4.6 %collective-permute-start.8 = (bf16[2,32,512]{2,1,0:T(8,128)(2,1)S(1)}, bf16[2,32,512]{2,1,0:T(8,128)(2,1)S(1)}, u32[]{:S(2)}, u32[]{:S(2)}) collective-permute-start(bf16[2,32,512]{2,1,0:T(8,128)(2,1)S(1)} %get-tuple-element.40), channel_id=1, source_target_pairs={{0,3},{1,2},{2,1},{3,0},{4,7},{5,6},{6,5},{7,4},{8,11},{9,10},{10,... | collective-permute-start | bytes 196616 | tf_op jit(solution)/shard_map/ppermute | solution.py:233
